TPU v7x, 512 devices: a whole 4x8x8 slice. The times are simulated.
512 devices in a mesh: gx: 16 (over x, y_hi), yz: 32 (over y_lo, z, core).
Axes of the slice: x: 4, y: 8 (y_hi: 4, y_lo: 2; y = y_hi * 2 + y_lo), z: 8, core: 2. Of those that a mesh axis runs over, the one named last changes fastest.
Arguments:
- tokens: bfloat16 [2048, 4096], P('gx', 'yz'), may hold values from -6 to 6
- gate_weight: bfloat16 [4096, 14336], P('gx', 'yz'), may hold values from -0.09375 to 0.09375
- up_weight: bfloat16 [4096, 14336], P('gx', 'yz'), may hold values from -0.09375 to 0.09375
- down_weight: bfloat16 [14336, 4096], P('yz', 'gx'), may hold values from -0.046875 to 0.046875
- decode_in: bfloat16 [4, 96, 4096], P(None, 'gx'), may hold values from -6 to 6
Outputs:
- prefill_out: bfloat16 [2048, 4096], P(('gx', 'yz'))
- decode_out: bfloat16 [4, 96, 4096], P(None, 'yz', 'gx')
All inputs are finite; a program needn't handle non-finite values.
Results may differ from a plain program's by a relative error of at most 0.0049.
Values may be sent and summed in bfloat16 or wider, within the bound.
No kernel may reach another device: no remote copies, remote signals or barrier semaphores. Data moves between devices by JAX's collectives and lax.ppermute only.
A program may use at most 64 MiB of HBM per device.

v0:
```python
import jax
import jax.numpy as jnp
from jax import lax
from jax.sharding import PartitionSpec as P


def local(tokens, gate_weight, up_weight, down_weight, decode_in):
    gathered = lax.all_gather(tokens, "yz", axis=1, tiled=True)
    gate_sum = jnp.dot(
        gathered,
        lax.all_gather(gate_weight, "gx", axis=0, tiled=True),
        preferred_element_type=jnp.float32,
    )
    up_sum = jnp.dot(
        gathered,
        lax.all_gather(up_weight, "gx", axis=0, tiled=True),
        preferred_element_type=jnp.float32,
    )
    hidden = (jax.nn.silu(gate_sum) * up_sum).astype(jnp.bfloat16)
    partials = jnp.dot(
        hidden,
        lax.all_gather(down_weight, "gx", axis=1, tiled=True),
        preferred_element_type=jnp.float32,
    )
    prefill_out = lax.psum_scatter(partials, "yz", scatter_dimension=0, tiled=True).astype(
        jnp.bfloat16
    )
    results = []
    for step in range(decode_in.shape[0]):
        relaid_step = lax.all_to_all(decode_in[step], "gx", split_axis=1, concat_axis=0, tiled=True)
        gate_local = jnp.dot(relaid_step, gate_weight, preferred_element_type=jnp.float32)
        up_local = jnp.dot(relaid_step, up_weight, preferred_element_type=jnp.float32)
        decode_gate_sum = lax.psum_scatter(gate_local, "gx", scatter_dimension=0, tiled=True)
        decode_up_sum = lax.psum_scatter(up_local, "gx", scatter_dimension=0, tiled=True)
        step_hidden = (jax.nn.silu(decode_gate_sum) * decode_up_sum).astype(jnp.bfloat16)
        step_terms = jnp.dot(
            lax.all_gather(step_hidden, "gx", axis=0, tiled=True),
            down_weight,
            preferred_element_type=jnp.float32,
        )
        results.append(
            lax.psum_scatter(step_terms, "yz", scatter_dimension=0, tiled=True).astype(jnp.bfloat16)
        )
    decode_out = jnp.stack(results)
    return (prefill_out, decode_out)


def solution(mesh):
    return jax.shard_map(
        local,
        mesh=mesh,
        in_specs=(P("gx", "yz"), P("gx", "yz"), P("gx", "yz"), P("yz", "gx"), P(None, "gx", None)),
        out_specs=(P(("gx", "yz"), None), P(None, "yz", "gx")),
        check_vma=False,
    )
```

profile of v0, /device:TPU:6, one launch (start us, length us, event | category | flops | bytes accessed | tf_op | source)
XLA Modules:
  0.0 570.2 jit_solution(9573976941193536492)
XLA Ops:
  12.8 17.9 %all_to_all.76 = bf16[6,16,256]{2,0,1:T(8,128)(2,1)S(1)} all-to-all(bf16[6,16,256]{2,0,1:T(8,128)(2,1)S(1)} %bitcast.74), channel_id=1, replica_groups=mesh['gx'=16,'yz'=32] {'gx'}, dimensions={1} | all-to-all | bytes 98304 | tf_op jit(solution)/shard_map/all_to_all | solution.py:30
  30.7 12.8 %all_to_all.77 = bf16[6,16,256]{2,0,1:T(8,128)(2,1)S(1)} all-to-all(bf16[6,16,256]{2,0,1:T(8,128)(2,1)S(1)} %bitcast.73), channel_id=1, replica_groups=mesh['gx'=16,'yz'=32] {'gx'}, dimensions={1} | all-to-all | bytes 98304 | tf_op jit(solution)/shard_map/all_to_all | solution.py:30
  43.5 13.0 %all_to_all.78 = bf16[6,16,256]{2,0,1:T(8,128)(2,1)S(1)} all-to-all(bf16[6,16,256]{2,0,1:T(8,128)(2,1)S(1)} %bitcast.72), channel_id=1, replica_groups=mesh['gx'=16,'yz'=32] {'gx'}, dimensions={1} | all-to-all | bytes 98304 | tf_op jit(solution)/shard_map/all_to_all | solution.py:30
  56.5 5.5 all-to-all-start.2
  62.2 8.0 %all-to-all-done.2 = bf16[6,16,256]{2,0,1:T(8,128)(2,1)S(1)} async-done(((bf16[6,16,256]{2,0,1:T(8,128)(2,1)}), bf16[6,16,256]{2,0,1:T(8,128)(2,1)S(1)}, u32[]{:S(2)}, u32[]{:S(2)}) %all-to-all-start.2) | async-done | bytes 49184 | tf_op jit(solution)/shard_map/all_to_all | solution.py:30
  74.8 65.2 %fusion.33 = (f32[8,448]{1,0:T(8,128)S(1)}, f32[8,448]{1,0:T(8,128)S(1)}, f32[8,448]{1,0:T(8,128)S(1)}, f32[8,448]{1,0:T(8,128)S(1)}, f32[8,448]{1,0:T(8,128)S(1...) fusion(f32[96,448]{1,0:T(8,128)S(1)} %fusion.45, f32[96,448]{1,0:T(8,128)S(1)} %fusion.44, ...), kind=kCustom, calls=%all-reduce-scatter.8 | all-reduce-scatter fusion | flops 458753 | bytes 1492992
  147.1 3.6 collective-permute-start.12
  158.4 4.5 collective-permute-start.9
  174.8 3.4 collective-permute-start
  185.6 3.6 collective-permute-start.22
  189.6 4.3 collective-permute-start.21
  199.5 48.7 %all-gather = bf16[16,6,448]{2,1,0:T(8,128)(2,1)S(1)} all-gather(bf16[1,6,448]{2,1,0:T(8,128)(2,1)S(1)} %fusion.27), channel_id=1, replica_groups=mesh['gx'=16,'yz'=32] {'gx'}, dimensions={0}, use_global_device_ids=true | all-gather | bytes 91392 | tf_op jit(solution)/shard_map/all_gather | solution.py:37
  248.2 7.5 %collective-permute-start.17 = (f32[8,448]{1,0:T(8,128)S(1)}, f32[8,448]{1,0:T(8,128)S(1)}, u32[]{:S(2)}, u32[]{:S(2)}) collective-permute-start(f32[8,448]{1,0:T(8,128)S(1)} %get-tuple-element.28), channel_id=1, source_target_pairs={{0,64},{32,96},{64,128},{96,160},{128,192},{160,224},{192,256},{22... | collective-permute-start | bytes 43016
  255.7 5.6 collective-permute-start.16
  262.6 36.0 %all-gather.1 = bf16[16,6,448]{2,1,0:T(8,128)(2,1)S(1)} all-gather(bf16[1,6,448]{2,1,0:T(8,128)(2,1)S(1)} %fusion.26), channel_id=1, replica_groups=mesh['gx'=16,'yz'=32] {'gx'}, dimensions={0}, use_global_device_ids=true | all-gather | bytes 91392 | tf_op jit(solution)/shard_map/all_gather | solution.py:37
  298.8 7.4 %collective-permute-start.30 = (f32[8,448]{1,0:T(8,128)S(1)}, f32[8,448]{1,0:T(8,128)S(1)}, u32[]{:S(2)}, u32[]{:S(2)}) collective-permute-start(f32[8,448]{1,0:T(8,128)S(1)} %get-tuple-element.25), channel_id=1, source_target_pairs={{0,96},{32,128},{64,160},{96,192},{128,224},{160,256},{192,288},{2... | collective-permute-start | bytes 43016
  308.5 3.6 collective-permute-start.28
  316.9 46.5 %all-gather.2 = bf16[16,6,448]{2,1,0:T(8,128)(2,1)S(1)} all-gather(bf16[1,6,448]{2,1,0:T(8,128)(2,1)S(1)} %fusion.25), channel_id=1, replica_groups=mesh['gx'=16,'yz'=32] {'gx'}, dimensions={0}, use_global_device_ids=true | all-gather | bytes 91392 | tf_op jit(solution)/shard_map/all_gather | solution.py:37
  363.4 7.4 %collective-permute-start.25 = (f32[8,448]{1,0:T(8,128)S(1)}, f32[8,448]{1,0:T(8,128)S(1)}, u32[]{:S(2)}, u32[]{:S(2)}) collective-permute-start(f32[8,448]{1,0:T(8,128)S(1)} %get-tuple-element.26), channel_id=1, source_target_pairs={{0,64},{32,96},{64,128},{96,160},{128,192},{160,224},{192,256},{22... | collective-permute-start | bytes 43016
  370.9 5.1 collective-permute-start.24
  382.1 35.6 %all-gather.3 = bf16[16,6,448]{2,1,0:T(8,128)(2,1)S(1)} all-gather(bf16[1,6,448]{2,1,0:T(8,128)(2,1)S(1)} %fusion.24), channel_id=1, replica_groups=mesh['gx'=16,'yz'=32] {'gx'}, dimensions={0}, use_global_device_ids=true | all-gather | bytes 91392 | tf_op jit(solution)/shard_map/all_gather | solution.py:37
  418.6 3.6 fusion.34
  422.2 6.0 %fusion.9 = f32[128,4096]{1,0:T(8,128)S(1)} fusion(bf16[448,4096]{1,0:T(8,128)(2,1)} %all-gather.15.cloned.1.call-done, bf16[128,4096]{1,0:T(8,128)(2,1)S(1)} %copy-done.3, bf16[4096,448]{0,1:T(8,128)(2,1)} %all-gather.13.cloned.1.call-done, f32[128,448]{0,1:T(8,128)S(1)} %fusion.34), kind=kOutput, calls=%fused_computation.2 | convolution fusion | flops 939868160 | bytes 10715136 | tf_op jit(solution)/shard_map/dot_general | solution.py:20
  428.2 134.2 %all-reduce.24 = (bf16[128,4096]{1,0:T(8,128)(2,1)S(1)}, bf16[96,256]{1,0:T(8,128)(2,1)S(1)}, bf16[96,256]{1,0:T(8,128)(2,1)S(1)}, bf16[96,256]{1,0:T(8,128)(2,1)S(1)}, bf16[96,256]{1,0:T(8,128)(2,1)S(1)}) all-reduce(f32[128,4096]{1,0:T(8,128)S(1)} %fusion.9, f32[96,256]{1,0:T(8,128)} %fusion.46, ...), channel_id=2, replica_groups=mesh['gx'=16,'yz'=32] {'yz'}, use_global_device_ids=true, to_apply=%region_0.1.clone | all-reduce | flops 622592 | bytes 3735552
  (121 shorter events, 64.8 us)
Async XLA Ops:
  7.2 411.4 %all-gather.9.cloned.1.call-start = ((), (), s32[]{:S(2)}) async-start(), calls=%async_computation.4 | async-start | bytes 1081344 | tf_op jit(solution)/shard_map/all_gather | solution.py:8
  7.9 410.7 %all-gather.11.cloned.1.call-start = ((), (), s32[]{:S(2)}) async-start(), calls=%async_computation.5 | async-start | bytes 3899392 | tf_op jit(solution)/shard_map/all_gather | solution.py:11
  8.7 413.5 %all-gather.13.cloned.1.call-start = ((), (), s32[]{:S(2)}) async-start(), calls=%async_computation.6 | async-start | bytes 3899392 | tf_op jit(solution)/shard_map/all_gather | solution.py:16
  9.4 412.8 %all-gather.15.cloned.1.call-start = ((), (), s32[]{:S(2)}) async-start(), calls=%async_computation.7 | async-start | bytes 3899392 | tf_op jit(solution)/shard_map/all_gather | solution.py:22
  141.3 21.6 %collective-permute-start.14 = (f32[8,448]{1,0:T(8,128)S(1)}, f32[8,448]{1,0:T(8,128)S(1)}, u32[]{:S(2)}, u32[]{:S(2)}) collective-permute-start(f32[8,448]{1,0:T(8,128)S(1)} %get-tuple-element.29), channel_id=1, source_target_pairs={{0,96},{32,128},{64,160},{96,192},{128,224},{160,256},{192,288},{2... | collective-permute-start | bytes 43016
  143.8 21.2 %collective-permute-start.13 = (f32[8,448]{1,0:T(8,128)S(1)}, f32[8,448]{1,0:T(8,128)S(1)}, u32[]{:S(2)}, u32[]{:S(2)}) collective-permute-start(f32[8,448]{1,0:T(8,128)S(1)} %get-tuple-element.29), channel_id=1, source_target_pairs={{0,64},{32,96},{64,128},{96,160},{128,192},{160,224},{192,256},{22... | collective-permute-start | bytes 43016
  147.1 19.9 %collective-permute-start.12 = (f32[8,448]{1,0:T(8,128)S(1)}, f32[8,448]{1,0:T(8,128)S(1)}, u32[]{:S(2)}, u32[]{:S(2)}) collective-permute-start(f32[8,448]{1,0:T(8,128)S(1)} %get-tuple-element.29), channel_id=1, source_target_pairs={{0,32},{32,64},{64,96},{96,128},{128,160},{160,192},{192,224},{224... | collective-permute-start | bytes 43016
  170.9 23.0 %collective-permute-start.2 = (f32[8,448]{1,0:T(8,128)S(1)}, f32[8,448]{1,0:T(8,128)S(1)}, u32[]{:S(2)}, u32[]{:S(2)}) collective-permute-start(f32[8,448]{1,0:T(8,128)S(1)} %get-tuple-element.32), channel_id=1, source_target_pairs={{0,96},{32,128},{64,160},{96,192},{128,224},{160,256},{192,288},{2... | collective-permute-start | bytes 43016
  172.8 23.0 %collective-permute-start.1 = (f32[8,448]{1,0:T(8,128)S(1)}, f32[8,448]{1,0:T(8,128)S(1)}, u32[]{:S(2)}, u32[]{:S(2)}) collective-permute-start(f32[8,448]{1,0:T(8,128)S(1)} %get-tuple-element.32), channel_id=1, source_target_pairs={{0,64},{32,96},{64,128},{96,160},{128,192},{160,224},{192,256},{22... | collective-permute-start | bytes 43016
  174.8 23.0 %collective-permute-start = (f32[8,448]{1,0:T(8,128)S(1)}, f32[8,448]{1,0:T(8,128)S(1)}, u32[]{:S(2)}, u32[]{:S(2)}) collective-permute-start(f32[8,448]{1,0:T(8,128)S(1)} %get-tuple-element.32), channel_id=1, source_target_pairs={{0,32},{32,64},{64,96},{96,128},{128,160},{160,192},{192,224},{224... | collective-permute-start | bytes 43016
  185.6 70.1 %collective-permute-start.22 = (f32[8,448]{1,0:T(8,128)S(1)}, f32[8,448]{1,0:T(8,128)S(1)}, u32[]{:S(2)}, u32[]{:S(2)}) collective-permute-start(f32[8,448]{1,0:T(8,128)S(1)} %get-tuple-element.27), channel_id=1, source_target_pairs={{0,96},{32,128},{64,160},{96,192},{128,224},{160,256},{192,288},{2... | collective-permute-start | bytes 43016
  189.6 71.7 %collective-permute-start.21 = (f32[8,448]{1,0:T(8,128)S(1)}, f32[8,448]{1,0:T(8,128)S(1)}, u32[]{:S(2)}, u32[]{:S(2)}) collective-permute-start(f32[8,448]{1,0:T(8,128)S(1)} %get-tuple-element.27), channel_id=1, source_target_pairs={{0,64},{32,96},{64,128},{96,160},{128,192},{160,224},{192,256},{22... | collective-permute-start | bytes 43016
  193.9 104.9 %collective-permute-start.20 = (f32[8,448]{1,0:T(8,128)S(1)}, f32[8,448]{1,0:T(8,128)S(1)}, u32[]{:S(2)}, u32[]{:S(2)}) collective-permute-start(f32[8,448]{1,0:T(8,128)S(1)} %get-tuple-element.27), channel_id=1, source_target_pairs={{0,32},{32,64},{64,96},{96,128},{128,160},{160,192},{192,224},{224... | collective-permute-start | bytes 43016
  195.8 112.7 %collective-permute-start.18 = (f32[8,448]{1,0:T(8,128)S(1)}, f32[8,448]{1,0:T(8,128)S(1)}, u32[]{:S(2)}, u32[]{:S(2)}) collective-permute-start(f32[8,448]{1,0:T(8,128)S(1)} %get-tuple-element.28), channel_id=1, source_target_pairs={{0,96},{32,128},{64,160},{96,192},{128,224},{160,256},{192,288},{2... | collective-permute-start | bytes 43016
  197.8 50.4 %collective-permute-start.23 = (f32[6,448]{1,0:T(8,128)S(1)}, f32[6,448]{1,0:T(8,128)S(1)}, u32[]{:S(2)}, u32[]{:S(2)}) collective-permute-start(f32[6,448]{1,0:T(8,128)S(1)} %slice.21), channel_id=1, source_target_pairs={{0,128},{32,160},{64,192},{96,224},{128,256},{160,288},{192,320},{... | collective-permute-start | bytes 32264
  248.2 64.0 %collective-permute-start.17 = (f32[8,448]{1,0:T(8,128)S(1)}, f32[8,448]{1,0:T(8,128)S(1)}, u32[]{:S(2)}, u32[]{:S(2)}) collective-permute-start(f32[8,448]{1,0:T(8,128)S(1)} %get-tuple-element.28), channel_id=1, source_target_pairs={{0,64},{32,96},{64,128},{96,160},{128,192},{160,224},{192,256},{22... | collective-permute-start | bytes 43016
  255.7 58.4 %collective-permute-start.16 = (f32[8,448]{1,0:T(8,128)S(1)}, f32[8,448]{1,0:T(8,128)S(1)}, u32[]{:S(2)}, u32[]{:S(2)}) collective-permute-start(f32[8,448]{1,0:T(8,128)S(1)} %get-tuple-element.28), channel_id=1, source_target_pairs={{0,32},{32,64},{64,96},{96,128},{128,160},{160,192},{192,224},{224... | collective-permute-start | bytes 43016
  261.3 45.3 %collective-permute-start.19 = (f32[6,448]{1,0:T(8,128)S(1)}, f32[6,448]{1,0:T(8,128)S(1)}, u32[]{:S(2)}, u32[]{:S(2)}) collective-permute-start(f32[6,448]{1,0:T(8,128)S(1)} %slice.20), channel_id=1, source_target_pairs={{0,128},{32,160},{64,192},{96,224},{128,256},{160,288},{192,320},{... | collective-permute-start | bytes 32264
  298.8 72.1 %collective-permute-start.30 = (f32[8,448]{1,0:T(8,128)S(1)}, f32[8,448]{1,0:T(8,128)S(1)}, u32[]{:S(2)}, u32[]{:S(2)}) collective-permute-start(f32[8,448]{1,0:T(8,128)S(1)} %get-tuple-element.25), channel_id=1, source_target_pairs={{0,96},{32,128},{64,160},{96,192},{128,224},{160,256},{192,288},{2... | collective-permute-start | bytes 43016
  306.6 69.4 %collective-permute-start.29 = (f32[8,448]{1,0:T(8,128)S(1)}, f32[8,448]{1,0:T(8,128)S(1)}, u32[]{:S(2)}, u32[]{:S(2)}) collective-permute-start(f32[8,448]{1,0:T(8,128)S(1)} %get-tuple-element.25), channel_id=1, source_target_pairs={{0,64},{32,96},{64,128},{96,160},{128,192},{160,224},{192,256},{22... | collective-permute-start | bytes 43016
  308.5 69.6 %collective-permute-start.28 = (f32[8,448]{1,0:T(8,128)S(1)}, f32[8,448]{1,0:T(8,128)S(1)}, u32[]{:S(2)}, u32[]{:S(2)}) collective-permute-start(f32[8,448]{1,0:T(8,128)S(1)} %get-tuple-element.25), channel_id=1, source_target_pairs={{0,32},{32,64},{64,96},{96,128},{128,160},{160,192},{192,224},{224... | collective-permute-start | bytes 43016
  312.2 69.4 %collective-permute-start.26 = (f32[8,448]{1,0:T(8,128)S(1)}, f32[8,448]{1,0:T(8,128)S(1)}, u32[]{:S(2)}, u32[]{:S(2)}) collective-permute-start(f32[8,448]{1,0:T(8,128)S(1)} %get-tuple-element.26), channel_id=1, source_target_pairs={{0,96},{32,128},{64,160},{96,192},{128,224},{160,256},{192,288},{2... | collective-permute-start | bytes 43016
  314.1 49.3 %collective-permute-start.31 = (f32[6,448]{1,0:T(8,128)S(1)}, f32[6,448]{1,0:T(8,128)S(1)}, u32[]{:S(2)}, u32[]{:S(2)}) collective-permute-start(f32[6,448]{1,0:T(8,128)S(1)} %slice.23), channel_id=1, source_target_pairs={{0,128},{32,160},{64,192},{96,224},{128,256},{160,288},{192,320},{... | collective-permute-start | bytes 32264
  363.4 18.2 %collective-permute-start.25 = (f32[8,448]{1,0:T(8,128)S(1)}, f32[8,448]{1,0:T(8,128)S(1)}, u32[]{:S(2)}, u32[]{:S(2)}) collective-permute-start(f32[8,448]{1,0:T(8,128)S(1)} %get-tuple-element.26), channel_id=1, source_target_pairs={{0,64},{32,96},{64,128},{96,160},{128,192},{160,224},{192,256},{22... | collective-permute-start | bytes 43016
  (17 other events, 524.3 us)
Sparse Core Ops, SparseCore 0:
  10.1 70.4 all-gather.8
  83.5 91.4 all-gather.10
  178.1 89.8 all-gather.12
  270.8 85.7 all-gather.14
where the time goes:
time: 579 us; the launch traced here: 570 us
  blocking collectives  410 us (71%)
  starting transfers between devices  97.8 us (17%)
  waiting for transfers between devices  19 us (3%)
  matrix products  16.7 us (3%)
  between operations  16.5 us (3%)
  local copies, waits for them, and re-layouts  10.3 us (2%)
    unnamed x2, blocking collectives  199 us
    all_gather x4, blocking collectives, local(): lax.all_gather(step_hidden, 'gx', axis=0, tiled=True)  167 us
    unnamed x32, starting transfers between devices  92.1 us
    all_to_all x3, blocking collectives, local(): lax.all_to_all(decode_in[step], 'gx', split_axis=1, concat_axis=0, tiled=...  43.7 us
  transfers between devices with their start and end apart: 37, of which 5 were waited for; matrix products, arithmetic and copies ran while one was open for 15% of the time, Pallas kernels for 0%

commit v1 on v0

v1 whole, which is shorter than its diff:
```python
import jax
import jax.numpy as jnp
from jax import lax
from jax.sharding import Mesh, PartitionSpec as P

BF16 = jnp.bfloat16
F32 = jnp.float32
SIZES = (("x", 4), ("h", 4), ("l", 2), ("a", 2), ("b", 4), ("c", 2))
GX = ("x", "h")
LZ = ("l", "a", "b")


def swap_cores(value):
    return lax.ppermute(value, "c", [(0, 1), (1, 0)])


def exchange(blocks, axes):
    return lax.all_to_all(blocks, axes, split_axis=0, concat_axis=0, tiled=True)


def local(tokens, gate_weight, up_weight, down_weight, decode_in):
    core = lax.axis_index("c")
    yz = lax.axis_index(("l", "a", "b", "c"))
    steps, rows, width = decode_in.shape
    ff = gate_weight.shape[1]
    n_rows = tokens.shape[0]
    n_dec = steps * rows
    block = tokens.shape[1]

    halves = down_weight.reshape(ff, 2, block)
    kept = lax.dynamic_index_in_dim(halves, core, 1, keepdims=False)
    given = lax.dynamic_index_in_dim(halves, 1 - core, 1, keepdims=False)
    taken = swap_cores(given)
    both = jnp.where(core == 0, jnp.stack([kept, taken]), jnp.stack([taken, kept]))
    gate_up = jnp.concatenate([gate_weight, up_weight], axis=1)
    gate_up = lax.all_gather(gate_up, "x", axis=0, tiled=True)
    down = lax.all_gather(both.reshape(2 * ff, block), GX, axis=0, tiled=False)

    decode_part = lax.dynamic_slice_in_dim(decode_in.reshape(n_dec, width), yz * block, block, 1)
    feats = jnp.concatenate([tokens, decode_part], axis=0)
    feats = lax.ppermute(
        feats, ("h", "b"), [(h * 4 + b, b * 4 + h) for h in range(4) for b in range(4)]
    )
    total = n_rows + n_dec
    feats = exchange(jnp.broadcast_to(feats, (16, total, block)), LZ)
    other = swap_cores(feats)
    pair = jnp.where(core == 0, jnp.stack([feats, other]), jnp.stack([other, feats]))
    feats = pair.reshape(2, 4, 4, total, block).transpose(2, 3, 1, 0, 4).reshape(4 * total, -1)

    partial = jnp.dot(feats, gate_up, preferred_element_type=F32).astype(BF16)
    sums = exchange(partial.reshape(4, total, 2 * ff), "h").astype(F32).sum(0)
    hidden = (jax.nn.silu(sums[:, :ff]) * sums[:, ff:]).astype(BF16)

    other = swap_cores(hidden)
    hidden = jnp.where(
        core == 0,
        jnp.concatenate([hidden, other], axis=1),
        jnp.concatenate([other, hidden], axis=1),
    )
    out = jnp.einsum("rk,gkn->rgn", hidden, down, preferred_element_type=F32).astype(BF16)
    prefill = out[:n_rows].reshape(16, n_rows, block)
    decode = out[n_rows:].transpose(1, 0, 2)
    sums = exchange(jnp.concatenate([prefill, decode], axis=1), LZ).astype(F32).sum(0).astype(BF16)

    prefill = sums[:n_rows].reshape(2, n_rows // 2, block)
    decode = sums[n_rows:].reshape(steps, 2, rows // 2, block).transpose(1, 0, 2, 3)
    decode = decode.reshape(2, n_dec // 2, block)
    mine = jnp.concatenate([prefill, decode], axis=1)
    kept = lax.dynamic_index_in_dim(mine, core, 0, keepdims=False)
    given = lax.dynamic_index_in_dim(mine, 1 - core, 0, keepdims=False)
    taken = swap_cores(given)
    joined = jnp.where(
        core == 0,
        jnp.concatenate([kept, taken], axis=1),
        jnp.concatenate([taken, kept], axis=1),
    )
    prefill_out = joined[: n_rows // 2].reshape(n_rows // 32, 16 * 2 * block)
    decode = joined[n_rows // 2 :]
    decode = lax.ppermute(
        decode,
        ("x", "h", "l", "a", "b"),
        [(g * 16 + y, y * 16 + g) for g in range(16) for y in range(16)],
    )
    decode_out = decode.reshape(steps, rows // 2, 2 * block)
    return prefill_out, decode_out


def solution(mesh):
    sizes = [size for _, size in SIZES]
    fine = Mesh(mesh.devices.reshape(sizes), [name for name, _ in SIZES])
    gx, yz = GX, ("l", "a", "b", "c")
    return jax.shard_map(
        local,
        mesh=fine,
        in_specs=(P(gx, yz), P(gx, yz), P(gx, yz), P(yz, gx), P(None, gx, None)),
        out_specs=(P(gx + yz, None), P(None, yz, gx)),
        check_vma=False,
    )
```

time: 579 us -> 202 us (0.35); the launches traced: 570 us -> 202 us
  blocking collectives: 410 us -> 112 us
  starting transfers between devices: 97.8 us -> 12.3 us
  waiting for transfers between devices: 19 us -> 49.3 us
  matrix products: 16.7 us -> 5.89 us
    unnamed x2 -> x0, blocking collectives: 199 us -> none
    all_gather x4 -> x0, blocking collectives: 167 us -> none  [local(): lax.all_gather(step_hidden, 'gx', axis=0, tiled=True)]
    unnamed x32 -> x0, starting transfers between devices: 92.1 us -> none
    all_to_all x3, blocking collectives: 43.7 us -> 112 us  [exchange(): return lax.all_to_all(blocks, axes, split_axis=0, concat_axis=0, tiled=True)]
    all_gather x4 -> x2, waiting for transfers between devices: 0.04 us -> 35.6 us  [the longest x1 35.6 us: local(): down = lax.all_gather(both.reshape(2 * ff, block), GX, axis=0, tiled=False)]
    ppermute x0 -> x6, waiting for transfers between devices: none -> 13.7 us  [the longest x1 7.87 us: local(): lax.ppermute(decode, ('x', 'h', 'l', 'a', 'b'), [(g * 16 + y, y * 16 + g)...]
    ppermute x0 -> x6, starting transfers between devices: none -> 12.3 us  [the longest x4 7.67 us: swap_cores(): return lax.ppermute(value, 'c', [(0, 1), (1, 0)])]
    unnamed x36 -> x2, waiting for transfers between devices: 11 us -> 0.03 us
  transfers between devices with their start and end apart: 37 -> 8, of which waited for: 5 -> 6; matrix products, arithmetic and copies ran while one was open for 15% -> 4% of each run, Pallas kernels for 0% -> 0%
where the time goes in v1:
time: 202 us
  blocking collectives  112 us (55%)
  waiting for transfers between devices  49.3 us (24%)
  between operations  14.4 us (7%)
  starting transfers between devices  12.3 us (6%)
  matrix products  5.89 us (3%)
  local copies, waits for them, and re-layouts  4.75 us (2%)
  other arithmetic  3.25 us (2%)
    all_to_all x3, blocking collectives, exchange(): return lax.all_to_all(blocks, axes, split_axis=0, concat_axis=0, tiled=True)  112 us
    all_gather x1, waiting for transfers between devices, local(): down = lax.all_gather(both.reshape(2 * ff, block), GX, axis=0, tiled=False)  35.6 us
    ppermute x1, waiting for transfers between devices, local(): lax.ppermute(decode, ('x', 'h', 'l', 'a', 'b'), [(g * 16 + y, y * 16 + g)...  7.87 us
    ppermute x4, starting transfers between devices, swap_cores(): return lax.ppermute(value, 'c', [(0, 1), (1, 0)])  7.67 us
    ppermute x4, waiting for transfers between devices, swap_cores(): return lax.ppermute(value, 'c', [(0, 1), (1, 0)])  5.78 us
  transfers between devices with their start and end apart: 8, of which 6 were waited for; matrix products, arithmetic and copies ran while one was open for 4% of the time, Pallas kernels for 0%

profile of v1, /device:TPU:6, one launch (start us, length us, event | category | flops | bytes accessed | tf_op | source)
XLA Modules:
  0.0 201.8 jit_solution(10682929698955288211)
XLA Ops:
  7.2 1.9 pad_maximum_fusion.1
  9.3 0.5 constant_dynamic-slice_fusion.1
  9.8 1.9 collective-permute-start.3
  11.8 1.3 collective-permute-done.3
  13.0 0.7 maximum_select_fusion.2
  14.0 0.7 collective-permute-start
  14.8 41.0 %all_to_all.15 = bf16[16,152,128]{2,1,0:T(8,128)(2,1)S(1)} all-to-all(bf16[16,152,128]{2,1,0:T(8,128)(2,1)S(1)} %broadcast_in_dim.3), channel_id=1, replica_groups=mesh['x'=4,'h'=4,'l'=2,'a'=2,'b'=4,'c'=2] {'l','a','b'}, dimensions={0} | all-to-all | bytes 1245184 | tf_op jit(solution)/shard_map/all_to_all | solution.py:18
  55.8 1.9 collective-permute-start.1
  57.7 2.0 collective-permute-done.1
  60.0 1.3 copy.19
  61.3 0.9 reshape.64
  62.2 3.0 %convolution_convert_fusion = bf16[608,896]{1,0:T(8,128)(2,1)S(1)} fusion(bf16[608,1024]{1,0:T(8,128)(2,1)S(1)} %reshape.64, bf16[1024,896]{0,1:T(8,128)(2,1)} %all-gather.3.cloned.1.call-done), kind=kOutput, calls=%fused_computation.1 | convolution fusion | flops 1116229632 | bytes 4169728 | tf_op jit(solution)/shard_map/dot_general | solution.py:50
  65.2 41.5 %all_to_all.16 = bf16[4,152,896]{2,1,0:T(8,128)(2,1)S(1)} all-to-all(bf16[4,152,896]{2,1,0:T(8,128)(2,1)S(1)} %bitcast.31), channel_id=1, replica_groups=mesh['x'=4,'h'=4,'l'=2,'a'=2,'b'=4,'c'=2] {'h'}, dimensions={0} | all-to-all | bytes 2179072 | tf_op jit(solution)/shard_map/all_to_all | solution.py:18
  107.0 1.9 collective-permute-start.2
  108.9 1.3 collective-permute-done.2
  110.2 35.6 %all-gather.5.cloned.1.call-done = bf16[16,896,128]{2,1,0:T(8,128)(2,1)} async-done(((bf16[1,896,128]{2,1,0:T(8,128)(2,1)}), bf16[16,896,128]{2,1,0:T(8,128)(2,1)}) %all-gather.5.cloned.1.call-update) | async-done | bytes 3670032 | tf_op jit(solution)/shard_map/all_gather | solution.py:37
  145.8 2.9 %convolution_convert_fusion.1 = bf16[152,16,128]{2,0,1:T(8,128)(2,1)S(1)} fusion(bf16[16,896,128]{2,1,0:T(8,128)(2,1)} %all-gather.5.cloned.1.call-done, bf16[152,448]{1,0:T(8,128)(2,1)S(1)} %collective-permute-done.2, bf16[152,448]{1,0:T(8,128)(2,1)S(1)} %fusion.1, pred[]{:T(512)S(6)} %eq.2), kind=kOutput, calls=%fused_computation.2 | convolution fusion | flops 559379456 | bytes 4564993 | tf_op jit(solution)/shard_map/rk,gkn->rgn/dot_general | solution.py:60
  149.2 29.4 %all_to_all.17 = bf16[16,152,128]{2,1,0:T(8,128)(2,1)S(1)} all-to-all(bf16[16,152,128]{2,1,0:T(8,128)(2,1)S(1)} %pad_maximum_fusion), channel_id=1, replica_groups=mesh['x'=4,'h'=4,'l'=2,'a'=2,'b'=4,'c'=2] {'l','a','b'}, dimensions={0} | all-to-all | bytes 1245184 | tf_op jit(solution)/shard_map/all_to_all | solution.py:18
  178.8 1.9 collective-permute-start.4
  180.7 1.2 collective-permute-done.4
  181.9 3.9 %collective-permute-start.5 = (bf16[12,256]{1,0:T(8,128)(2,1)S(1)}, bf16[12,256]{1,0:T(8,128)(2,1)S(1)}, u32[]{:S(2)}, u32[]{:S(2)}) collective-permute-start(bf16[12,256]{1,0:T(8,128)(2,1)S(1)} %slice.39), channel_id=1, source_target_pairs={{0,0},{2,32},{4,64},{6,96},{8,128},{10,160},{12,192},{14,224},{16,... | collective-permute-start | bytes 18440 | tf_op jit(solution)/shard_map/ppermute | solution.py:79
  185.9 0.6 reshape.71
  186.5 7.9 %collective-permute-done.5 = bf16[12,256]{1,0:T(8,128)(2,1)S(1)} collective-permute-done((bf16[12,256]{1,0:T(8,128)(2,1)S(1)}, bf16[12,256]{1,0:T(8,128)(2,1)S(1)}, u32[]{:S(2)}, u32[]{:S(2)}) %collective-permute-start.5) | collective-permute-done | bytes 6176 | tf_op jit(solution)/shard_map/ppermute | solution.py:79
  194.4 0.6 copy.23
  (38 shorter events, 1.6 us)
Async XLA Ops:
  7.2 2.0 %copy-start = (bf16[448,256]{1,0:T(8,128)(2,1)S(1)}, bf16[448,256]{1,0:T(8,128)(2,1)}, u32[]{:S(2)}) copy-start(bf16[448,256]{1,0:T(8,128)(2,1)} %param.8) | copy-start | bytes 688132
  7.2 55.0 %all-gather.3.cloned.1.call-start = ((), (), s32[]{:S(2)}) async-start(), calls=%async_computation.3 | async-start | bytes 2293760 | tf_op jit(solution)/shard_map/all_gather | solution.py:36
  9.1 136.7 %all-gather.5.cloned.1.call-start = ((), (), s32[]{:S(2)}) async-start(), calls=%async_computation.4 | async-start | bytes 3899392 | tf_op jit(solution)/shard_map/all_gather | solution.py:37
  9.3 4.5 %copy-start.1 = (bf16[4,6,4096]{2,0,1:T(4,128)(2,1)S(1)}, bf16[4,6,4096]{2,0,1:T(4,128)(2,1)}, u32[]{:S(2)}) copy-start(bf16[4,6,4096]{2,0,1:T(4,128)(2,1)} %param.9) | copy-start | bytes 589828
  9.8 4.2 %copy-start.2 = (bf16[128,128]{1,0:T(8,128)(2,1)S(1)}, bf16[128,128]{1,0:T(8,128)(2,1)}, u32[]{:S(2)}) copy-start(bf16[128,128]{1,0:T(8,128)(2,1)} %param.5) | copy-start | bytes 98308
  9.8 3.2 %collective-permute-start.3 = (bf16[448,128]{1,0:T(8,128)(2,1)S(1)}, bf16[448,128]{1,0:T(8,128)(2,1)S(1)}, u32[]{:S(2)}, u32[]{:S(2)}) collective-permute-start(bf16[448,128]{1,0:T(8,128)(2,1)S(1)} %bitcast.37), channel_id=1, source_target_pairs={{0,1},{1,0},{2,3},{3,2},{4,5},{5,4},{6,7},{7,6},{8,9},{9,8},{10,11... | collective-permute-start | bytes 344072 | tf_op jit(solution)/shard_map/ppermute | solution.py:14
  14.0 0.7 collective-permute-start
  55.8 3.9 %collective-permute-start.1 = (bf16[16,152,128]{2,1,0:T(8,128)(2,1)S(1)}, bf16[16,152,128]{2,1,0:T(8,128)(2,1)S(1)}, u32[]{:S(2)}, u32[]{:S(2)}) collective-permute-start(bf16[16,152,128]{2,1,0:T(8,128)(2,1)S(1)} %all_to_all.15), channel_id=1, source_target_pairs={{0,1},{1,0},{2,3},{3,2},{4,5},{5,4},{6,7},{7,6},{8,9},{9,8},{10,11... | collective-permute-start | bytes 1867784 | tf_op jit(solution)/shard_map/ppermute | solution.py:14
  107.0 3.3 %collective-permute-start.2 = (bf16[152,448]{1,0:T(8,128)(2,1)S(1)}, bf16[152,448]{1,0:T(8,128)(2,1)S(1)}, u32[]{:S(2)}, u32[]{:S(2)}) collective-permute-start(bf16[152,448]{1,0:T(8,128)(2,1)S(1)} %fusion.1), channel_id=1, source_target_pairs={{0,1},{1,0},{2,3},{3,2},{4,5},{5,4},{6,7},{7,6},{8,9},{9,8},{10,11... | collective-permute-start | bytes 408584 | tf_op jit(solution)/shard_map/ppermute | solution.py:14
  178.8 3.1 %collective-permute-start.4 = (bf16[76,128]{1,0:T(8,128)(2,1)S(1)}, bf16[76,128]{1,0:T(8,128)(2,1)S(1)}, u32[]{:S(2)}, u32[]{:S(2)}) collective-permute-start(bf16[76,128]{1,0:T(8,128)(2,1)S(1)} %get-tuple-element.11), channel_id=1, source_target_pairs={{0,1},{1,0},{2,3},{3,2},{4,5},{5,4},{6,7},{7,6},{8,9},{9,8},{10,11... | collective-permute-start | bytes 58376 | tf_op jit(solution)/shard_map/ppermute | solution.py:14
  181.9 12.5 %collective-permute-start.5 = (bf16[12,256]{1,0:T(8,128)(2,1)S(1)}, bf16[12,256]{1,0:T(8,128)(2,1)S(1)}, u32[]{:S(2)}, u32[]{:S(2)}) collective-permute-start(bf16[12,256]{1,0:T(8,128)(2,1)S(1)} %slice.39), channel_id=1, source_target_pairs={{0,0},{2,32},{4,64},{6,96},{8,128},{10,160},{12,192},{14,224},{16,... | collective-permute-start | bytes 18440 | tf_op jit(solution)/shard_map/ppermute | solution.py:79
Sparse Core Ops, SparseCore 0:
  10.1 41.6 all-gather.2
  54.8 90.9 all-gather.4

commit v2 on v1

v2 whole, which is shorter than its diff:
```python
import jax
import jax.numpy as jnp
from jax import lax
from jax.experimental import pallas as pl
from jax.experimental.pallas import tpu as pltpu
from jax.sharding import Mesh, PartitionSpec as P

BF16 = jnp.bfloat16
F32 = jnp.float32
SIZES = (("x", 4), ("h", 4), ("l", 2), ("a", 2), ("b", 4), ("c", 2))
GX = ("x", "h")
LZ = ("l", "a", "b")
UP = [(i, (i + 1) % 4) for i in range(4)]
DOWN = [(i, (i + 3) % 4) for i in range(4)]
VMEM = 16 * 2**20
HINTS = (20, 3)


def swap_cores(value):
    return lax.ppermute(value, "c", [(0, 1), (1, 0)])


def exchange(blocks, axes):
    return lax.all_to_all(blocks, axes, split_axis=0, concat_axis=0, tiled=True)


def near(value, axis):
    return lax.ppermute(value, axis, DOWN), lax.ppermute(value, axis, UP)


def far(following, previous, axis, hint):
    shape = previous.shape[:-2] + (previous.shape[-2] // 2, previous.shape[-1])
    halves = jax.ShapeDtypeStruct(shape, BF16)
    up, down = call(halves_kernel, (halves, halves), hint)(previous, following)
    return lax.ppermute(up, axis, UP), lax.ppermute(down, axis, DOWN)


def call(kernel, outs, hint, scratch=()):
    return pl.pallas_call(
        kernel,
        out_shape=outs,
        scratch_shapes=list(scratch),
        compiler_params=pltpu.CompilerParams(vmem_limit_bytes=VMEM),
        cost_estimate=pl.CostEstimate(flops=int(hint * 1.1e9), bytes_accessed=2**20, transcendentals=0),
    )


def dot(lhs, rhs):
    return jnp.dot(lhs, rhs, preferred_element_type=F32)


def weights_kernel(gate, up, down, out):
    depth, ff = gate.shape
    whole = ff // 128
    for k in range(whole):
        out[k * depth : (k + 1) * depth] = gate[:, k * 128 : (k + 1) * 128]
        out[(whole + k) * depth : (whole + k + 1) * depth] = up[:, k * 128 : (k + 1) * 128]
    out[2 * whole * depth : (2 * whole + 1) * depth] = jnp.concatenate(
        [gate[:, whole * 128 :], up[:, whole * 128 :]], axis=1
    )
    base = (2 * whole + 1) * depth
    for k in range(down.shape[1] // 128):
        out[base + k * ff : base + (k + 1) * ff] = down[:, k * 128 : (k + 1) * 128]


def halves_kernel(previous, following, up, down):
    half = up.shape[-2]
    up[...] = previous[..., :half, :]
    down[...] = following[..., half:, :]


def gate_up_kernel(mine, other, own, following, first, second, previous, partial, kept, opposite):
    x, h, core = lax.axis_index("x"), lax.axis_index("h"), lax.axis_index("c")
    half = first.shape[0]
    depth = 2 * mine.shape[2]
    tiles = partial.shape[2] // 128
    opposite[:half] = first[...]
    opposite[half:] = second[...]

    def rows(b, carry):
        total = None
        for slot, weight in enumerate((own, following, opposite, previous)):
            at = lax.rem(x + slot, 4) * 4 + b
            left = jnp.where(core == 0, mine[at], other[at])
            right = jnp.where(core == 0, other[at], mine[at])
            wide = jnp.concatenate([weight[k * depth : (k + 1) * depth] for k in range(tiles)], axis=1)
            term = dot(jnp.concatenate([left, right], axis=1), wide)
            total = term if total is None else total + term
        partial[b] = total.astype(BF16)

        @pl.when(b == h)
        def _():
            kept[...] = total

        return carry

    lax.fori_loop(0, 4, rows, 0)


def hidden_kernel(parts, own_part, out):
    h = lax.axis_index("h")
    copies, _, ff = out.shape
    sums = own_part[...]
    for source in range(4):
        part = parts[source].astype(F32)
        sums = sums + jnp.where(source == h, jnp.zeros_like(part), part)
    even = ff // 128 * 128
    gate, up, tail = sums[:, :even], sums[:, even : 2 * even], sums[:, 2 * even :]
    wide = (gate / (1.0 + jnp.exp(-gate)) * up).astype(BF16)
    gate, up = tail[:, : ff - even], tail[:, ff - even :]
    last = (gate / (1.0 + jnp.exp(-gate)) * up).astype(BF16)
    for k in range(copies):
        out[k, :, :even] = wide
        out[k, :, even:] = last


def down_kernel(hidden, own, following, second, previous, kept, given):
    x, core = lax.axis_index("x"), lax.axis_index("c")
    blocks, rows, ff = hidden.shape
    half = rows // 2
    tiles = kept.shape[2] // 128
    mine = pl.ds(pl.multiple_of(core * half, 16), half)
    other = pl.ds(pl.multiple_of((1 - core) * half, 16), half)
    lhs = jnp.concatenate([hidden[k, part] for part in (mine, other) for k in range(blocks)], axis=0)
    for slot, weight in enumerate((own, following, second, previous)):
        base = weight.shape[0] - tiles * ff
        wide = jnp.concatenate([weight[base + t * ff : base + (t + 1) * ff] for t in range(tiles)], axis=1)
        terms = dot(lhs, wide)
        at = lax.rem(x + slot, 4) * blocks
        for k in range(blocks):
            kept[at + k] = terms[k * half : (k + 1) * half]
            given[at + k] = terms[(blocks + k) * half : (blocks + k + 1) * half].astype(BF16)


def local(tokens, gate_weight, up_weight, down_weight, decode_in):
    yz = lax.axis_index(("l", "a", "b", "c"))
    steps, rows, _ = decode_in.shape
    depth, ff = gate_weight.shape
    n_rows, block = tokens.shape
    n_dec = steps * rows
    width = down_weight.shape[1]
    each = -(-(n_rows + n_dec) // 32) * 16
    total = 2 * each
    fill = each - (n_rows + n_dec) // 2

    decode_part = lax.dynamic_slice_in_dim(decode_in, yz * block, block, 2)
    feats = jnp.concatenate(
        [
            tokens.reshape(16, 2, 4, block).transpose(1, 0, 2, 3).reshape(2, n_rows // 2, block),
            decode_part.reshape(steps, 2, rows // 2, block).transpose(1, 0, 2, 3).reshape(2, n_dec // 2, block),
            jnp.zeros((2, fill, block), BF16),
        ],
        axis=1,
    ).reshape(total, block)
    feats = lax.ppermute(
        feats, ("h", "b"), [(h * 4 + b, b * 4 + h) for h in range(4) for b in range(4)]
    )
    feats = exchange(jnp.broadcast_to(feats, (16, total, block)), LZ)
    pieces = (2 * ff // 128 * depth + width // 128 * ff, 128)
    own = call(weights_kernel, jax.ShapeDtypeStruct(pieces, BF16), 1)(gate_weight, up_weight, down_weight)
    own_near = near(own, "x")
    own_far = far(*own_near, "x", HINTS[0])
    other = swap_cores(feats)

    partial, kept = call(
        gate_up_kernel,
        (
            jax.ShapeDtypeStruct((4, total, 2 * ff), BF16),
            jax.ShapeDtypeStruct((total, 2 * ff), F32),
        ),
        HINTS[1],
        [pltpu.VMEM(pieces, BF16)],
    )(feats, other, own, own_near[0], *own_far, own_near[1])
    parts = exchange(partial, "h")
    hidden = call(hidden_kernel, jax.ShapeDtypeStruct((4, total, ff), BF16), 2)(parts, kept)
    hidden = exchange(hidden, "h")
    kept, given = call(
        down_kernel,
        (
            jax.ShapeDtypeStruct((16, each, width), F32),
            jax.ShapeDtypeStruct((16, each, width), BF16),
        ),
        2,
    )(hidden, own, own_near[0], own_far[1], own_near[1])
    sums = (kept + swap_cores(given).astype(F32)).astype(BF16)

    half = n_rows // 2
    prefill = sums[:, :half].reshape(16, 16, 4, width).transpose(1, 0, 2, 3).reshape(16, half, width)
    sums = exchange(jnp.concatenate([prefill, sums[:, half:]], axis=1), LZ)
    sums = sums.astype(F32).sum(0).astype(BF16)
    decode_out = lax.ppermute(
        sums[half : half + n_dec // 2],
        ("x", "l", "a"),
        [(i * 4 + j, j * 4 + i) for i in range(4) for j in range(4)],
    ).reshape(steps, rows // 2, width)
    prefill_out = exchange(sums[:half].reshape(4, 4, 4, width).transpose(1, 0, 2, 3), "h")
    prefill_out = prefill_out.transpose(2, 1, 0, 3).reshape(4, 16 * width)
    return prefill_out, decode_out


def solution(mesh):
    sizes = [size for _, size in SIZES]
    fine = Mesh(mesh.devices.reshape(sizes), [name for name, _ in SIZES])
    gx, yz = GX, ("l", "a", "b", "c")
    return jax.shard_map(
        local,
        mesh=fine,
        in_specs=(P(gx, yz), P(gx, yz), P(gx, yz), P(yz, gx), P(None, gx, None)),
        out_specs=(P(gx + yz, None), P(None, yz, gx)),
        check_vma=False,
    )
```

time: 202 us -> 167 us (0.83)
  starting transfers between devices: 12.3 us -> 46.1 us
  blocking collectives: 112 us -> 78.8 us
  waiting for transfers between devices: 49.3 us -> 30.4 us
  between operations: 14.4 us -> 0.93 us
  matrix products: 5.89 us -> 0 us
  Pallas kernels: 0 us -> 3.61 us
  other arithmetic: 3.25 us -> 0.45 us
    all_gather x2 -> x0, waiting for transfers between devices: 35.6 us -> none  [the longest x1 35.6 us: local(): down = lax.all_gather(both.reshape(2 * ff, block), GX, axis=0, tiled=False)]
    all_to_all x3, blocking collectives: 112 us -> 78.8 us  [exchange(): return lax.all_to_all(blocks, axes, split_axis=0, concat_axis=0, tiled=True)]
    all_to_all x0 -> x2, starting transfers between devices: none -> 26.1 us  [exchange(): return lax.all_to_all(blocks, axes, split_axis=0, concat_axis=0, tiled=True)]
    ppermute x1 -> x5, starting transfers between devices: 3.94 us -> 15.5 us  [the longest x2 5.84 us: near(): return (lax.ppermute(value, axis, DOWN), lax.ppermute(value, axis, UP))]
    ppermute x1 -> x5, waiting for transfers between devices: 7.87 us -> 19.4 us  [the longest x1 8.65 us: local(): lax.ppermute(sums[half:half + n_dec // 2], ('x', 'l', 'a'), [(i * 4 + j,...]
    all_to_all x0 -> x2, waiting for transfers between devices: none -> 8.96 us  [exchange(): return lax.all_to_all(blocks, axes, split_axis=0, concat_axis=0, tiled=True)]
    dot_general x2 -> x0, matrix products: 5.89 us -> none  [the longest x1 2.98 us: local(): partial = jnp.dot(feats, gate_up, preferred_element_type=F32).astype(BF16)]
    ppermute x4 -> x2, starting transfers between devices: 7.67 us -> 3.83 us  [swap_cores(): return lax.ppermute(value, 'c', [(0, 1), (1, 0)])]
  transfers between devices with their start and end apart: 8 -> 10, of which waited for: 6 -> 7; matrix products, arithmetic and copies ran while one was open for 4% -> 1% of each run, Pallas kernels for 0% -> 0%
where the time goes in v2:
time: 167 us; the launch traced here: 166 us
  blocking collectives  78.8 us (47%)
  starting transfers between devices  46.1 us (28%)
  waiting for transfers between devices  30.4 us (18%)
  local copies, waits for them, and re-layouts  5.43 us (3%)
  Pallas kernels  3.61 us (2%)
    all_to_all x3, blocking collectives, exchange(): return lax.all_to_all(blocks, axes, split_axis=0, concat_axis=0, tiled=True)  78.8 us
    all_to_all x2, starting transfers between devices, exchange(): return lax.all_to_all(blocks, axes, split_axis=0, concat_axis=0, tiled=True)  26.1 us
    all_to_all x2, waiting for transfers between devices, exchange(): return lax.all_to_all(blocks, axes, split_axis=0, concat_axis=0, tiled=True)  8.96 us
    ppermute x1, waiting for transfers between devices, local(): lax.ppermute(sums[half:half + n_dec // 2], ('x', 'l', 'a'), [(i * 4 + j,...  8.65 us
    ppermute x2, waiting for transfers between devices, far(): return (lax.ppermute(up, axis, UP), lax.ppermute(down, axis, DOWN))  6.69 us
    ppermute x2, starting transfers between devices, near(): return (lax.ppermute(value, axis, DOWN), lax.ppermute(value, axis, UP))  5.84 us
    ppermute x2, starting transfers between devices, far(): return (lax.ppermute(up, axis, UP), lax.ppermute(down, axis, DOWN))  5.84 us
    ppermute x2, waiting for transfers between devices, near(): return (lax.ppermute(value, axis, DOWN), lax.ppermute(value, axis, UP))  4.05 us
  transfers between devices with their start and end apart: 10, of which 7 were waited for; matrix products, arithmetic and copies ran while one was open for 1% of the time, Pallas kernels for 0%

profile of v2, /device:TPU:6, one launch (start us, length us, event | category | flops | bytes accessed | tf_op | source)
XLA Modules:
  0.0 165.7 jit_solution(18299442134627456820)
XLA Ops:
  0.7 0.9 copy-done
  1.6 0.8 copy.27
  3.2 0.9 broadcast_in_dim.7
  4.2 22.7 %all-to-all-start = ((bf16[16,160,128]{2,1,0:T(8,128)(2,1)}), bf16[16,160,128]{2,1,0:T(8,128)(2,1)S(1)}, u32[]{:S(2)}, u32[]{:S(2)}) async-start(bf16[16,160,128]{2,1,0:T(8,128)(2,1)} %broadcast_in_dim.7), calls=%async_computation | async-start | bytes 1310720 | tf_op jit(solution)/shard_map/all_to_all | solution.py:24
  27.3 2.4 %collective-permute-start.3 = (bf16[2688,128]{1,0:T(8,128)(2,1)S(1)}, bf16[2688,128]{1,0:T(8,128)(2,1)S(1)}, u32[]{:S(2)}, u32[]{:S(2)}) collective-permute-start(bf16[2688,128]{1,0:T(8,128)(2,1)S(1)} %shard_map.68.own), channel_id=1, source_target_pairs={{0,128},{128,256},{256,384},{384,0},{1,129},{129,257},{257,385},{3... | collective-permute-start | bytes 2064392 | tf_op jit(solution)/shard_map/ppermute | solution.py:28
  29.7 3.5 %collective-permute-start.2 = (bf16[2688,128]{1,0:T(8,128)(2,1)S(1)}, bf16[2688,128]{1,0:T(8,128)(2,1)S(1)}, u32[]{:S(2)}, u32[]{:S(2)}) collective-permute-start(bf16[2688,128]{1,0:T(8,128)(2,1)S(1)} %shard_map.68.own), channel_id=1, source_target_pairs={{0,384},{128,0},{256,128},{384,256},{1,385},{129,1},{257,129},{385... | collective-permute-start | bytes 2064392 | tf_op jit(solution)/shard_map/ppermute | solution.py:28
  33.1 9.0 %all-to-all-done.mine = bf16[16,160,128]{2,1,0:T(8,128)(2,1)S(1)} async-done(((bf16[16,160,128]{2,1,0:T(8,128)(2,1)}), bf16[16,160,128]{2,1,0:T(8,128)(2,1)S(1)}, u32[]{:S(2)}, u32[]{:S(2)}) %all-to-all-start) | async-done | bytes 655392 | tf_op jit(solution)/shard_map/all_to_all | solution.py:24
  42.1 1.9 %collective-permute-start.1 = (bf16[16,160,128]{2,1,0:T(8,128)(2,1)S(1)}, bf16[16,160,128]{2,1,0:T(8,128)(2,1)S(1)}, u32[]{:S(2)}, u32[]{:S(2)}) collective-permute-start(bf16[16,160,128]{2,1,0:T(8,128)(2,1)S(1)} %all-to-all-done.mine), channel_id=1, source_target_pairs={{0,1},{1,0},{2,3},{3,2},{4,5},{5,4},{6,7},{7,6},{8,9},{9,8},{10,11... | collective-permute-start | bytes 1966088 | tf_op jit(solution)/shard_map/ppermute | solution.py:20
  44.0 0.7 collective-permute-done.3.previous
  44.7 3.3 %collective-permute-done.2.following = bf16[2688,128]{1,0:T(8,128)(2,1)S(1)} collective-permute-done((bf16[2688,128]{1,0:T(8,128)(2,1)S(1)}, bf16[2688,128]{1,0:T(8,128)(2,1)S(1)}, u32[]{:S(2)}, u32[]{:S(2)}) %collective-permute-start.2) | collective-permute-done | bytes 688160 | tf_op jit(solution)/shard_map/ppermute | solution.py:28
  48.1 2.2 %collective-permute-start.4 = (bf16[1344,128]{1,0:T(8,128)(2,1)S(1)}, bf16[1344,128]{1,0:T(8,128)(2,1)S(1)}, u32[]{:S(2)}, u32[]{:S(2)}) collective-permute-start(bf16[1344,128]{1,0:T(8,128)(2,1)S(1)} %get-tuple-element.8), channel_id=1, source_target_pairs={{0,128},{128,256},{256,384},{384,0},{1,129},{129,257},{257,385},{3... | collective-permute-start | bytes 1032200 | tf_op jit(solution)/shard_map/ppermute | solution.py:35
  50.3 3.7 %collective-permute-start.5 = (bf16[1344,128]{1,0:T(8,128)(2,1)S(1)}, bf16[1344,128]{1,0:T(8,128)(2,1)S(1)}, u32[]{:S(2)}, u32[]{:S(2)}) collective-permute-start(bf16[1344,128]{1,0:T(8,128)(2,1)S(1)} %get-tuple-element.9), channel_id=1, source_target_pairs={{0,384},{128,0},{256,128},{384,256},{1,385},{129,1},{257,129},{385... | collective-permute-start | bytes 1032200 | tf_op jit(solution)/shard_map/ppermute | solution.py:35
  54.0 3.3 %collective-permute-done.4.first = bf16[1344,128]{1,0:T(8,128)(2,1)S(1)} collective-permute-done((bf16[1344,128]{1,0:T(8,128)(2,1)S(1)}, bf16[1344,128]{1,0:T(8,128)(2,1)S(1)}, u32[]{:S(2)}, u32[]{:S(2)}) %collective-permute-start.4) | collective-permute-done | bytes 344096 | tf_op jit(solution)/shard_map/ppermute | solution.py:35
  57.3 3.4 %collective-permute-done.5.second = bf16[1344,128]{1,0:T(8,128)(2,1)S(1)} collective-permute-done((bf16[1344,128]{1,0:T(8,128)(2,1)S(1)}, bf16[1344,128]{1,0:T(8,128)(2,1)S(1)}, u32[]{:S(2)}, u32[]{:S(2)}) %collective-permute-start.5) | collective-permute-done | bytes 344096 | tf_op jit(solution)/shard_map/ppermute | solution.py:35
  60.7 2.1 %shard_map.70 = (bf16[4,160,896]{2,1,0:T(8,128)(2,1)S(1)}, f32[160,896]{1,0:T(8,128)S(1)}) custom-call(bf16[16,160,128]{2,1,0:T(8,128)(2,1)S(1)} %all-to-all-done.mine, bf16[16,160,128]{2,1,0:T(8,128)(2,1)S(1)} %collective-permute-done.1.other, bf16[2688,128]{1,0:T(8,128)(2,1)S(1)} %shard_map.68.own, bf16[2688,128]{1,0:T(8,128)(2,1)S(1)} %collective-permute-done.2.following, ...), custom_call_target="tpu_custom_call" | custom-call | flops 3300000000 | bytes 1048576 | tf_op jit(solution)/shard_map/pallas_call | solution.py:165
  62.8 28.9 %all_to_all.25.parts = bf16[4,160,896]{2,1,0:T(8,128)(2,1)S(1)} all-to-all(bf16[4,160,896]{2,1,0:T(8,128)(2,1)S(1)} %get-tuple-element.10), channel_id=1, replica_groups=mesh['x'=4,'h'=4,'l'=2,'a'=2,'b'=4,'c'=2] {'h'}, dimensions={0} | all-to-all | bytes 2293760 | tf_op jit(solution)/shard_map/all_to_all | solution.py:24
  92.2 21.2 %all_to_all.26.hidden = bf16[4,160,448]{2,1,0:T(8,128)(2,1)S(1)} all-to-all(bf16[4,160,448]{2,1,0:T(8,128)(2,1)S(1)} %shard_map.71), channel_id=1, replica_groups=mesh['x'=4,'h'=4,'l'=2,'a'=2,'b'=4,'c'=2] {'h'}, dimensions={0} | all-to-all | bytes 1146880 | tf_op jit(solution)/shard_map/all_to_all | solution.py:24
  113.4 0.8 shard_map.72
  114.3 1.9 %collective-permute-start.6 = (bf16[16,80,256]{2,1,0:T(8,128)(2,1)S(1)}, bf16[16,80,256]{2,1,0:T(8,128)(2,1)S(1)}, u32[]{:S(2)}, u32[]{:S(2)}) collective-permute-start(bf16[16,80,256]{2,1,0:T(8,128)(2,1)S(1)} %get-tuple-element.13), channel_id=1, source_target_pairs={{0,1},{1,0},{2,3},{3,2},{4,5},{5,4},{6,7},{7,6},{8,9},{9,8},{10,11... | collective-permute-start | bytes 1966088 | tf_op jit(solution)/shard_map/ppermute | solution.py:20
  116.2 2.1 %collective-permute-done.6 = bf16[16,80,256]{2,1,0:T(8,128)(2,1)S(1)} collective-permute-done((bf16[16,80,256]{2,1,0:T(8,128)(2,1)S(1)}, bf16[16,80,256]{2,1,0:T(8,128)(2,1)S(1)}, u32[]{:S(2)}, u32[]{:S(2)}) %collective-permute-start.6) | collective-permute-done | bytes 655392 | tf_op jit(solution)/shard_map/ppermute | solution.py:20
  119.1 28.7 %all_to_all.27 = bf16[16,80,256]{2,1,0:T(8,128)(2,1)S(1)} all-to-all(bf16[16,80,256]{2,1,0:T(8,128)(2,1)S(1)} %copy.34), channel_id=1, replica_groups=mesh['x'=4,'h'=4,'l'=2,'a'=2,'b'=4,'c'=2] {'l','a','b'}, dimensions={0} | all-to-all | bytes 1310720 | tf_op jit(solution)/shard_map/all_to_all | solution.py:24
  148.5 3.5 %all-to-all-start.4 = ((bf16[4,4,4,256]{3,2,1,0:T(4,128)(2,1)}), bf16[4,4,4,256]{3,2,1,0:T(4,128)(2,1)S(1)}, u32[]{:S(2)}, u32[]{:S(2)}) async-start(bf16[4,4,4,256]{3,2,1,0:T(4,128)(2,1)} %copy.35), calls=%async_computation.4 | async-start | bytes 65536 | tf_op jit(solution)/shard_map/all_to_all | solution.py:24
  152.0 3.8 %collective-permute-start.7 = (bf16[12,256]{1,0:T(8,128)(2,1)S(1)}, bf16[12,256]{1,0:T(8,128)(2,1)S(1)}, u32[]{:S(2)}, u32[]{:S(2)}) collective-permute-start(bf16[12,256]{1,0:T(8,128)(2,1)S(1)} %slice.19), channel_id=1, source_target_pairs={{0,0},{8,128},{16,256},{24,384},{128,8},{136,136},{144,264},{152,3... | collective-permute-start | bytes 18440 | tf_op jit(solution)/shard_map/ppermute | solution.py:191
  155.8 8.7 %collective-permute-done.7 = bf16[12,256]{1,0:T(8,128)(2,1)S(1)} collective-permute-done((bf16[12,256]{1,0:T(8,128)(2,1)S(1)}, bf16[12,256]{1,0:T(8,128)(2,1)S(1)}, u32[]{:S(2)}, u32[]{:S(2)}) %collective-permute-start.7) | collective-permute-done | bytes 6176 | tf_op jit(solution)/shard_map/ppermute | solution.py:191
  (39 shorter events, 4.6 us)
Async XLA Ops:
  0.6 0.9 copy-start
  0.6 26.2 %copy-start.2 = (bf16[256,448]{0,1:T(8,128)(2,1)S(1)}, bf16[256,448]{0,1:T(8,128)(2,1)}, u32[]{:S(2)}) copy-start(bf16[256,448]{0,1:T(8,128)(2,1)} %param.6) | copy-start | bytes 688132
  2.4 24.6 %copy-start.3 = (bf16[256,448]{0,1:T(8,128)(2,1)S(1)}, bf16[256,448]{0,1:T(8,128)(2,1)}, u32[]{:S(2)}) copy-start(bf16[256,448]{0,1:T(8,128)(2,1)} %param.7) | copy-start | bytes 688132
  2.6 0.7 collective-permute-start
  4.2 23.0 %copy-start.1 = (bf16[448,256]{1,0:T(8,128)(2,1)S(1)}, bf16[448,256]{1,0:T(8,128)(2,1)}, u32[]{:S(2)}) copy-start(bf16[448,256]{1,0:T(8,128)(2,1)} %down.1) | copy-start | bytes 688132
  4.2 37.9 %all-to-all-start = ((bf16[16,160,128]{2,1,0:T(8,128)(2,1)}), bf16[16,160,128]{2,1,0:T(8,128)(2,1)S(1)}, u32[]{:S(2)}, u32[]{:S(2)}) async-start(bf16[16,160,128]{2,1,0:T(8,128)(2,1)} %broadcast_in_dim.7), calls=%async_computation | async-start | bytes 1310720 | tf_op jit(solution)/shard_map/all_to_all | solution.py:24
  27.3 17.5 %collective-permute-start.3 = (bf16[2688,128]{1,0:T(8,128)(2,1)S(1)}, bf16[2688,128]{1,0:T(8,128)(2,1)S(1)}, u32[]{:S(2)}, u32[]{:S(2)}) collective-permute-start(bf16[2688,128]{1,0:T(8,128)(2,1)S(1)} %shard_map.68.own), channel_id=1, source_target_pairs={{0,128},{128,256},{256,384},{384,0},{1,129},{129,257},{257,385},{3... | collective-permute-start | bytes 2064392 | tf_op jit(solution)/shard_map/ppermute | solution.py:28
  29.7 18.4 %collective-permute-start.2 = (bf16[2688,128]{1,0:T(8,128)(2,1)S(1)}, bf16[2688,128]{1,0:T(8,128)(2,1)S(1)}, u32[]{:S(2)}, u32[]{:S(2)}) collective-permute-start(bf16[2688,128]{1,0:T(8,128)(2,1)S(1)} %shard_map.68.own), channel_id=1, source_target_pairs={{0,384},{128,0},{256,128},{384,256},{1,385},{129,1},{257,129},{385... | collective-permute-start | bytes 2064392 | tf_op jit(solution)/shard_map/ppermute | solution.py:28
  42.1 18.6 %collective-permute-start.1 = (bf16[16,160,128]{2,1,0:T(8,128)(2,1)S(1)}, bf16[16,160,128]{2,1,0:T(8,128)(2,1)S(1)}, u32[]{:S(2)}, u32[]{:S(2)}) collective-permute-start(bf16[16,160,128]{2,1,0:T(8,128)(2,1)S(1)} %all-to-all-done.mine), channel_id=1, source_target_pairs={{0,1},{1,0},{2,3},{3,2},{4,5},{5,4},{6,7},{7,6},{8,9},{9,8},{10,11... | collective-permute-start | bytes 1966088 | tf_op jit(solution)/shard_map/ppermute | solution.py:20
  48.1 9.1 %collective-permute-start.4 = (bf16[1344,128]{1,0:T(8,128)(2,1)S(1)}, bf16[1344,128]{1,0:T(8,128)(2,1)S(1)}, u32[]{:S(2)}, u32[]{:S(2)}) collective-permute-start(bf16[1344,128]{1,0:T(8,128)(2,1)S(1)} %get-tuple-element.8), channel_id=1, source_target_pairs={{0,128},{128,256},{256,384},{384,0},{1,129},{129,257},{257,385},{3... | collective-permute-start | bytes 1032200 | tf_op jit(solution)/shard_map/ppermute | solution.py:35
  50.3 10.4 %collective-permute-start.5 = (bf16[1344,128]{1,0:T(8,128)(2,1)S(1)}, bf16[1344,128]{1,0:T(8,128)(2,1)S(1)}, u32[]{:S(2)}, u32[]{:S(2)}) collective-permute-start(bf16[1344,128]{1,0:T(8,128)(2,1)S(1)} %get-tuple-element.9), channel_id=1, source_target_pairs={{0,384},{128,0},{256,128},{384,256},{1,385},{129,1},{257,129},{385... | collective-permute-start | bytes 1032200 | tf_op jit(solution)/shard_map/ppermute | solution.py:35
  114.3 4.0 %collective-permute-start.6 = (bf16[16,80,256]{2,1,0:T(8,128)(2,1)S(1)}, bf16[16,80,256]{2,1,0:T(8,128)(2,1)S(1)}, u32[]{:S(2)}, u32[]{:S(2)}) collective-permute-start(bf16[16,80,256]{2,1,0:T(8,128)(2,1)S(1)} %get-tuple-element.13), channel_id=1, source_target_pairs={{0,1},{1,0},{2,3},{3,2},{4,5},{5,4},{6,7},{7,6},{8,9},{9,8},{10,11... | collective-permute-start | bytes 1966088 | tf_op jit(solution)/shard_map/ppermute | solution.py:20
  148.5 16.5 %all-to-all-start.4 = ((bf16[4,4,4,256]{3,2,1,0:T(4,128)(2,1)}), bf16[4,4,4,256]{3,2,1,0:T(4,128)(2,1)S(1)}, u32[]{:S(2)}, u32[]{:S(2)}) async-start(bf16[4,4,4,256]{3,2,1,0:T(4,128)(2,1)} %copy.35), calls=%async_computation.4 | async-start | bytes 65536 | tf_op jit(solution)/shard_map/all_to_all | solution.py:24
  152.0 12.4 %collective-permute-start.7 = (bf16[12,256]{1,0:T(8,128)(2,1)S(1)}, bf16[12,256]{1,0:T(8,128)(2,1)S(1)}, u32[]{:S(2)}, u32[]{:S(2)}) collective-permute-start(bf16[12,256]{1,0:T(8,128)(2,1)S(1)} %slice.19), channel_id=1, source_target_pairs={{0,0},{8,128},{16,256},{24,384},{128,8},{136,136},{144,264},{152,3... | collective-permute-start | bytes 18440 | tf_op jit(solution)/shard_map/ppermute | solution.py:191

commit v3 on v2

v3 whole, which is shorter than its diff:
```python
import jax
import jax.numpy as jnp
from jax import lax
from jax.experimental import pallas as pl
from jax.experimental.pallas import tpu as pltpu
from jax.sharding import Mesh, PartitionSpec as P

BF16 = jnp.bfloat16
F32 = jnp.float32
SIZES = (("x", 4), ("h", 4), ("l", 2), ("a", 2), ("b", 4), ("c", 2))
GX = ("x", "h")
LZ = ("l", "a", "b")
UP = [(i, (i + 1) % 4) for i in range(4)]
DOWN = [(i, (i + 3) % 4) for i in range(4)]
VMEM = 16 * 2**20
HINTS = (5.5, 0.1, 1, 8, 5)


def swap_cores(value):
    return lax.ppermute(value, "c", [(0, 1), (1, 0)])


def exchange(blocks, axes):
    return lax.all_to_all(blocks, axes, split_axis=0, concat_axis=0, tiled=True)


def near(value, axis):
    return lax.ppermute(value, axis, DOWN), lax.ppermute(value, axis, UP)


def far(following, previous, axis, hint):
    shape = previous.shape[:-2] + (previous.shape[-2] // 2, previous.shape[-1])
    halves = jax.ShapeDtypeStruct(shape, BF16)
    up, down = call(halves_kernel, (halves, halves), hint)(previous, following)
    return lax.ppermute(up, axis, UP), lax.ppermute(down, axis, DOWN)


def call(kernel, outs, hint, scratch=(), vmem=VMEM, **more):
    return pl.pallas_call(
        kernel,
        out_shape=outs,
        scratch_shapes=list(scratch),
        compiler_params=pltpu.CompilerParams(vmem_limit_bytes=vmem),
        cost_estimate=pl.CostEstimate(flops=int(hint * 1.1e9), bytes_accessed=2**20, transcendentals=0),
        **more,
    )


def dot(lhs, rhs):
    return jnp.dot(lhs, rhs, preferred_element_type=F32)


def weights_kernel(gate, up, out):
    ff = gate.shape[0]
    even = ff // 128 * 128
    out[:even] = gate[:even]
    out[even : 2 * even] = up[:even]
    out[2 * even : even + ff] = gate[even:]
    out[even + ff :] = up[even:]


def halves_kernel(previous, following, up, down):
    half = up.shape[-2]
    up[...] = previous[..., :half, :]
    down[...] = following[..., half:, :]


def pair_kernel(own, opposite, out):
    out[0] = own[...]
    out[1] = opposite[...]


def gate_up_kernel(mine, other, own, following, first, second, previous, partial, residue):
    x, h, core = lax.axis_index("x"), lax.axis_index("h"), lax.axis_index("c")
    blocks, rows, _ = partial.shape
    opposite = jnp.concatenate([first[...], second[...]], axis=0)
    total = None
    for slot, weight in enumerate((own[...], following[...], opposite, previous[...])):
        lhs = []
        for b in range(blocks):
            at = lax.rem(x + slot, 4) * 4 + b
            left = jnp.where(core == 0, mine[at], other[at])
            right = jnp.where(core == 0, other[at], mine[at])
            lhs.append(jnp.concatenate([left, right], axis=1))
        term = lax.dot_general(
            jnp.concatenate(lhs, axis=0), weight, (((1,), (1,)), ((), ())), preferred_element_type=F32
        )
        total = term if total is None else total + term
    for b in range(blocks):
        part = total[b * rows : (b + 1) * rows]
        rounded = part.astype(BF16)
        partial[b] = rounded

        @pl.when(b == h)
        def _():
            residue[...] = (part - rounded.astype(F32)).astype(BF16)


def hidden_kernel(parts, residue, out):
    ff = out.shape[1]
    sums = residue[...].astype(F32)
    for source in range(4):
        sums = sums + parts[source].astype(F32)
    even = ff // 128 * 128
    gate, up, tail = sums[:, :even], sums[:, even : 2 * even], sums[:, 2 * even :]
    out[:, :even] = (gate / (1.0 + jnp.exp(-gate)) * up).astype(BF16)
    gate, up = tail[:, : ff - even], tail[:, ff - even :]
    out[:, even:] = (gate / (1.0 + jnp.exp(-gate)) * up).astype(BF16)


def down_kernel(hidden, partner, own, following, first, second, previous, kept, given):
    x, core = lax.axis_index("x"), lax.axis_index("c")
    half = hidden.shape[0] // 2
    mine = pl.ds(pl.multiple_of(core * half, 16), half)
    other = pl.ds(pl.multiple_of((1 - core) * half, 16), half)
    lhs = jnp.concatenate([ref[part] for part in (mine, other) for ref in (hidden, partner)], axis=0)
    for slot in range(4):
        for k in range(2):
            if slot == 2:
                weight = jnp.concatenate([first[k], second[k]], axis=0)
            else:
                weight = (own, following, None, previous)[slot][k]
            terms = dot(lhs, weight)
            at = lax.rem(x + slot, 4) * 4 + k * 2
            for r in range(2):
                kept[at + r] = terms[r * half : (r + 1) * half]
                given[at + r] = terms[(2 + r) * half : (3 + r) * half].astype(BF16)


def decode_kernel(rows, out):
    steps = out.shape[1]
    wide = rows[...].astype(F32)
    for i in range(out.shape[0]):
        out[i] = wide[i * steps : (i + 1) * steps].astype(BF16)


def local(tokens, gate_weight, up_weight, down_weight, decode_in):
    yz = lax.axis_index(("l", "a", "b", "c"))
    steps, rows, _ = decode_in.shape
    depth, ff = gate_weight.shape
    n_rows, block = tokens.shape
    n_dec = steps * rows
    width = down_weight.shape[1]
    each = -(-(n_rows + n_dec) // 32) * 16
    total = 2 * each
    fill = each - (n_rows + n_dec) // 2

    decode_part = lax.dynamic_slice_in_dim(decode_in, yz * block, block, 2)
    feats = jnp.concatenate(
        [
            tokens.reshape(16, 2, 4, block).transpose(1, 0, 2, 3).reshape(2, n_rows // 2, block),
            decode_part.transpose(1, 0, 2).reshape(2, n_dec // 2, block),
            jnp.zeros((2, fill, block), BF16),
        ],
        axis=1,
    ).reshape(total, block)
    feats = lax.ppermute(
        feats, ("h", "b"), [(h * 4 + b, b * 4 + h) for h in range(4) for b in range(4)]
    )
    feats = exchange(jnp.broadcast_to(feats, (16, total, block)), LZ)
    own = call(weights_kernel, jax.ShapeDtypeStruct((2 * ff, depth), BF16), 1)(
        gate_weight.T, up_weight.T
    )
    own_near = near(own, "x")
    own_far = far(*own_near, "x", HINTS[0])
    opposite = lax.ppermute(down_weight, "h", [(i, (i + 2) % 4) for i in range(4)])
    feats, own_far = lax.optimization_barrier((feats, own_far))
    other = swap_cores(feats)
    down = call(pair_kernel, jax.ShapeDtypeStruct((2, ff, width), BF16), HINTS[3])(down_weight, opposite)
    other, down = lax.optimization_barrier((other, down))

    partial, residue = call(
        gate_up_kernel,
        (
            jax.ShapeDtypeStruct((4, total, 2 * ff), BF16),
            jax.ShapeDtypeStruct((total, 2 * ff), BF16),
        ),
        HINTS[1],
    )(feats, other, own, own_near[0], *own_far, own_near[1])
    parts = exchange(partial, "h")
    hidden = call(hidden_kernel, jax.ShapeDtypeStruct((total, ff), BF16), 1)(parts, residue)
    beside = [(0, 1), (1, 0), (2, 3), (3, 2)]
    partner = lax.ppermute(hidden, "h", beside)
    down_near = near(down, "x")
    down_far = far(*down_near, "x", HINTS[2])
    kept, given = call(
        down_kernel,
        (
            jax.ShapeDtypeStruct((16, each, width), F32),
            jax.ShapeDtypeStruct((16, each, width), BF16),
        ),
        2,
    )(hidden, partner, down, down_near[0], *down_far, down_near[1])
    sums = (kept + swap_cores(given).astype(F32)).astype(BF16)

    half = n_rows // 2
    prefill = sums[:, :half].reshape(16, 16, 4, width).transpose(1, 0, 2, 3).reshape(16, half, width)
    sums = exchange(jnp.concatenate([prefill, sums[:, half:]], axis=1), LZ)
    sums = sums.astype(F32).sum(0).astype(BF16)
    decode_out = lax.ppermute(
        sums[half : half + n_dec // 2],
        ("x", "h", "l", "a", "b"),
        [
            (
                x * 64 + h * 16 + q * 4 + k * 2 + r,
                q * 64 + (h ^ 2 * k) * 16 + x * 4 + (h ^ r),
            )
            for x in range(4)
            for h in range(4)
            for q in range(4)
            for k in range(2)
            for r in range(2)
        ],
    )
    decode_out = call(decode_kernel, jax.ShapeDtypeStruct((rows // 2, steps, width), BF16), HINTS[4])(decode_out)
    decode_out = decode_out.transpose(1, 0, 2)
    h = lax.axis_index("h")
    mine = sums[:half].reshape(4, 2, 2, 4, width)
    theirs = lax.ppermute(mine[:, :, 1], "h", beside)
    both = jnp.stack([mine[:, :, 0], theirs], axis=2)
    both = jnp.where(h % 2 == 1, both[:, :, ::-1], both)
    both = jnp.where(h // 2 == 1, both[:, ::-1], both)
    prefill_out = both.transpose(3, 0, 1, 2, 4).reshape(4, 16 * width)
    return prefill_out, decode_out


def solution(mesh):
    sizes = [size for _, size in SIZES]
    fine = Mesh(mesh.devices.reshape(sizes), [name for name, _ in SIZES])
    gx, yz = GX, ("l", "a", "b", "c")
    return jax.shard_map(
        local,
        mesh=fine,
        in_specs=(P(gx, yz), P(gx, yz), P(gx, yz), P(yz, gx), P(None, gx, None)),
        out_specs=(P(gx + yz, None), P(None, yz, gx)),
        check_vma=False,
    )
```

time: 167 us -> 150 us (0.90)
  blocking collectives: 78.8 us -> 0 us
  starting transfers between devices: 46.1 us -> 89.7 us
  waiting for transfers between devices: 30.4 us -> 41.7 us
  local copies, waits for them, and re-layouts: 5.43 us -> 8.27 us
  Pallas kernels: 3.61 us -> 6.4 us
    all_to_all x3 -> x0, blocking collectives: 78.8 us -> none  [exchange(): return lax.all_to_all(blocks, axes, split_axis=0, concat_axis=0, tiled=True)]
    ppermute x1 -> x4, starting transfers between devices: 3.79 us -> 25.8 us  [the longest x1 8.01 us: local(): partner = lax.ppermute(hidden, 'h', beside)]
    all_to_all x2 -> x3, waiting for transfers between devices: 8.96 us -> 21.9 us  [exchange(): return lax.all_to_all(blocks, axes, split_axis=0, concat_axis=0, tiled=True)]
    ppermute x2 -> x4, starting transfers between devices: 5.84 us -> 16.7 us  [near(): return (lax.ppermute(value, axis, DOWN), lax.ppermute(value, axis, UP))]
    ppermute x2 -> x4, starting transfers between devices: 5.84 us -> 13.4 us  [far(): return (lax.ppermute(up, axis, UP), lax.ppermute(down, axis, DOWN))]
    ppermute x2 -> x4, waiting for transfers between devices: 6.69 us -> 1.49 us  [far(): return (lax.ppermute(up, axis, UP), lax.ppermute(down, axis, DOWN))]
    all_to_all x2 -> x3, starting transfers between devices: 26.1 us -> 29.2 us  [exchange(): return lax.all_to_all(blocks, axes, split_axis=0, concat_axis=0, tiled=True)]
    unnamed x11 -> x13, local copies, waits for them, and re-layouts: 1.79 us -> 4.43 us
  transfers between devices with their start and end apart: 10 -> 18, of which waited for: 7 -> 9; matrix products, arithmetic and copies ran while one was open for 1% -> 1% of each run, Pallas kernels for 0% -> 1%
where the time goes in v3:
time: 150 us; the launch traced here: 148 us
  starting transfers between devices  89.7 us (60%)
  waiting for transfers between devices  41.7 us (28%)
  local copies, waits for them, and re-layouts  8.27 us (6%)
  Pallas kernels  6.4 us (4%)
    all_to_all x3, starting transfers between devices, exchange(): return lax.all_to_all(blocks, axes, split_axis=0, concat_axis=0, tiled=True)  29.2 us
    all_to_all x3, waiting for transfers between devices, exchange(): return lax.all_to_all(blocks, axes, split_axis=0, concat_axis=0, tiled=True)  21.9 us
    ppermute x4, starting transfers between devices, near(): return (lax.ppermute(value, axis, DOWN), lax.ppermute(value, axis, UP))  16.7 us
    ppermute x4, starting transfers between devices, far(): return (lax.ppermute(up, axis, UP), lax.ppermute(down, axis, DOWN))  13.4 us
    ppermute x1, starting transfers between devices, local(): partner = lax.ppermute(hidden, 'h', beside)  8.01 us
    ppermute x1, starting transfers between devices, local(): lax.ppermute(sums[half:half + n_dec // 2], ('x', 'h', 'l', 'a', 'b'), [(x...  7.62 us
    ppermute x1, waiting for transfers between devices, local(): partner = lax.ppermute(hidden, 'h', beside)  6.77 us
    ppermute x4, waiting for transfers between devices, near(): return (lax.ppermute(value, axis, DOWN), lax.ppermute(value, axis, UP))  6.67 us
  transfers between devices with their start and end apart: 18, of which 9 were waited for; matrix products, arithmetic and copies ran while one was open for 1% of the time, Pallas kernels for 1%

profile of v3, /device:TPU:6, one launch (start us, length us, event | category | flops | bytes accessed | tf_op | source)
XLA Modules:
  0.0 147.6 jit_solution(3505968481640749323)
XLA Ops:
  5.1 7.8 %collective-permute-start.1 = (bf16[896,256]{1,0:T(8,128)(2,1)S(1)}, bf16[896,256]{1,0:T(8,128)(2,1)S(1)}, u32[]{:S(2)}, u32[]{:S(2)}) collective-permute-start(bf16[896,256]{1,0:T(8,128)(2,1)S(1)} %shard_map.68.own), channel_id=1, source_target_pairs={{0,128},{128,256},{256,384},{384,0},{1,129},{129,257},{257,385},{3... | collective-permute-start | bytes 1376264 | tf_op jit(solution)/shard_map/ppermute | solution.py:28
  12.9 1.9 %collective-permute-start.2 = (bf16[896,256]{1,0:T(8,128)(2,1)S(1)}, bf16[896,256]{1,0:T(8,128)(2,1)S(1)}, u32[]{:S(2)}, u32[]{:S(2)}) collective-permute-start(bf16[896,256]{1,0:T(8,128)(2,1)S(1)} %shard_map.68.own), channel_id=1, source_target_pairs={{0,384},{128,0},{256,128},{384,256},{1,385},{129,1},{257,129},{385... | collective-permute-start | bytes 1376264 | tf_op jit(solution)/shard_map/ppermute | solution.py:28
  15.7 13.7 %all-to-all-start = ((bf16[16,160,128]{2,1,0:T(8,128)(2,1)}), bf16[16,160,128]{2,1,0:T(8,128)(2,1)S(1)}, u32[]{:S(2)}, u32[]{:S(2)}) async-start(bf16[16,160,128]{2,1,0:T(8,128)(2,1)} %broadcast_in_dim.7), calls=%async_computation | async-start | bytes 1310720 | tf_op jit(solution)/shard_map/all_to_all | solution.py:24
  29.6 3.7 %collective-permute-start.3 = (bf16[448,256]{1,0:T(8,128)(2,1)S(1)}, bf16[448,256]{1,0:T(8,128)(2,1)S(1)}, u32[]{:S(2)}, u32[]{:S(2)}) collective-permute-start(bf16[448,256]{1,0:T(8,128)(2,1)S(1)} %get-tuple-element.15), channel_id=1, source_target_pairs={{0,128},{128,256},{256,384},{384,0},{1,129},{129,257},{257,385},{3... | collective-permute-start | bytes 688136 | tf_op jit(solution)/shard_map/ppermute | solution.py:35
  33.3 2.2 %collective-permute-start.4 = (bf16[448,256]{1,0:T(8,128)(2,1)S(1)}, bf16[448,256]{1,0:T(8,128)(2,1)S(1)}, u32[]{:S(2)}, u32[]{:S(2)}) collective-permute-start(bf16[448,256]{1,0:T(8,128)(2,1)S(1)} %get-tuple-element.16), channel_id=1, source_target_pairs={{0,384},{128,0},{256,128},{384,256},{1,385},{129,1},{257,129},{385... | collective-permute-start | bytes 688136 | tf_op jit(solution)/shard_map/ppermute | solution.py:35
  35.6 5.4 %collective-permute-start.6 = (bf16[448,256]{1,0:T(8,128)(2,1)S(1)}, bf16[448,256]{1,0:T(8,128)(2,1)S(1)}, u32[]{:S(2)}, u32[]{:S(2)}) collective-permute-start(bf16[448,256]{1,0:T(8,128)(2,1)S(1)} %copy-done.3), channel_id=1, source_target_pairs={{0,64},{32,96},{64,0},{96,32},{1,65},{33,97},{65,1},{97,33},{2,66}... | collective-permute-start | bytes 688136 | tf_op jit(solution)/shard_map/ppermute | solution.py:166
  42.4 3.2 %all-to-all-done.mine = bf16[16,160,128]{2,1,0:T(8,128)(2,1)S(1)} async-done(((bf16[16,160,128]{2,1,0:T(8,128)(2,1)}), bf16[16,160,128]{2,1,0:T(8,128)(2,1)S(1)}, u32[]{:S(2)}, u32[]{:S(2)}) %all-to-all-start) | async-done | bytes 655392 | tf_op jit(solution)/shard_map/all_to_all | solution.py:24
  45.6 1.9 %collective-permute-start.5 = (bf16[16,160,128]{2,1,0:T(8,128)(2,1)S(1)}, bf16[16,160,128]{2,1,0:T(8,128)(2,1)S(1)}, u32[]{:S(2)}, u32[]{:S(2)}) collective-permute-start(bf16[16,160,128]{2,1,0:T(8,128)(2,1)S(1)} %all-to-all-done.mine), channel_id=1, source_target_pairs={{0,1},{1,0},{2,3},{3,2},{4,5},{5,4},{6,7},{7,6},{8,9},{9,8},{10,11... | collective-permute-start | bytes 1966088 | tf_op jit(solution)/shard_map/ppermute | solution.py:20
  50.9 2.8 %shard_map.71 = (bf16[4,160,896]{2,1,0:T(8,128)(2,1)}, bf16[160,896]{1,0:T(8,128)(2,1)S(1)}) custom-call(bf16[16,160,128]{2,1,0:T(8,128)(2,1)S(1)} %all-to-all-done.mine, bf16[16,160,128]{2,1,0:T(8,128)(2,1)S(1)} %collective-permute-done.5.other, bf16[896,256]{1,0:T(8,128)(2,1)S(1)} %shard_map.68.own, bf16[896,256]{1,0:T(8,128)(2,1)S(1)} %collective-permute-done.2.following, ...), custom_call_target="tpu_custom_call" | custom-call | flops 110000000 | bytes 1048576 | tf_op jit(solution)/shard_map/pallas_call | solution.py:172
  53.7 7.1 %all-to-all-start.1 = ((bf16[4,160,896]{2,1,0:T(8,128)(2,1)}), bf16[4,160,896]{2,1,0:T(8,128)(2,1)S(1)}, u32[]{:S(2)}, u32[]{:S(2)}) async-start(bf16[4,160,896]{2,1,0:T(8,128)(2,1)} %get-tuple-element.21), calls=%async_computation.1 | async-start | bytes 2293760 | tf_op jit(solution)/shard_map/all_to_all | solution.py:24
  60.8 2.5 %collective-permute-start.8 = (bf16[2,448,256]{2,1,0:T(8,128)(2,1)S(1)}, bf16[2,448,256]{2,1,0:T(8,128)(2,1)S(1)}, u32[]{:S(2)}, u32[]{:S(2)}) collective-permute-start(bf16[2,448,256]{2,1,0:T(8,128)(2,1)S(1)} %shard_map.70.own), channel_id=1, source_target_pairs={{0,384},{128,0},{256,128},{384,256},{1,385},{129,1},{257,129},{385... | collective-permute-start | bytes 1376264 | tf_op jit(solution)/shard_map/ppermute | solution.py:28
  63.2 4.6 %collective-permute-start.9 = (bf16[2,448,256]{2,1,0:T(8,128)(2,1)S(1)}, bf16[2,448,256]{2,1,0:T(8,128)(2,1)S(1)}, u32[]{:S(2)}, u32[]{:S(2)}) collective-permute-start(bf16[2,448,256]{2,1,0:T(8,128)(2,1)S(1)} %shard_map.70.own), channel_id=1, source_target_pairs={{0,128},{128,256},{256,384},{384,0},{1,129},{129,257},{257,385},{3... | collective-permute-start | bytes 1376264 | tf_op jit(solution)/shard_map/ppermute | solution.py:28
  67.8 5.4 %collective-permute-done.8.following = bf16[2,448,256]{2,1,0:T(8,128)(2,1)S(1)} collective-permute-done((bf16[2,448,256]{2,1,0:T(8,128)(2,1)S(1)}, bf16[2,448,256]{2,1,0:T(8,128)(2,1)S(1)}, u32[]{:S(2)}, u32[]{:S(2)}) %collective-permute-start.8) | collective-permute-done | bytes 458784 | tf_op jit(solution)/shard_map/ppermute | solution.py:28
  75.3 5.5 %collective-permute-start.10 = (bf16[2,224,256]{2,1,0:T(8,128)(2,1)}, bf16[2,224,256]{2,1,0:T(8,128)(2,1)S(1)}, u32[]{:S(2)}, u32[]{:S(2)}) collective-permute-start(bf16[2,224,256]{2,1,0:T(8,128)(2,1)} %get-tuple-element.24), channel_id=1, source_target_pairs={{0,128},{128,256},{256,384},{384,0},{1,129},{129,257},{257,385},{3... | collective-permute-start | bytes 688136 | tf_op jit(solution)/shard_map/ppermute | solution.py:35
  80.8 1.9 %collective-permute-start.11 = (bf16[2,224,256]{2,1,0:T(8,128)(2,1)}, bf16[2,224,256]{2,1,0:T(8,128)(2,1)}, u32[]{:S(2)}, u32[]{:S(2)}) collective-permute-start(bf16[2,224,256]{2,1,0:T(8,128)(2,1)} %get-tuple-element.25), channel_id=1, source_target_pairs={{0,384},{128,0},{256,128},{384,256},{1,385},{129,1},{257,129},{385... | collective-permute-start | bytes 688136 | tf_op jit(solution)/shard_map/ppermute | solution.py:35
  83.1 8.0 %collective-permute-start.7 = (bf16[160,448]{1,0:T(8,128)(2,1)S(1)}, bf16[160,448]{1,0:T(8,128)(2,1)S(1)}, u32[]{:S(2)}, u32[]{:S(2)}) collective-permute-start(bf16[160,448]{1,0:T(8,128)(2,1)S(1)} %shard_map.72.hidden), channel_id=1, source_target_pairs={{0,32},{32,0},{64,96},{96,64},{1,33},{33,1},{65,97},{97,65},{2,34}... | collective-permute-start | bytes 430088 | tf_op jit(solution)/shard_map/ppermute | solution.py:183
  91.1 6.8 %collective-permute-done.7.partner = bf16[160,448]{1,0:T(8,128)(2,1)S(1)} collective-permute-done((bf16[160,448]{1,0:T(8,128)(2,1)S(1)}, bf16[160,448]{1,0:T(8,128)(2,1)S(1)}, u32[]{:S(2)}, u32[]{:S(2)}) %collective-permute-start.7) | collective-permute-done | bytes 143392 | tf_op jit(solution)/shard_map/ppermute | solution.py:183
  97.9 1.8 %shard_map.74 = (f32[16,80,256]{2,1,0:T(8,128)S(1)}, bf16[16,80,256]{2,1,0:T(8,128)(2,1)S(1)}) custom-call(bf16[160,448]{1,0:T(8,128)(2,1)S(1)} %shard_map.72.hidden, bf16[160,448]{1,0:T(8,128)(2,1)S(1)} %collective-permute-done.7.partner, bf16[2,448,256]{2,1,0:T(8,128)(2,1)S(1)} %shard_map.70.own, ...), custom_call_target="tpu_custom_call" | custom-call | flops 2200000000 | bytes 1048576 | tf_op jit(solution)/shard_map/pallas_call | solution.py:186
  99.7 1.9 %collective-permute-start.12 = (bf16[16,80,256]{2,1,0:T(8,128)(2,1)S(1)}, bf16[16,80,256]{2,1,0:T(8,128)(2,1)S(1)}, u32[]{:S(2)}, u32[]{:S(2)}) collective-permute-start(bf16[16,80,256]{2,1,0:T(8,128)(2,1)S(1)} %get-tuple-element.27), channel_id=1, source_target_pairs={{0,1},{1,0},{2,3},{3,2},{4,5},{5,4},{6,7},{7,6},{8,9},{9,8},{10,11... | collective-permute-start | bytes 1966088 | tf_op jit(solution)/shard_map/ppermute | solution.py:20
  101.6 2.1 %collective-permute-done.12 = bf16[16,80,256]{2,1,0:T(8,128)(2,1)S(1)} collective-permute-done((bf16[16,80,256]{2,1,0:T(8,128)(2,1)S(1)}, bf16[16,80,256]{2,1,0:T(8,128)(2,1)S(1)}, u32[]{:S(2)}, u32[]{:S(2)}) %collective-permute-start.12) | collective-permute-done | bytes 655392 | tf_op jit(solution)/shard_map/ppermute | solution.py:20
  105.3 8.4 %all-to-all-start.2 = ((bf16[16,80,256]{2,1,0:T(8,128)(2,1)}), bf16[16,80,256]{2,1,0:T(8,128)(2,1)S(1)}, u32[]{:S(2)}, u32[]{:S(2)}) async-start(bf16[16,80,256]{2,1,0:T(8,128)(2,1)} %copy.17), calls=%async_computation.2 | async-start | bytes 1310720 | tf_op jit(solution)/shard_map/all_to_all | solution.py:24
  113.8 18.7 %all-to-all-done.2 = bf16[16,80,256]{2,1,0:T(8,128)(2,1)S(1)} async-done(((bf16[16,80,256]{2,1,0:T(8,128)(2,1)}), bf16[16,80,256]{2,1,0:T(8,128)(2,1)S(1)}, u32[]{:S(2)}, u32[]{:S(2)}) %all-to-all-start.2) | async-done | bytes 655392 | tf_op jit(solution)/shard_map/all_to_all | solution.py:24
  132.7 7.6 %collective-permute-start.14 = (bf16[12,256]{1,0:T(8,128)(2,1)S(1)}, bf16[12,256]{1,0:T(8,128)(2,1)S(1)}, u32[]{:S(2)}, u32[]{:S(2)}) collective-permute-start(bf16[12,256]{1,0:T(8,128)(2,1)S(1)} %slice.29), channel_id=1, source_target_pairs={{0,0},{2,2},{4,64},{6,66},{8,128},{10,130},{12,192},{14,194},{16,2... | collective-permute-start | bytes 18440 | tf_op jit(solution)/shard_map/ppermute | solution.py:200
  140.3 4.8 %collective-permute-start.13 = (bf16[4,2,4,256]{3,2,1,0:T(4,128)(2,1)S(1)}, bf16[4,2,4,256]{3,2,1,0:T(4,128)(2,1)S(1)}, u32[]{:S(2)}, u32[]{:S(2)}) collective-permute-start(bf16[4,2,4,256]{3,2,1,0:T(4,128)(2,1)S(1)} %get-tuple-element.29), channel_id=1, source_target_pairs={{0,32},{32,0},{64,96},{96,64},{1,33},{33,1},{65,97},{97,65},{2,34}... | collective-permute-start | bytes 49160 | tf_op jit(solution)/shard_map/ppermute | solution.py:219
  (57 shorter events, 16.8 us)
Async XLA Ops:
  0.6 0.9 copy-start
  2.5 12.3 %collective-permute-start = (bf16[160,128]{1,0:T(8,128)(2,1)S(1)}, bf16[160,128]{1,0:T(8,128)(2,1)S(1)}, u32[]{:S(2)}, u32[]{:S(2)}) collective-permute-start(bf16[160,128]{1,0:T(8,128)(2,1)S(1)} %bitcast.24), channel_id=1, source_target_pairs={{0,0},{2,32},{4,64},{6,96},{32,2},{34,34},{36,66},{38,98},{64,4},{... | collective-permute-start | bytes 122888 | tf_op jit(solution)/shard_map/ppermute | solution.py:157
  3.2 0.9 copy-start.1
  4.1 0.9 copy-start.2
  5.1 24.4 %collective-permute-start.1 = (bf16[896,256]{1,0:T(8,128)(2,1)S(1)}, bf16[896,256]{1,0:T(8,128)(2,1)S(1)}, u32[]{:S(2)}, u32[]{:S(2)}) collective-permute-start(bf16[896,256]{1,0:T(8,128)(2,1)S(1)} %shard_map.68.own), channel_id=1, source_target_pairs={{0,128},{128,256},{256,384},{384,0},{1,129},{129,257},{257,385},{3... | collective-permute-start | bytes 1376264 | tf_op jit(solution)/shard_map/ppermute | solution.py:28
  12.9 16.6 %collective-permute-start.2 = (bf16[896,256]{1,0:T(8,128)(2,1)S(1)}, bf16[896,256]{1,0:T(8,128)(2,1)S(1)}, u32[]{:S(2)}, u32[]{:S(2)}) collective-permute-start(bf16[896,256]{1,0:T(8,128)(2,1)S(1)} %shard_map.68.own), channel_id=1, source_target_pairs={{0,384},{128,0},{256,128},{384,256},{1,385},{129,1},{257,129},{385... | collective-permute-start | bytes 1376264 | tf_op jit(solution)/shard_map/ppermute | solution.py:28
  15.7 29.9 %all-to-all-start = ((bf16[16,160,128]{2,1,0:T(8,128)(2,1)}), bf16[16,160,128]{2,1,0:T(8,128)(2,1)S(1)}, u32[]{:S(2)}, u32[]{:S(2)}) async-start(bf16[16,160,128]{2,1,0:T(8,128)(2,1)} %broadcast_in_dim.7), calls=%async_computation | async-start | bytes 1310720 | tf_op jit(solution)/shard_map/all_to_all | solution.py:24
  29.5 6.1 %copy-start.3 = (bf16[448,256]{1,0:T(8,128)(2,1)S(1)}, bf16[448,256]{1,0:T(8,128)(2,1)}, u32[]{:S(2)}) copy-start(bf16[448,256]{1,0:T(8,128)(2,1)} %own.1) | copy-start | bytes 688132
  29.6 11.4 %collective-permute-start.3 = (bf16[448,256]{1,0:T(8,128)(2,1)S(1)}, bf16[448,256]{1,0:T(8,128)(2,1)S(1)}, u32[]{:S(2)}, u32[]{:S(2)}) collective-permute-start(bf16[448,256]{1,0:T(8,128)(2,1)S(1)} %get-tuple-element.15), channel_id=1, source_target_pairs={{0,128},{128,256},{256,384},{384,0},{1,129},{129,257},{257,385},{3... | collective-permute-start | bytes 688136 | tf_op jit(solution)/shard_map/ppermute | solution.py:35
  33.3 9.1 %collective-permute-start.4 = (bf16[448,256]{1,0:T(8,128)(2,1)S(1)}, bf16[448,256]{1,0:T(8,128)(2,1)S(1)}, u32[]{:S(2)}, u32[]{:S(2)}) collective-permute-start(bf16[448,256]{1,0:T(8,128)(2,1)S(1)} %get-tuple-element.16), channel_id=1, source_target_pairs={{0,384},{128,0},{256,128},{384,256},{1,385},{129,1},{257,129},{385... | collective-permute-start | bytes 688136 | tf_op jit(solution)/shard_map/ppermute | solution.py:35
  35.6 13.7 %collective-permute-start.6 = (bf16[448,256]{1,0:T(8,128)(2,1)S(1)}, bf16[448,256]{1,0:T(8,128)(2,1)S(1)}, u32[]{:S(2)}, u32[]{:S(2)}) collective-permute-start(bf16[448,256]{1,0:T(8,128)(2,1)S(1)} %copy-done.3), channel_id=1, source_target_pairs={{0,64},{32,96},{64,0},{96,32},{1,65},{33,97},{65,1},{97,33},{2,66}... | collective-permute-start | bytes 688136 | tf_op jit(solution)/shard_map/ppermute | solution.py:166
  45.6 5.2 %collective-permute-start.5 = (bf16[16,160,128]{2,1,0:T(8,128)(2,1)S(1)}, bf16[16,160,128]{2,1,0:T(8,128)(2,1)S(1)}, u32[]{:S(2)}, u32[]{:S(2)}) collective-permute-start(bf16[16,160,128]{2,1,0:T(8,128)(2,1)S(1)} %all-to-all-done.mine), channel_id=1, source_target_pairs={{0,1},{1,0},{2,3},{3,2},{4,5},{5,4},{6,7},{7,6},{8,9},{9,8},{10,11... | collective-permute-start | bytes 1966088 | tf_op jit(solution)/shard_map/ppermute | solution.py:20
  49.2 0.7 copy-start.4
  49.9 0.9 copy-start.5
  53.7 29.1 %all-to-all-start.1 = ((bf16[4,160,896]{2,1,0:T(8,128)(2,1)}), bf16[4,160,896]{2,1,0:T(8,128)(2,1)S(1)}, u32[]{:S(2)}, u32[]{:S(2)}) async-start(bf16[4,160,896]{2,1,0:T(8,128)(2,1)} %get-tuple-element.21), calls=%async_computation.1 | async-start | bytes 2293760 | tf_op jit(solution)/shard_map/all_to_all | solution.py:24
  60.8 12.5 %collective-permute-start.8 = (bf16[2,448,256]{2,1,0:T(8,128)(2,1)S(1)}, bf16[2,448,256]{2,1,0:T(8,128)(2,1)S(1)}, u32[]{:S(2)}, u32[]{:S(2)}) collective-permute-start(bf16[2,448,256]{2,1,0:T(8,128)(2,1)S(1)} %shard_map.70.own), channel_id=1, source_target_pairs={{0,384},{128,0},{256,128},{384,256},{1,385},{129,1},{257,129},{385... | collective-permute-start | bytes 1376264 | tf_op jit(solution)/shard_map/ppermute | solution.py:28
  63.2 11.2 %collective-permute-start.9 = (bf16[2,448,256]{2,1,0:T(8,128)(2,1)S(1)}, bf16[2,448,256]{2,1,0:T(8,128)(2,1)S(1)}, u32[]{:S(2)}, u32[]{:S(2)}) collective-permute-start(bf16[2,448,256]{2,1,0:T(8,128)(2,1)S(1)} %shard_map.70.own), channel_id=1, source_target_pairs={{0,128},{128,256},{256,384},{384,0},{1,129},{129,257},{257,385},{3... | collective-permute-start | bytes 1376264 | tf_op jit(solution)/shard_map/ppermute | solution.py:28
  75.3 15.8 %collective-permute-start.10 = (bf16[2,224,256]{2,1,0:T(8,128)(2,1)}, bf16[2,224,256]{2,1,0:T(8,128)(2,1)S(1)}, u32[]{:S(2)}, u32[]{:S(2)}) collective-permute-start(bf16[2,224,256]{2,1,0:T(8,128)(2,1)} %get-tuple-element.24), channel_id=1, source_target_pairs={{0,128},{128,256},{256,384},{384,0},{1,129},{129,257},{257,385},{3... | collective-permute-start | bytes 688136 | tf_op jit(solution)/shard_map/ppermute | solution.py:35
  80.8 10.3 %collective-permute-start.11 = (bf16[2,224,256]{2,1,0:T(8,128)(2,1)}, bf16[2,224,256]{2,1,0:T(8,128)(2,1)}, u32[]{:S(2)}, u32[]{:S(2)}) collective-permute-start(bf16[2,224,256]{2,1,0:T(8,128)(2,1)} %get-tuple-element.25), channel_id=1, source_target_pairs={{0,384},{128,0},{256,128},{384,256},{1,385},{129,1},{257,129},{385... | collective-permute-start | bytes 688136 | tf_op jit(solution)/shard_map/ppermute | solution.py:35
  83.1 14.8 %collective-permute-start.7 = (bf16[160,448]{1,0:T(8,128)(2,1)S(1)}, bf16[160,448]{1,0:T(8,128)(2,1)S(1)}, u32[]{:S(2)}, u32[]{:S(2)}) collective-permute-start(bf16[160,448]{1,0:T(8,128)(2,1)S(1)} %shard_map.72.hidden), channel_id=1, source_target_pairs={{0,32},{32,0},{64,96},{96,64},{1,33},{33,1},{65,97},{97,65},{2,34}... | collective-permute-start | bytes 430088 | tf_op jit(solution)/shard_map/ppermute | solution.py:183
  99.7 4.0 %collective-permute-start.12 = (bf16[16,80,256]{2,1,0:T(8,128)(2,1)S(1)}, bf16[16,80,256]{2,1,0:T(8,128)(2,1)S(1)}, u32[]{:S(2)}, u32[]{:S(2)}) collective-permute-start(bf16[16,80,256]{2,1,0:T(8,128)(2,1)S(1)} %get-tuple-element.27), channel_id=1, source_target_pairs={{0,1},{1,0},{2,3},{3,2},{4,5},{5,4},{6,7},{7,6},{8,9},{9,8},{10,11... | collective-permute-start | bytes 1966088 | tf_op jit(solution)/shard_map/ppermute | solution.py:20
  105.3 27.2 %all-to-all-start.2 = ((bf16[16,80,256]{2,1,0:T(8,128)(2,1)}), bf16[16,80,256]{2,1,0:T(8,128)(2,1)S(1)}, u32[]{:S(2)}, u32[]{:S(2)}) async-start(bf16[16,80,256]{2,1,0:T(8,128)(2,1)} %copy.17), calls=%async_computation.2 | async-start | bytes 1310720 | tf_op jit(solution)/shard_map/all_to_all | solution.py:24
  132.7 12.5 %collective-permute-start.14 = (bf16[12,256]{1,0:T(8,128)(2,1)S(1)}, bf16[12,256]{1,0:T(8,128)(2,1)S(1)}, u32[]{:S(2)}, u32[]{:S(2)}) collective-permute-start(bf16[12,256]{1,0:T(8,128)(2,1)S(1)} %slice.29), channel_id=1, source_target_pairs={{0,0},{2,2},{4,64},{6,66},{8,128},{10,130},{12,192},{14,194},{16,2... | collective-permute-start | bytes 18440 | tf_op jit(solution)/shard_map/ppermute | solution.py:200
  140.3 6.6 %collective-permute-start.13 = (bf16[4,2,4,256]{3,2,1,0:T(4,128)(2,1)S(1)}, bf16[4,2,4,256]{3,2,1,0:T(4,128)(2,1)S(1)}, u32[]{:S(2)}, u32[]{:S(2)}) collective-permute-start(bf16[4,2,4,256]{3,2,1,0:T(4,128)(2,1)S(1)} %get-tuple-element.29), channel_id=1, source_target_pairs={{0,32},{32,0},{64,96},{96,64},{1,33},{33,1},{65,97},{97,65},{2,34}... | collective-permute-start | bytes 49160 | tf_op jit(solution)/shard_map/ppermute | solution.py:219

commit v4 on v3

--- a/solution.py
+++ b/solution.py
@@ -13,7 +13,7 @@
 UP = [(i, (i + 1) % 4) for i in range(4)]
 DOWN = [(i, (i + 3) % 4) for i in range(4)]
 VMEM = 16 * 2**20
-HINTS = (5.5, 0.1, 1, 8, 5)
+HINTS = (5.5, 0.1, 1, 0.1, 5, 8, 5)
 
 
 def swap_cores(value):
@@ -70,24 +70,32 @@
     out[1] = opposite[...]
 
 
-def gate_up_kernel(mine, other, own, following, first, second, previous, partial, residue):
-    x, h, core = lax.axis_index("x"), lax.axis_index("h"), lax.axis_index("c")
+def half_product(feats, weights, which):
+    x = lax.axis_index("x")
+    own, following, first, second, previous = weights
+    block = feats.shape[2]
+    part = pl.ds(pl.multiple_of(which * block, block), block)
+    opposite = jnp.concatenate([first[:, part], second[:, part]], axis=0)
+    total = None
+    for slot, weight in enumerate((own[:, part], following[:, part], opposite, previous[:, part])):
+        lhs = jnp.concatenate([feats[lax.rem(x + slot, 4) * 4 + b] for b in range(4)], axis=0)
+        term = lax.dot_general(lhs, weight, (((1,), (1,)), ((), ())), preferred_element_type=F32)
+        total = term if total is None else total + term
+    return total
+
+
+def gate_up_start_kernel(feats, own, following, first, second, previous, out):
+    out[...] = half_product(feats, (own, following, first, second, previous), lax.axis_index("c"))
+
+
+def gate_up_kernel(feats, started, own, following, first, second, previous, partial, residue):
+    h = lax.axis_index("h")
     blocks, rows, _ = partial.shape
-    opposite = jnp.concatenate([first[...], second[...]], axis=0)
-    total = None
-    for slot, weight in enumerate((own[...], following[...], opposite, previous[...])):
-        lhs = []
-        for b in range(blocks):
-            at = lax.rem(x + slot, 4) * 4 + b
-            left = jnp.where(core == 0, mine[at], other[at])
-            right = jnp.where(core == 0, other[at], mine[at])
-            lhs.append(jnp.concatenate([left, right], axis=1))
-        term = lax.dot_general(
-            jnp.concatenate(lhs, axis=0), weight, (((1,), (1,)), ((), ())), preferred_element_type=F32
-        )
-        total = term if total is None else total + term
+    stride = feats.shape[1]
+    weights = (own, following, first, second, previous)
+    total = started[...] + half_product(feats, weights, 1 - lax.axis_index("c"))
     for b in range(blocks):
-        part = total[b * rows : (b + 1) * rows]
+        part = total[b * stride : b * stride + rows]
         rounded = part.astype(BF16)
         partial[b] = rounded
 
@@ -108,12 +116,15 @@
     out[:, even:] = (gate / (1.0 + jnp.exp(-gate)) * up).astype(BF16)
 
 
-def down_kernel(hidden, partner, own, following, first, second, previous, kept, given):
+def down_products(half, hidden, own, following, first, second, previous, store):
     x, core = lax.axis_index("x"), lax.axis_index("c")
-    half = hidden.shape[0] // 2
-    mine = pl.ds(pl.multiple_of(core * half, 16), half)
-    other = pl.ds(pl.multiple_of((1 - core) * half, 16), half)
-    lhs = jnp.concatenate([ref[part] for part in (mine, other) for ref in (hidden, partner)], axis=0)
+    mine = hidden[pl.ds(pl.multiple_of(core * half, 16), half)]
+    other = hidden[pl.ds(pl.multiple_of((1 - core) * half, 16), half)]
+    decode = hidden[2 * half :].astype(F32)
+    low, high = decode[:16].astype(BF16), decode[8:].astype(BF16)
+    lhs = jnp.concatenate(
+        [mine, jnp.where(core == 0, low, high), other, jnp.where(core == 0, high, low)], axis=0
+    )
     for slot in range(4):
         for k in range(2):
             if slot == 2:
@@ -121,17 +132,46 @@
             else:
                 weight = (own, following, None, previous)[slot][k]
             terms = dot(lhs, weight)
-            at = lax.rem(x + slot, 4) * 4 + k * 2
-            for r in range(2):
-                kept[at + r] = terms[r * half : (r + 1) * half]
-                given[at + r] = terms[(2 + r) * half : (3 + r) * half].astype(BF16)
+            store(lax.rem(x + slot, 4) * 2 + k, terms[: half + 16], terms[half + 16 :].astype(BF16))
+
+
+def down_start_kernel(hidden, own, following, first, second, previous, kept, given):
+    def store(at, mine, other):
+        kept[at] = mine
+        given[at] = other
+
+    down_products(kept.shape[1] - 16, hidden, own, following, first, second, previous, store)
+
+
+def down_kernel(hidden, own, following, first, second, previous, kept0, given0, kept, given):
+    def store(at, mine, other):
+        kept[at, 1] = mine
+        given[at, 1] = other
+
+    down_products(kept.shape[2] - 16, hidden, own, following, first, second, previous, store)
+    kept[:, 0] = kept0[...]
+    given[:, 0] = given0[...]
+
+
+def prefill_kernel(mine, theirs, out):
+    h = lax.axis_index("h")
+    width = mine.shape[3]
+    for q in range(mine.shape[0]):
+        for k in range(mine.shape[1]):
+            column = lax.bitwise_xor(h, 2 * k)
+            for ref, at in ((mine, column), (theirs, lax.bitwise_xor(column, 1))):
+                out[:, pl.ds(pl.multiple_of((q * 4 + at) * width, width), width)] = ref[q, k]
 
 
 def decode_kernel(rows, out):
-    steps = out.shape[1]
+    core = lax.axis_index("c")
+    count, steps, _ = out.shape
     wide = rows[...].astype(F32)
-    for i in range(out.shape[0]):
-        out[i] = wide[i * steps : (i + 1) * steps].astype(BF16)
+    skip = wide.shape[0] - count * steps
+    for i in range(count):
+        at = i * steps
+        low, high = wide[at : at + steps], wide[skip + at : skip + at + steps]
+        out[i] = jnp.where(core == 0, low, high).astype(BF16)
 
 
 def local(tokens, gate_weight, up_weight, down_weight, decode_in):
@@ -142,18 +182,17 @@
     n_dec = steps * rows
     width = down_weight.shape[1]
     each = -(-(n_rows + n_dec) // 32) * 16
-    total = 2 * each
-    fill = each - (n_rows + n_dec) // 2
+    used, total = n_rows + n_dec, 2 * each
 
     decode_part = lax.dynamic_slice_in_dim(decode_in, yz * block, block, 2)
     feats = jnp.concatenate(
         [
-            tokens.reshape(16, 2, 4, block).transpose(1, 0, 2, 3).reshape(2, n_rows // 2, block),
-            decode_part.transpose(1, 0, 2).reshape(2, n_dec // 2, block),
-            jnp.zeros((2, fill, block), BF16),
+            tokens.reshape(16, 2, 4, block).transpose(1, 0, 2, 3).reshape(n_rows, block),
+            decode_part.transpose(1, 0, 2).reshape(n_dec, block),
+            jnp.zeros((total - used, block), BF16),
         ],
-        axis=1,
-    ).reshape(total, block)
+        axis=0,
+    )
     feats = lax.ppermute(
         feats, ("h", "b"), [(h * 4 + b, b * 4 + h) for h in range(4) for b in range(4)]
     )
@@ -166,39 +205,47 @@
     opposite = lax.ppermute(down_weight, "h", [(i, (i + 2) % 4) for i in range(4)])
     feats, own_far = lax.optimization_barrier((feats, own_far))
     other = swap_cores(feats)
-    down = call(pair_kernel, jax.ShapeDtypeStruct((2, ff, width), BF16), HINTS[3])(down_weight, opposite)
-    other, down = lax.optimization_barrier((other, down))
-
+
+    weights = (own, own_near[0], *own_far, own_near[1])
+    started = call(gate_up_start_kernel, jax.ShapeDtypeStruct((4 * total, 2 * ff), F32), HINTS[5])(feats, *weights)
+    other, opposite = lax.optimization_barrier((other, opposite))
     partial, residue = call(
         gate_up_kernel,
         (
-            jax.ShapeDtypeStruct((4, total, 2 * ff), BF16),
-            jax.ShapeDtypeStruct((total, 2 * ff), BF16),
+            jax.ShapeDtypeStruct((4, used, 2 * ff), BF16),
+            jax.ShapeDtypeStruct((used, 2 * ff), BF16),
         ),
         HINTS[1],
-    )(feats, other, own, own_near[0], *own_far, own_near[1])
+    )(other, started, *weights)
     parts = exchange(partial, "h")
-    hidden = call(hidden_kernel, jax.ShapeDtypeStruct((total, ff), BF16), 1)(parts, residue)
+    hidden = call(hidden_kernel, jax.ShapeDtypeStruct((used, ff), BF16), 1)(parts, residue)
     beside = [(0, 1), (1, 0), (2, 3), (3, 2)]
     partner = lax.ppermute(hidden, "h", beside)
+    down = call(pair_kernel, jax.ShapeDtypeStruct((2, ff, width), BF16), HINTS[3])(down_weight, opposite)
     down_near = near(down, "x")
     down_far = far(*down_near, "x", HINTS[2])
+    weights = (down, down_near[0], *down_far, down_near[1])
+    shape = (8, each, width)
+    started = call(
+        down_start_kernel,
+        (jax.ShapeDtypeStruct(shape, F32), jax.ShapeDtypeStruct(shape, BF16)),
+        HINTS[6],
+    )(hidden, *weights)
+    started, partner = lax.optimization_barrier((started, partner))
+    shape = (8, 2, each, width)
     kept, given = call(
         down_kernel,
-        (
-            jax.ShapeDtypeStruct((16, each, width), F32),
-            jax.ShapeDtypeStruct((16, each, width), BF16),
-        ),
-        2,
-    )(hidden, partner, down, down_near[0], *down_far, down_near[1])
-    sums = (kept + swap_cores(given).astype(F32)).astype(BF16)
+        (jax.ShapeDtypeStruct(shape, F32), jax.ShapeDtypeStruct(shape, BF16)),
+        0.1,
+    )(partner, *weights, *started)
+    sums = (kept + swap_cores(given).astype(F32)).astype(BF16).reshape(16, each, width)
 
     half = n_rows // 2
     prefill = sums[:, :half].reshape(16, 16, 4, width).transpose(1, 0, 2, 3).reshape(16, half, width)
     sums = exchange(jnp.concatenate([prefill, sums[:, half:]], axis=1), LZ)
     sums = sums.astype(F32).sum(0).astype(BF16)
     decode_out = lax.ppermute(
-        sums[half : half + n_dec // 2],
+        sums[half:],
         ("x", "h", "l", "a", "b"),
         [
             (
@@ -214,13 +261,9 @@
     )
     decode_out = call(decode_kernel, jax.ShapeDtypeStruct((rows // 2, steps, width), BF16), HINTS[4])(decode_out)
     decode_out = decode_out.transpose(1, 0, 2)
-    h = lax.axis_index("h")
     mine = sums[:half].reshape(4, 2, 2, 4, width)
     theirs = lax.ppermute(mine[:, :, 1], "h", beside)
-    both = jnp.stack([mine[:, :, 0], theirs], axis=2)
-    both = jnp.where(h % 2 == 1, both[:, :, ::-1], both)
-    both = jnp.where(h // 2 == 1, both[:, ::-1], both)
-    prefill_out = both.transpose(3, 0, 1, 2, 4).reshape(4, 16 * width)
+    prefill_out = call(prefill_kernel, jax.ShapeDtypeStruct((4, 16 * width), BF16), 0.1)(mine[:, :, 0], theirs)
     return prefill_out, decode_out
 
 

time: 150 us -> 145 us (0.967)
  the two profiles are of different devices: /device:TPU:6 before, /device:TPU:56 now
where the time goes in v4:
time: 145 us; the launch traced here: 144 us
  starting transfers between devices  70.7 us (49%)
  waiting for transfers between devices  31.5 us (22%)
  blocking collectives  28.3 us (20%)
  Pallas kernels  7.42 us (5%)
  local copies, waits for them, and re-layouts  4.75 us (3%)
    all_to_all x1, blocking collectives, exchange(): return lax.all_to_all(blocks, axes, split_axis=0, concat_axis=0, tiled=True)  28.3 us
    all_to_all x2, starting transfers between devices, exchange(): return lax.all_to_all(blocks, axes, split_axis=0, concat_axis=0, tiled=True)  17.4 us
    ppermute x4, starting transfers between devices, far(): return (lax.ppermute(up, axis, UP), lax.ppermute(down, axis, DOWN))  14.2 us
    ppermute x4, starting transfers between devices, near(): return (lax.ppermute(value, axis, DOWN), lax.ppermute(value, axis, UP))  12.9 us
    ppermute x4, waiting for transfers between devices, near(): return (lax.ppermute(value, axis, DOWN), lax.ppermute(value, axis, UP))  10.2 us
    ppermute x1, starting transfers between devices, local(): lax.ppermute(feats, ('h', 'b'), [(h * 4 + b, b * 4 + h) for h in range(4)...  8.11 us
    ppermute x1, waiting for transfers between devices, local(): lax.ppermute(sums[half:], ('x', 'h', 'l', 'a', 'b'), [(x * 64 + h * 16 +...  6.87 us
    all_to_all x2, waiting for transfers between devices, exchange(): return lax.all_to_all(blocks, axes, split_axis=0, concat_axis=0, tiled=True)  6.15 us
  transfers between devices with their start and end apart: 17, of which 8 were waited for; matrix products, arithmetic and copies ran while one was open for 1% of the time, Pallas kernels for 3%

profile of v4, /device:TPU:56, one launch (start us, length us, event | category | flops | bytes accessed | tf_op | source)
XLA Modules:
  0.0 144.2 jit_solution(11518680750786973594)
XLA Ops:
  1.8 8.1 %collective-permute-start = (bf16[160,128]{1,0:T(8,128)(2,1)S(1)}, bf16[160,128]{1,0:T(8,128)(2,1)S(1)}, u32[]{:S(2)}, u32[]{:S(2)}) collective-permute-start(bf16[160,128]{1,0:T(8,128)(2,1)S(1)} %maximum_maximum_fusion), channel_id=1, source_target_pairs={{0,0},{2,32},{4,64},{6,96},{32,2},{34,34},{36,66},{38,98},{64,4},{... | collective-permute-start | bytes 122888 | tf_op jit(solution)/shard_map/ppermute | solution.py:196
  11.8 3.4 %collective-permute-start.1 = (bf16[896,256]{1,0:T(8,128)(2,1)S(1)}, bf16[896,256]{1,0:T(8,128)(2,1)S(1)}, u32[]{:S(2)}, u32[]{:S(2)}) collective-permute-start(bf16[896,256]{1,0:T(8,128)(2,1)S(1)} %shard_map.68.own), channel_id=1, source_target_pairs={{0,128},{128,256},{256,384},{384,0},{1,129},{129,257},{257,385},{3... | collective-permute-start | bytes 1376264 | tf_op jit(solution)/shard_map/ppermute | solution.py:28
  15.2 3.7 %collective-permute-start.2 = (bf16[896,256]{1,0:T(8,128)(2,1)S(1)}, bf16[896,256]{1,0:T(8,128)(2,1)S(1)}, u32[]{:S(2)}, u32[]{:S(2)}) collective-permute-start(bf16[896,256]{1,0:T(8,128)(2,1)S(1)} %shard_map.68.own), channel_id=1, source_target_pairs={{0,384},{128,0},{256,128},{384,256},{1,385},{129,1},{257,129},{385... | collective-permute-start | bytes 1376264 | tf_op jit(solution)/shard_map/ppermute | solution.py:28
  19.8 10.2 %all-to-all-start = ((bf16[16,160,128]{2,1,0:T(8,128)(2,1)}), bf16[16,160,128]{2,1,0:T(8,128)(2,1)S(1)}, u32[]{:S(2)}, u32[]{:S(2)}) async-start(bf16[16,160,128]{2,1,0:T(8,128)(2,1)} %broadcast_in_dim.7), calls=%async_computation | async-start | bytes 1310720 | tf_op jit(solution)/shard_map/all_to_all | solution.py:24
  30.1 2.3 %collective-permute-start.3 = (bf16[448,256]{1,0:T(8,128)(2,1)S(1)}, bf16[448,256]{1,0:T(8,128)(2,1)S(1)}, u32[]{:S(2)}, u32[]{:S(2)}) collective-permute-start(bf16[448,256]{1,0:T(8,128)(2,1)S(1)} %get-tuple-element.20), channel_id=1, source_target_pairs={{0,128},{128,256},{256,384},{384,0},{1,129},{129,257},{257,385},{3... | collective-permute-start | bytes 688136 | tf_op jit(solution)/shard_map/ppermute | solution.py:35
  32.4 4.9 %collective-permute-start.4 = (bf16[448,256]{1,0:T(8,128)(2,1)S(1)}, bf16[448,256]{1,0:T(8,128)(2,1)S(1)}, u32[]{:S(2)}, u32[]{:S(2)}) collective-permute-start(bf16[448,256]{1,0:T(8,128)(2,1)S(1)} %get-tuple-element.21), channel_id=1, source_target_pairs={{0,384},{128,0},{256,128},{384,256},{1,385},{129,1},{257,129},{385... | collective-permute-start | bytes 688136 | tf_op jit(solution)/shard_map/ppermute | solution.py:35
  37.3 3.2 %collective-permute-start.6 = (bf16[448,256]{1,0:T(8,128)(2,1)S(1)}, bf16[448,256]{1,0:T(8,128)(2,1)S(1)}, u32[]{:S(2)}, u32[]{:S(2)}) collective-permute-start(bf16[448,256]{1,0:T(8,128)(2,1)S(1)} %copy-done.1), channel_id=1, source_target_pairs={{0,64},{32,96},{64,0},{96,32},{1,65},{33,97},{65,1},{97,33},{2,66}... | collective-permute-start | bytes 688136 | tf_op jit(solution)/shard_map/ppermute | solution.py:205
  40.8 6.1 %all-to-all-done.feats = bf16[16,160,128]{2,1,0:T(8,128)(2,1)S(1)} async-done(((bf16[16,160,128]{2,1,0:T(8,128)(2,1)}), bf16[16,160,128]{2,1,0:T(8,128)(2,1)S(1)}, u32[]{:S(2)}, u32[]{:S(2)}) %all-to-all-start) | async-done | bytes 655392 | tf_op jit(solution)/shard_map/all_to_all | solution.py:24
  46.9 1.9 %collective-permute-start.5 = (bf16[16,160,128]{2,1,0:T(8,128)(2,1)S(1)}, bf16[16,160,128]{2,1,0:T(8,128)(2,1)S(1)}, u32[]{:S(2)}, u32[]{:S(2)}) collective-permute-start(bf16[16,160,128]{2,1,0:T(8,128)(2,1)S(1)} %all-to-all-done.feats), channel_id=1, source_target_pairs={{0,1},{1,0},{2,3},{3,2},{4,5},{5,4},{6,7},{7,6},{8,9},{9,8},{10,11... | collective-permute-start | bytes 1966088 | tf_op jit(solution)/shard_map/ppermute | solution.py:20
  51.3 2.6 %shard_map.71 = (bf16[4,152,896]{2,1,0:T(8,128)(2,1)}, bf16[152,896]{1,0:T(8,128)(2,1)S(1)}) custom-call(bf16[16,160,128]{2,1,0:T(8,128)(2,1)S(1)} %collective-permute-done.5.feats, f32[640,896]{1,0:T(8,128)S(1)} %shard_map.70.started, bf16[896,256]{1,0:T(8,128)(2,1)S(1)} %shard_map.68.own, bf16[896,256]{1,0:T(8,128)(2,1)S(1)} %collective-permute-done.2.following, ...), custom_call_target="tpu_custom_call" | custom-call | flops 110000000 | bytes 1048576 | tf_op jit(solution)/shard_map/pallas_call | solution.py:212
  53.9 7.2 %all-to-all-start.1 = ((bf16[4,152,896]{2,1,0:T(8,128)(2,1)}), bf16[4,152,896]{2,1,0:T(8,128)(2,1)S(1)}, u32[]{:S(2)}, u32[]{:S(2)}) async-start(bf16[4,152,896]{2,1,0:T(8,128)(2,1)} %get-tuple-element.26), calls=%async_computation.1 | async-start | bytes 2179072 | tf_op jit(solution)/shard_map/all_to_all | solution.py:24
  61.2 2.4 %collective-permute-start.7 = (bf16[2,448,256]{2,1,0:T(8,128)(2,1)S(1)}, bf16[2,448,256]{2,1,0:T(8,128)(2,1)S(1)}, u32[]{:S(2)}, u32[]{:S(2)}) collective-permute-start(bf16[2,448,256]{2,1,0:T(8,128)(2,1)S(1)} %shard_map.73.own), channel_id=1, source_target_pairs={{0,384},{128,0},{256,128},{384,256},{1,385},{129,1},{257,129},{385... | collective-permute-start | bytes 1376264 | tf_op jit(solution)/shard_map/ppermute | solution.py:28
  63.6 3.4 %collective-permute-start.8 = (bf16[2,448,256]{2,1,0:T(8,128)(2,1)S(1)}, bf16[2,448,256]{2,1,0:T(8,128)(2,1)S(1)}, u32[]{:S(2)}, u32[]{:S(2)}) collective-permute-start(bf16[2,448,256]{2,1,0:T(8,128)(2,1)S(1)} %shard_map.73.own), channel_id=1, source_target_pairs={{0,128},{128,256},{256,384},{384,0},{1,129},{129,257},{257,385},{3... | collective-permute-start | bytes 1376264 | tf_op jit(solution)/shard_map/ppermute | solution.py:28
  67.1 6.3 %collective-permute-done.7.following = bf16[2,448,256]{2,1,0:T(8,128)(2,1)S(1)} collective-permute-done((bf16[2,448,256]{2,1,0:T(8,128)(2,1)S(1)}, bf16[2,448,256]{2,1,0:T(8,128)(2,1)S(1)}, u32[]{:S(2)}, u32[]{:S(2)}) %collective-permute-start.7) | collective-permute-done | bytes 458784 | tf_op jit(solution)/shard_map/ppermute | solution.py:28
  73.4 3.9 %collective-permute-done.8.previous = bf16[2,448,256]{2,1,0:T(8,128)(2,1)S(1)} collective-permute-done((bf16[2,448,256]{2,1,0:T(8,128)(2,1)S(1)}, bf16[2,448,256]{2,1,0:T(8,128)(2,1)S(1)}, u32[]{:S(2)}, u32[]{:S(2)}) %collective-permute-start.8) | collective-permute-done | bytes 458784 | tf_op jit(solution)/shard_map/ppermute | solution.py:28
  80.0 5.1 %collective-permute-start.10 = (bf16[2,224,256]{2,1,0:T(8,128)(2,1)}, bf16[2,224,256]{2,1,0:T(8,128)(2,1)S(1)}, u32[]{:S(2)}, u32[]{:S(2)}) collective-permute-start(bf16[2,224,256]{2,1,0:T(8,128)(2,1)} %get-tuple-element.30), channel_id=1, source_target_pairs={{0,384},{128,0},{256,128},{384,256},{1,385},{129,1},{257,129},{385... | collective-permute-start | bytes 688136 | tf_op jit(solution)/shard_map/ppermute | solution.py:35
  85.4 4.3 %collective-permute-start.11 = (bf16[152,448]{1,0:T(8,128)(2,1)S(1)}, bf16[152,448]{1,0:T(8,128)(2,1)S(1)}, u32[]{:S(2)}, u32[]{:S(2)}) collective-permute-start(bf16[152,448]{1,0:T(8,128)(2,1)S(1)} %shard_map.72.hidden), channel_id=1, source_target_pairs={{0,32},{32,0},{64,96},{96,64},{1,33},{33,1},{65,97},{97,65},{2,34}... | collective-permute-start | bytes 408584 | tf_op jit(solution)/shard_map/ppermute | solution.py:223
  90.3 4.9 %collective-permute-done.11.hidden = bf16[152,448]{1,0:T(8,128)(2,1)S(1)} collective-permute-done((bf16[152,448]{1,0:T(8,128)(2,1)S(1)}, bf16[152,448]{1,0:T(8,128)(2,1)S(1)}, u32[]{:S(2)}, u32[]{:S(2)}) %collective-permute-start.11) | collective-permute-done | bytes 136224 | tf_op jit(solution)/shard_map/ppermute | solution.py:223
  95.6 1.9 %collective-permute-start.12 = (bf16[8,2,80,256]{3,2,1,0:T(8,128)(2,1)S(1)}, bf16[8,2,80,256]{3,2,1,0:T(8,128)(2,1)S(1)}, u32[]{:S(2)}, u32[]{:S(2)}) collective-permute-start(bf16[8,2,80,256]{3,2,1,0:T(8,128)(2,1)S(1)} %get-tuple-element.37), channel_id=1, source_target_pairs={{0,1},{1,0},{2,3},{3,2},{4,5},{5,4},{6,7},{7,6},{8,9},{9,8},{10,11... | collective-permute-start | bytes 1966088 | tf_op jit(solution)/shard_map/ppermute | solution.py:20
  97.6 2.1 %collective-permute-done.12 = bf16[8,2,80,256]{3,2,1,0:T(8,128)(2,1)S(1)} collective-permute-done((bf16[8,2,80,256]{3,2,1,0:T(8,128)(2,1)S(1)}, bf16[8,2,80,256]{3,2,1,0:T(8,128)(2,1)S(1)}, u32[]{:S(2)}, u32[]{:S(2)}) %collective-permute-start.12) | collective-permute-done | bytes 655392 | tf_op jit(solution)/shard_map/ppermute | solution.py:20
  100.9 28.3 %all_to_all.15 = bf16[16,80,256]{2,1,0:T(8,128)(2,1)S(1)} all-to-all(bf16[16,80,256]{2,1,0:T(8,128)(2,1)S(1)} %copy.24), channel_id=1, replica_groups=mesh['x'=4,'h'=4,'l'=2,'a'=2,'b'=4,'c'=2] {'l','a','b'}, dimensions={0} | all-to-all | bytes 1310720 | tf_op jit(solution)/shard_map/all_to_all | solution.py:24
  129.3 4.4 %collective-permute-start.14 = (bf16[16,256]{1,0:T(8,128)(2,1)S(1)}, bf16[16,256]{1,0:T(8,128)(2,1)S(1)}, u32[]{:S(2)}, u32[]{:S(2)}) collective-permute-start(bf16[16,256]{1,0:T(8,128)(2,1)S(1)} %slice.29), channel_id=1, source_target_pairs={{0,0},{2,2},{4,64},{6,66},{8,128},{10,130},{12,192},{14,194},{16,2... | collective-permute-start | bytes 24584 | tf_op jit(solution)/shard_map/ppermute | solution.py:247
  133.7 2.4 %collective-permute-start.13 = (bf16[4,2,4,256]{3,2,1,0:T(4,128)(2,1)S(1)}, bf16[4,2,4,256]{3,2,1,0:T(4,128)(2,1)S(1)}, u32[]{:S(2)}, u32[]{:S(2)}) collective-permute-start(bf16[4,2,4,256]{3,2,1,0:T(4,128)(2,1)S(1)} %get-tuple-element.38), channel_id=1, source_target_pairs={{0,32},{32,0},{64,96},{96,64},{1,33},{33,1},{65,97},{97,65},{2,34}... | collective-permute-start | bytes 49160 | tf_op jit(solution)/shard_map/ppermute | solution.py:265
  136.1 6.9 %collective-permute-done.14.rows = bf16[16,256]{1,0:T(8,128)(2,1)S(1)} collective-permute-done((bf16[16,256]{1,0:T(8,128)(2,1)S(1)}, bf16[16,256]{1,0:T(8,128)(2,1)S(1)}, u32[]{:S(2)}, u32[]{:S(2)}) %collective-permute-start.14) | collective-permute-done | bytes 8224 | tf_op jit(solution)/shard_map/ppermute | solution.py:247
  (49 shorter events, 13.3 us)
Async XLA Ops:
  0.6 0.9 copy-start
  1.8 17.1 %collective-permute-start = (bf16[160,128]{1,0:T(8,128)(2,1)S(1)}, bf16[160,128]{1,0:T(8,128)(2,1)S(1)}, u32[]{:S(2)}, u32[]{:S(2)}) collective-permute-start(bf16[160,128]{1,0:T(8,128)(2,1)S(1)} %maximum_maximum_fusion), channel_id=1, source_target_pairs={{0,0},{2,32},{4,64},{6,96},{32,2},{34,34},{36,66},{38,98},{64,4},{... | collective-permute-start | bytes 122888 | tf_op jit(solution)/shard_map/ppermute | solution.py:196
  9.9 0.9 copy-start.2
  10.8 0.9 copy-start.3
  11.8 18.2 %collective-permute-start.1 = (bf16[896,256]{1,0:T(8,128)(2,1)S(1)}, bf16[896,256]{1,0:T(8,128)(2,1)S(1)}, u32[]{:S(2)}, u32[]{:S(2)}) collective-permute-start(bf16[896,256]{1,0:T(8,128)(2,1)S(1)} %shard_map.68.own), channel_id=1, source_target_pairs={{0,128},{128,256},{256,384},{384,0},{1,129},{129,257},{257,385},{3... | collective-permute-start | bytes 1376264 | tf_op jit(solution)/shard_map/ppermute | solution.py:28
  15.2 14.8 %collective-permute-start.2 = (bf16[896,256]{1,0:T(8,128)(2,1)S(1)}, bf16[896,256]{1,0:T(8,128)(2,1)S(1)}, u32[]{:S(2)}, u32[]{:S(2)}) collective-permute-start(bf16[896,256]{1,0:T(8,128)(2,1)S(1)} %shard_map.68.own), channel_id=1, source_target_pairs={{0,384},{128,0},{256,128},{384,256},{1,385},{129,1},{257,129},{385... | collective-permute-start | bytes 1376264 | tf_op jit(solution)/shard_map/ppermute | solution.py:28
  19.8 27.1 %all-to-all-start = ((bf16[16,160,128]{2,1,0:T(8,128)(2,1)}), bf16[16,160,128]{2,1,0:T(8,128)(2,1)S(1)}, u32[]{:S(2)}, u32[]{:S(2)}) async-start(bf16[16,160,128]{2,1,0:T(8,128)(2,1)} %broadcast_in_dim.7), calls=%async_computation | async-start | bytes 1310720 | tf_op jit(solution)/shard_map/all_to_all | solution.py:24
  30.0 7.3 %copy-start.1 = (bf16[448,256]{1,0:T(8,128)(2,1)S(1)}, bf16[448,256]{1,0:T(8,128)(2,1)}, u32[]{:S(2)}) copy-start(bf16[448,256]{1,0:T(8,128)(2,1)} %own.1) | copy-start | bytes 688132
  30.1 10.4 %collective-permute-start.3 = (bf16[448,256]{1,0:T(8,128)(2,1)S(1)}, bf16[448,256]{1,0:T(8,128)(2,1)S(1)}, u32[]{:S(2)}, u32[]{:S(2)}) collective-permute-start(bf16[448,256]{1,0:T(8,128)(2,1)S(1)} %get-tuple-element.20), channel_id=1, source_target_pairs={{0,128},{128,256},{256,384},{384,0},{1,129},{129,257},{257,385},{3... | collective-permute-start | bytes 688136 | tf_op jit(solution)/shard_map/ppermute | solution.py:35
  32.4 8.4 %collective-permute-start.4 = (bf16[448,256]{1,0:T(8,128)(2,1)S(1)}, bf16[448,256]{1,0:T(8,128)(2,1)S(1)}, u32[]{:S(2)}, u32[]{:S(2)}) collective-permute-start(bf16[448,256]{1,0:T(8,128)(2,1)S(1)} %get-tuple-element.21), channel_id=1, source_target_pairs={{0,384},{128,0},{256,128},{384,256},{1,385},{129,1},{257,129},{385... | collective-permute-start | bytes 688136 | tf_op jit(solution)/shard_map/ppermute | solution.py:35
  37.3 14.0 %collective-permute-start.6 = (bf16[448,256]{1,0:T(8,128)(2,1)S(1)}, bf16[448,256]{1,0:T(8,128)(2,1)S(1)}, u32[]{:S(2)}, u32[]{:S(2)}) collective-permute-start(bf16[448,256]{1,0:T(8,128)(2,1)S(1)} %copy-done.1), channel_id=1, source_target_pairs={{0,64},{32,96},{64,0},{96,32},{1,65},{33,97},{65,1},{97,33},{2,66}... | collective-permute-start | bytes 688136 | tf_op jit(solution)/shard_map/ppermute | solution.py:205
  46.9 4.4 %collective-permute-start.5 = (bf16[16,160,128]{2,1,0:T(8,128)(2,1)S(1)}, bf16[16,160,128]{2,1,0:T(8,128)(2,1)S(1)}, u32[]{:S(2)}, u32[]{:S(2)}) collective-permute-start(bf16[16,160,128]{2,1,0:T(8,128)(2,1)S(1)} %all-to-all-done.feats), channel_id=1, source_target_pairs={{0,1},{1,0},{2,3},{3,2},{4,5},{5,4},{6,7},{7,6},{8,9},{9,8},{10,11... | collective-permute-start | bytes 1966088 | tf_op jit(solution)/shard_map/ppermute | solution.py:20
  53.9 31.2 %all-to-all-start.1 = ((bf16[4,152,896]{2,1,0:T(8,128)(2,1)}), bf16[4,152,896]{2,1,0:T(8,128)(2,1)S(1)}, u32[]{:S(2)}, u32[]{:S(2)}) async-start(bf16[4,152,896]{2,1,0:T(8,128)(2,1)} %get-tuple-element.26), calls=%async_computation.1 | async-start | bytes 2179072 | tf_op jit(solution)/shard_map/all_to_all | solution.py:24
  61.2 12.2 %collective-permute-start.7 = (bf16[2,448,256]{2,1,0:T(8,128)(2,1)S(1)}, bf16[2,448,256]{2,1,0:T(8,128)(2,1)S(1)}, u32[]{:S(2)}, u32[]{:S(2)}) collective-permute-start(bf16[2,448,256]{2,1,0:T(8,128)(2,1)S(1)} %shard_map.73.own), channel_id=1, source_target_pairs={{0,384},{128,0},{256,128},{384,256},{1,385},{129,1},{257,129},{385... | collective-permute-start | bytes 1376264 | tf_op jit(solution)/shard_map/ppermute | solution.py:28
  63.6 13.6 %collective-permute-start.8 = (bf16[2,448,256]{2,1,0:T(8,128)(2,1)S(1)}, bf16[2,448,256]{2,1,0:T(8,128)(2,1)S(1)}, u32[]{:S(2)}, u32[]{:S(2)}) collective-permute-start(bf16[2,448,256]{2,1,0:T(8,128)(2,1)S(1)} %shard_map.73.own), channel_id=1, source_target_pairs={{0,128},{128,256},{256,384},{384,0},{1,129},{129,257},{257,385},{3... | collective-permute-start | bytes 1376264 | tf_op jit(solution)/shard_map/ppermute | solution.py:28
  78.1 11.7 %collective-permute-start.9 = (bf16[2,224,256]{2,1,0:T(8,128)(2,1)}, bf16[2,224,256]{2,1,0:T(8,128)(2,1)S(1)}, u32[]{:S(2)}, u32[]{:S(2)}) collective-permute-start(bf16[2,224,256]{2,1,0:T(8,128)(2,1)} %get-tuple-element.29), channel_id=1, source_target_pairs={{0,128},{128,256},{256,384},{384,0},{1,129},{129,257},{257,385},{3... | collective-permute-start | bytes 688136 | tf_op jit(solution)/shard_map/ppermute | solution.py:35
  80.0 9.8 %collective-permute-start.10 = (bf16[2,224,256]{2,1,0:T(8,128)(2,1)}, bf16[2,224,256]{2,1,0:T(8,128)(2,1)S(1)}, u32[]{:S(2)}, u32[]{:S(2)}) collective-permute-start(bf16[2,224,256]{2,1,0:T(8,128)(2,1)} %get-tuple-element.30), channel_id=1, source_target_pairs={{0,384},{128,0},{256,128},{384,256},{1,385},{129,1},{257,129},{385... | collective-permute-start | bytes 688136 | tf_op jit(solution)/shard_map/ppermute | solution.py:35
  85.4 9.7 %collective-permute-start.11 = (bf16[152,448]{1,0:T(8,128)(2,1)S(1)}, bf16[152,448]{1,0:T(8,128)(2,1)S(1)}, u32[]{:S(2)}, u32[]{:S(2)}) collective-permute-start(bf16[152,448]{1,0:T(8,128)(2,1)S(1)} %shard_map.72.hidden), channel_id=1, source_target_pairs={{0,32},{32,0},{64,96},{96,64},{1,33},{33,1},{65,97},{97,65},{2,34}... | collective-permute-start | bytes 408584 | tf_op jit(solution)/shard_map/ppermute | solution.py:223
  95.6 4.0 %collective-permute-start.12 = (bf16[8,2,80,256]{3,2,1,0:T(8,128)(2,1)S(1)}, bf16[8,2,80,256]{3,2,1,0:T(8,128)(2,1)S(1)}, u32[]{:S(2)}, u32[]{:S(2)}) collective-permute-start(bf16[8,2,80,256]{3,2,1,0:T(8,128)(2,1)S(1)} %get-tuple-element.37), channel_id=1, source_target_pairs={{0,1},{1,0},{2,3},{3,2},{4,5},{5,4},{6,7},{7,6},{8,9},{9,8},{10,11... | collective-permute-start | bytes 1966088 | tf_op jit(solution)/shard_map/ppermute | solution.py:20
  129.3 13.7 %collective-permute-start.14 = (bf16[16,256]{1,0:T(8,128)(2,1)S(1)}, bf16[16,256]{1,0:T(8,128)(2,1)S(1)}, u32[]{:S(2)}, u32[]{:S(2)}) collective-permute-start(bf16[16,256]{1,0:T(8,128)(2,1)S(1)} %slice.29), channel_id=1, source_target_pairs={{0,0},{2,2},{4,64},{6,66},{8,128},{10,130},{12,192},{14,194},{16,2... | collective-permute-start | bytes 24584 | tf_op jit(solution)/shard_map/ppermute | solution.py:247
  133.7 9.9 %collective-permute-start.13 = (bf16[4,2,4,256]{3,2,1,0:T(4,128)(2,1)S(1)}, bf16[4,2,4,256]{3,2,1,0:T(4,128)(2,1)S(1)}, u32[]{:S(2)}, u32[]{:S(2)}) collective-permute-start(bf16[4,2,4,256]{3,2,1,0:T(4,128)(2,1)S(1)} %get-tuple-element.38), channel_id=1, source_target_pairs={{0,32},{32,0},{64,96},{96,64},{1,33},{33,1},{65,97},{97,65},{2,34}... | collective-permute-start | bytes 49160 | tf_op jit(solution)/shard_map/ppermute | solution.py:265

commit v5 on v4

--- a/solution.py
+++ b/solution.py
@@ -13,7 +13,7 @@
 UP = [(i, (i + 1) % 4) for i in range(4)]
 DOWN = [(i, (i + 3) % 4) for i in range(4)]
 VMEM = 16 * 2**20
-HINTS = (5.5, 0.1, 1, 0.1, 5, 8, 5)
+HINTS = (5.5, 0.1, 1, 0.1, 5, 8, 5, 5)
 
 
 def swap_cores(value):
@@ -59,6 +59,17 @@
     out[even + ff :] = up[even:]
 
 
+def rows_kernel(tokens, decode, out):
+    count = tokens.shape[0]
+    to = lax.broadcasted_iota(jnp.int32, (count, count), 0)
+    source = lax.broadcasted_iota(jnp.int32, (count, count), 1)
+    half = count // 2
+    place = to % half // 4 * 8 + to // half * 4 + to % 4
+    moved = dot((place == source).astype(BF16), tokens[...])
+    fill = jnp.zeros((out.shape[0] - count - decode.shape[0], tokens.shape[1]), F32)
+    out[...] = jnp.concatenate([moved, decode[...].astype(F32), fill], axis=0).astype(BF16)
+
+
 def halves_kernel(previous, following, up, down):
     half = up.shape[-2]
     up[...] = previous[..., :half, :]
@@ -76,12 +87,13 @@
     block = feats.shape[2]
     part = pl.ds(pl.multiple_of(which * block, block), block)
     opposite = jnp.concatenate([first[:, part], second[:, part]], axis=0)
-    total = None
-    for slot, weight in enumerate((own[:, part], following[:, part], opposite, previous[:, part])):
-        lhs = jnp.concatenate([feats[lax.rem(x + slot, 4) * 4 + b] for b in range(4)], axis=0)
-        term = lax.dot_general(lhs, weight, (((1,), (1,)), ((), ())), preferred_element_type=F32)
-        total = term if total is None else total + term
-    return total
+    rhs = jnp.concatenate([own[:, part], following[:, part], opposite, previous[:, part]], axis=1)
+    lhs = [
+        jnp.concatenate([feats[lax.rem(x + slot, 4) * 4 + b] for b in range(4)], axis=0) for slot in range(4)
+    ]
+    return lax.dot_general(
+        jnp.concatenate(lhs, axis=1), rhs, (((1,), (1,)), ((), ())), preferred_element_type=F32
+    )
 
 
 def gate_up_start_kernel(feats, own, following, first, second, previous, out):
@@ -185,13 +197,8 @@
     used, total = n_rows + n_dec, 2 * each
 
     decode_part = lax.dynamic_slice_in_dim(decode_in, yz * block, block, 2)
-    feats = jnp.concatenate(
-        [
-            tokens.reshape(16, 2, 4, block).transpose(1, 0, 2, 3).reshape(n_rows, block),
-            decode_part.transpose(1, 0, 2).reshape(n_dec, block),
-            jnp.zeros((total - used, block), BF16),
-        ],
-        axis=0,
+    feats = call(rows_kernel, jax.ShapeDtypeStruct((total, block), BF16), HINTS[7])(
+        tokens, decode_part.transpose(1, 0, 2).reshape(n_dec, block)
     )
     feats = lax.ppermute(
         feats, ("h", "b"), [(h * 4 + b, b * 4 + h) for h in range(4) for b in range(4)]

time: 145 us -> 143 us (0.986)
  waiting for transfers between devices: 31.5 us -> 33.1 us
  transfers between devices with their start and end apart: 17 -> 17, of which waited for: 8 -> 8; matrix products, arithmetic and copies ran while one was open for 1% -> 1% of each run, Pallas kernels for 3% -> 2%
where the time goes in v5:
time: 143 us
  starting transfers between devices  69.7 us (49%)
  waiting for transfers between devices  33.1 us (23%)
  blocking collectives  28.3 us (20%)
  Pallas kernels  6.61 us (5%)
  local copies, waits for them, and re-layouts  3.54 us (2%)
    all_to_all x1, blocking collectives, exchange(): return lax.all_to_all(blocks, axes, split_axis=0, concat_axis=0, tiled=True)  28.3 us
    all_to_all x2, starting transfers between devices, exchange(): return lax.all_to_all(blocks, axes, split_axis=0, concat_axis=0, tiled=True)  17.4 us
    ppermute x4, starting transfers between devices, far(): return (lax.ppermute(up, axis, UP), lax.ppermute(down, axis, DOWN))  14.2 us
    ppermute x4, starting transfers between devices, near(): return (lax.ppermute(value, axis, DOWN), lax.ppermute(value, axis, UP))  12.9 us
    ppermute x4, waiting for transfers between devices, near(): return (lax.ppermute(value, axis, DOWN), lax.ppermute(value, axis, UP))  10.9 us
    ppermute x1, starting transfers between devices, local(): lax.ppermute(feats, ('h', 'b'), [(h * 4 + b, b * 4 + h) for h in range(4)...  8.25 us
    ppermute x1, waiting for transfers between devices, local(): lax.ppermute(sums[half:], ('x', 'h', 'l', 'a', 'b'), [(x * 64 + h * 16 +...  7.96 us
    all_to_all x2, waiting for transfers between devices, exchange(): return lax.all_to_all(blocks, axes, split_axis=0, concat_axis=0, tiled=True)  6.15 us
  transfers between devices with their start and end apart: 17, of which 8 were waited for; matrix products, arithmetic and copies ran while one was open for 1% of the time, Pallas kernels for 2%

profile of v5, /device:TPU:56, one launch (start us, length us, event | category | flops | bytes accessed | tf_op | source)
XLA Modules:
  0.0 142.7 jit_solution(4800632986528011205)
XLA Ops:
  2.5 8.2 %collective-permute-start = (bf16[160,128]{1,0:T(8,128)(2,1)S(1)}, bf16[160,128]{1,0:T(8,128)(2,1)S(1)}, u32[]{:S(2)}, u32[]{:S(2)}) collective-permute-start(bf16[160,128]{1,0:T(8,128)(2,1)S(1)} %shard_map.68), channel_id=1, source_target_pairs={{0,0},{2,32},{4,64},{6,96},{32,2},{34,34},{36,66},{38,98},{64,4},{... | collective-permute-start | bytes 122888 | tf_op jit(solution)/shard_map/ppermute | solution.py:203
  10.8 3.4 %collective-permute-start.1 = (bf16[896,256]{1,0:T(8,128)(2,1)S(1)}, bf16[896,256]{1,0:T(8,128)(2,1)S(1)}, u32[]{:S(2)}, u32[]{:S(2)}) collective-permute-start(bf16[896,256]{1,0:T(8,128)(2,1)S(1)} %shard_map.69.own), channel_id=1, source_target_pairs={{0,128},{128,256},{256,384},{384,0},{1,129},{129,257},{257,385},{3... | collective-permute-start | bytes 1376264 | tf_op jit(solution)/shard_map/ppermute | solution.py:28
  14.2 3.7 %collective-permute-start.2 = (bf16[896,256]{1,0:T(8,128)(2,1)S(1)}, bf16[896,256]{1,0:T(8,128)(2,1)S(1)}, u32[]{:S(2)}, u32[]{:S(2)}) collective-permute-start(bf16[896,256]{1,0:T(8,128)(2,1)S(1)} %shard_map.69.own), channel_id=1, source_target_pairs={{0,384},{128,0},{256,128},{384,256},{1,385},{129,1},{257,129},{385... | collective-permute-start | bytes 1376264 | tf_op jit(solution)/shard_map/ppermute | solution.py:28
  18.8 10.2 %all-to-all-start = ((bf16[16,160,128]{2,1,0:T(8,128)(2,1)}), bf16[16,160,128]{2,1,0:T(8,128)(2,1)S(1)}, u32[]{:S(2)}, u32[]{:S(2)}) async-start(bf16[16,160,128]{2,1,0:T(8,128)(2,1)} %broadcast_in_dim.3), calls=%async_computation | async-start | bytes 1310720 | tf_op jit(solution)/shard_map/all_to_all | solution.py:24
  29.1 2.3 %collective-permute-start.3 = (bf16[448,256]{1,0:T(8,128)(2,1)S(1)}, bf16[448,256]{1,0:T(8,128)(2,1)S(1)}, u32[]{:S(2)}, u32[]{:S(2)}) collective-permute-start(bf16[448,256]{1,0:T(8,128)(2,1)S(1)} %get-tuple-element.20), channel_id=1, source_target_pairs={{0,128},{128,256},{256,384},{384,0},{1,129},{129,257},{257,385},{3... | collective-permute-start | bytes 688136 | tf_op jit(solution)/shard_map/ppermute | solution.py:35
  31.4 4.9 %collective-permute-start.4 = (bf16[448,256]{1,0:T(8,128)(2,1)S(1)}, bf16[448,256]{1,0:T(8,128)(2,1)S(1)}, u32[]{:S(2)}, u32[]{:S(2)}) collective-permute-start(bf16[448,256]{1,0:T(8,128)(2,1)S(1)} %get-tuple-element.21), channel_id=1, source_target_pairs={{0,384},{128,0},{256,128},{384,256},{1,385},{129,1},{257,129},{385... | collective-permute-start | bytes 688136 | tf_op jit(solution)/shard_map/ppermute | solution.py:35
  36.3 3.2 %collective-permute-start.6 = (bf16[448,256]{1,0:T(8,128)(2,1)S(1)}, bf16[448,256]{1,0:T(8,128)(2,1)S(1)}, u32[]{:S(2)}, u32[]{:S(2)}) collective-permute-start(bf16[448,256]{1,0:T(8,128)(2,1)S(1)} %copy-done.1), channel_id=1, source_target_pairs={{0,64},{32,96},{64,0},{96,32},{1,65},{33,97},{65,1},{97,33},{2,66}... | collective-permute-start | bytes 688136 | tf_op jit(solution)/shard_map/ppermute | solution.py:212
  39.8 6.1 %all-to-all-done.feats = bf16[16,160,128]{2,1,0:T(8,128)(2,1)S(1)} async-done(((bf16[16,160,128]{2,1,0:T(8,128)(2,1)}), bf16[16,160,128]{2,1,0:T(8,128)(2,1)S(1)}, u32[]{:S(2)}, u32[]{:S(2)}) %all-to-all-start) | async-done | bytes 655392 | tf_op jit(solution)/shard_map/all_to_all | solution.py:24
  45.9 1.9 %collective-permute-start.5 = (bf16[16,160,128]{2,1,0:T(8,128)(2,1)S(1)}, bf16[16,160,128]{2,1,0:T(8,128)(2,1)S(1)}, u32[]{:S(2)}, u32[]{:S(2)}) collective-permute-start(bf16[16,160,128]{2,1,0:T(8,128)(2,1)S(1)} %all-to-all-done.feats), channel_id=1, source_target_pairs={{0,1},{1,0},{2,3},{3,2},{4,5},{5,4},{6,7},{7,6},{8,9},{9,8},{10,11... | collective-permute-start | bytes 1966088 | tf_op jit(solution)/shard_map/ppermute | solution.py:20
  50.3 2.1 %shard_map.72 = (bf16[4,152,896]{2,1,0:T(8,128)(2,1)}, bf16[152,896]{1,0:T(8,128)(2,1)S(1)}) custom-call(bf16[16,160,128]{2,1,0:T(8,128)(2,1)S(1)} %collective-permute-done.5.feats, f32[640,896]{1,0:T(8,128)S(1)} %shard_map.71.started, bf16[896,256]{1,0:T(8,128)(2,1)S(1)} %shard_map.69.own, bf16[896,256]{1,0:T(8,128)(2,1)S(1)} %collective-permute-done.2.following, ...), custom_call_target="tpu_custom_call" | custom-call | flops 110000000 | bytes 1048576 | tf_op jit(solution)/shard_map/pallas_call | solution.py:219
  52.4 7.2 %all-to-all-start.1 = ((bf16[4,152,896]{2,1,0:T(8,128)(2,1)}), bf16[4,152,896]{2,1,0:T(8,128)(2,1)S(1)}, u32[]{:S(2)}, u32[]{:S(2)}) async-start(bf16[4,152,896]{2,1,0:T(8,128)(2,1)} %get-tuple-element.26), calls=%async_computation.1 | async-start | bytes 2179072 | tf_op jit(solution)/shard_map/all_to_all | solution.py:24
  59.7 2.9 %collective-permute-start.7 = (bf16[2,448,256]{2,1,0:T(8,128)(2,1)S(1)}, bf16[2,448,256]{2,1,0:T(8,128)(2,1)S(1)}, u32[]{:S(2)}, u32[]{:S(2)}) collective-permute-start(bf16[2,448,256]{2,1,0:T(8,128)(2,1)S(1)} %shard_map.74.own), channel_id=1, source_target_pairs={{0,384},{128,0},{256,128},{384,256},{1,385},{129,1},{257,129},{385... | collective-permute-start | bytes 1376264 | tf_op jit(solution)/shard_map/ppermute | solution.py:28
  62.5 3.0 %collective-permute-start.8 = (bf16[2,448,256]{2,1,0:T(8,128)(2,1)S(1)}, bf16[2,448,256]{2,1,0:T(8,128)(2,1)S(1)}, u32[]{:S(2)}, u32[]{:S(2)}) collective-permute-start(bf16[2,448,256]{2,1,0:T(8,128)(2,1)S(1)} %shard_map.74.own), channel_id=1, source_target_pairs={{0,128},{128,256},{256,384},{384,0},{1,129},{129,257},{257,385},{3... | collective-permute-start | bytes 1376264 | tf_op jit(solution)/shard_map/ppermute | solution.py:28
  65.5 6.3 %collective-permute-done.7.following = bf16[2,448,256]{2,1,0:T(8,128)(2,1)S(1)} collective-permute-done((bf16[2,448,256]{2,1,0:T(8,128)(2,1)S(1)}, bf16[2,448,256]{2,1,0:T(8,128)(2,1)S(1)}, u32[]{:S(2)}, u32[]{:S(2)}) %collective-permute-start.7) | collective-permute-done | bytes 458784 | tf_op jit(solution)/shard_map/ppermute | solution.py:28
  71.9 4.6 %collective-permute-done.8.previous = bf16[2,448,256]{2,1,0:T(8,128)(2,1)S(1)} collective-permute-done((bf16[2,448,256]{2,1,0:T(8,128)(2,1)S(1)}, bf16[2,448,256]{2,1,0:T(8,128)(2,1)S(1)}, u32[]{:S(2)}, u32[]{:S(2)}) %collective-permute-start.8) | collective-permute-done | bytes 458784 | tf_op jit(solution)/shard_map/ppermute | solution.py:28
  79.1 5.1 %collective-permute-start.10 = (bf16[2,224,256]{2,1,0:T(8,128)(2,1)}, bf16[2,224,256]{2,1,0:T(8,128)(2,1)S(1)}, u32[]{:S(2)}, u32[]{:S(2)}) collective-permute-start(bf16[2,224,256]{2,1,0:T(8,128)(2,1)} %get-tuple-element.30), channel_id=1, source_target_pairs={{0,384},{128,0},{256,128},{384,256},{1,385},{129,1},{257,129},{385... | collective-permute-start | bytes 688136 | tf_op jit(solution)/shard_map/ppermute | solution.py:35
  84.6 4.3 %collective-permute-start.11 = (bf16[152,448]{1,0:T(8,128)(2,1)S(1)}, bf16[152,448]{1,0:T(8,128)(2,1)S(1)}, u32[]{:S(2)}, u32[]{:S(2)}) collective-permute-start(bf16[152,448]{1,0:T(8,128)(2,1)S(1)} %shard_map.73.hidden), channel_id=1, source_target_pairs={{0,32},{32,0},{64,96},{96,64},{1,33},{33,1},{65,97},{97,65},{2,34}... | collective-permute-start | bytes 408584 | tf_op jit(solution)/shard_map/ppermute | solution.py:230
  89.4 4.2 %collective-permute-done.11.hidden = bf16[152,448]{1,0:T(8,128)(2,1)S(1)} collective-permute-done((bf16[152,448]{1,0:T(8,128)(2,1)S(1)}, bf16[152,448]{1,0:T(8,128)(2,1)S(1)}, u32[]{:S(2)}, u32[]{:S(2)}) %collective-permute-start.11) | collective-permute-done | bytes 136224 | tf_op jit(solution)/shard_map/ppermute | solution.py:230
  94.1 1.9 %collective-permute-start.12 = (bf16[8,2,80,256]{3,2,1,0:T(8,128)(2,1)S(1)}, bf16[8,2,80,256]{3,2,1,0:T(8,128)(2,1)S(1)}, u32[]{:S(2)}, u32[]{:S(2)}) collective-permute-start(bf16[8,2,80,256]{3,2,1,0:T(8,128)(2,1)S(1)} %get-tuple-element.37), channel_id=1, source_target_pairs={{0,1},{1,0},{2,3},{3,2},{4,5},{5,4},{6,7},{7,6},{8,9},{9,8},{10,11... | collective-permute-start | bytes 1966088 | tf_op jit(solution)/shard_map/ppermute | solution.py:20
  96.0 2.1 %collective-permute-done.12 = bf16[8,2,80,256]{3,2,1,0:T(8,128)(2,1)S(1)} collective-permute-done((bf16[8,2,80,256]{3,2,1,0:T(8,128)(2,1)S(1)}, bf16[8,2,80,256]{3,2,1,0:T(8,128)(2,1)S(1)}, u32[]{:S(2)}, u32[]{:S(2)}) %collective-permute-start.12) | collective-permute-done | bytes 655392 | tf_op jit(solution)/shard_map/ppermute | solution.py:20
  99.3 28.3 %all_to_all.15 = bf16[16,80,256]{2,1,0:T(8,128)(2,1)S(1)} all-to-all(bf16[16,80,256]{2,1,0:T(8,128)(2,1)S(1)} %copy.20), channel_id=1, replica_groups=mesh['x'=4,'h'=4,'l'=2,'a'=2,'b'=4,'c'=2] {'l','a','b'}, dimensions={0} | all-to-all | bytes 1310720 | tf_op jit(solution)/shard_map/all_to_all | solution.py:24
  127.8 3.1 %collective-permute-start.14 = (bf16[16,256]{1,0:T(8,128)(2,1)S(1)}, bf16[16,256]{1,0:T(8,128)(2,1)S(1)}, u32[]{:S(2)}, u32[]{:S(2)}) collective-permute-start(bf16[16,256]{1,0:T(8,128)(2,1)S(1)} %slice.29), channel_id=1, source_target_pairs={{0,0},{2,2},{4,64},{6,66},{8,128},{10,130},{12,192},{14,194},{16,2... | collective-permute-start | bytes 24584 | tf_op jit(solution)/shard_map/ppermute | solution.py:254
  130.9 2.5 %collective-permute-start.13 = (bf16[4,2,4,256]{3,2,1,0:T(4,128)(2,1)S(1)}, bf16[4,2,4,256]{3,2,1,0:T(4,128)(2,1)S(1)}, u32[]{:S(2)}, u32[]{:S(2)}) collective-permute-start(bf16[4,2,4,256]{3,2,1,0:T(4,128)(2,1)S(1)} %get-tuple-element.38), channel_id=1, source_target_pairs={{0,32},{32,0},{64,96},{96,64},{1,33},{33,1},{65,97},{97,65},{2,34}... | collective-permute-start | bytes 49160 | tf_op jit(solution)/shard_map/ppermute | solution.py:272
  133.5 8.0 %collective-permute-done.14.rows = bf16[16,256]{1,0:T(8,128)(2,1)S(1)} collective-permute-done((bf16[16,256]{1,0:T(8,128)(2,1)S(1)}, bf16[16,256]{1,0:T(8,128)(2,1)S(1)}, u32[]{:S(2)}, u32[]{:S(2)}) %collective-permute-start.14) | collective-permute-done | bytes 8224 | tf_op jit(solution)/shard_map/ppermute | solution.py:254
  (48 shorter events, 12.2 us)
Async XLA Ops:
  0.6 0.9 copy-start
  1.6 0.8 copy-start.4
  2.3 8.4 %copy-start.2 = (bf16[256,448]{0,1:T(8,128)(2,1)S(1)}, bf16[256,448]{0,1:T(8,128)(2,1)}, u32[]{:S(2)}) copy-start(bf16[256,448]{0,1:T(8,128)(2,1)} %param.6) | copy-start | bytes 688132
  2.3 8.4 %copy-start.3 = (bf16[256,448]{0,1:T(8,128)(2,1)S(1)}, bf16[256,448]{0,1:T(8,128)(2,1)}, u32[]{:S(2)}) copy-start(bf16[256,448]{0,1:T(8,128)(2,1)} %param.7) | copy-start | bytes 688132
  2.5 15.4 %collective-permute-start = (bf16[160,128]{1,0:T(8,128)(2,1)S(1)}, bf16[160,128]{1,0:T(8,128)(2,1)S(1)}, u32[]{:S(2)}, u32[]{:S(2)}) collective-permute-start(bf16[160,128]{1,0:T(8,128)(2,1)S(1)} %shard_map.68), channel_id=1, source_target_pairs={{0,0},{2,32},{4,64},{6,96},{32,2},{34,34},{36,66},{38,98},{64,4},{... | collective-permute-start | bytes 122888 | tf_op jit(solution)/shard_map/ppermute | solution.py:203
  10.8 18.2 %collective-permute-start.1 = (bf16[896,256]{1,0:T(8,128)(2,1)S(1)}, bf16[896,256]{1,0:T(8,128)(2,1)S(1)}, u32[]{:S(2)}, u32[]{:S(2)}) collective-permute-start(bf16[896,256]{1,0:T(8,128)(2,1)S(1)} %shard_map.69.own), channel_id=1, source_target_pairs={{0,128},{128,256},{256,384},{384,0},{1,129},{129,257},{257,385},{3... | collective-permute-start | bytes 1376264 | tf_op jit(solution)/shard_map/ppermute | solution.py:28
  14.2 14.8 %collective-permute-start.2 = (bf16[896,256]{1,0:T(8,128)(2,1)S(1)}, bf16[896,256]{1,0:T(8,128)(2,1)S(1)}, u32[]{:S(2)}, u32[]{:S(2)}) collective-permute-start(bf16[896,256]{1,0:T(8,128)(2,1)S(1)} %shard_map.69.own), channel_id=1, source_target_pairs={{0,384},{128,0},{256,128},{384,256},{1,385},{129,1},{257,129},{385... | collective-permute-start | bytes 1376264 | tf_op jit(solution)/shard_map/ppermute | solution.py:28
  18.8 27.1 %all-to-all-start = ((bf16[16,160,128]{2,1,0:T(8,128)(2,1)}), bf16[16,160,128]{2,1,0:T(8,128)(2,1)S(1)}, u32[]{:S(2)}, u32[]{:S(2)}) async-start(bf16[16,160,128]{2,1,0:T(8,128)(2,1)} %broadcast_in_dim.3), calls=%async_computation | async-start | bytes 1310720 | tf_op jit(solution)/shard_map/all_to_all | solution.py:24
  29.0 7.3 %copy-start.1 = (bf16[448,256]{1,0:T(8,128)(2,1)S(1)}, bf16[448,256]{1,0:T(8,128)(2,1)}, u32[]{:S(2)}) copy-start(bf16[448,256]{1,0:T(8,128)(2,1)} %own.1) | copy-start | bytes 688132
  29.1 10.4 %collective-permute-start.3 = (bf16[448,256]{1,0:T(8,128)(2,1)S(1)}, bf16[448,256]{1,0:T(8,128)(2,1)S(1)}, u32[]{:S(2)}, u32[]{:S(2)}) collective-permute-start(bf16[448,256]{1,0:T(8,128)(2,1)S(1)} %get-tuple-element.20), channel_id=1, source_target_pairs={{0,128},{128,256},{256,384},{384,0},{1,129},{129,257},{257,385},{3... | collective-permute-start | bytes 688136 | tf_op jit(solution)/shard_map/ppermute | solution.py:35
  31.4 8.4 %collective-permute-start.4 = (bf16[448,256]{1,0:T(8,128)(2,1)S(1)}, bf16[448,256]{1,0:T(8,128)(2,1)S(1)}, u32[]{:S(2)}, u32[]{:S(2)}) collective-permute-start(bf16[448,256]{1,0:T(8,128)(2,1)S(1)} %get-tuple-element.21), channel_id=1, source_target_pairs={{0,384},{128,0},{256,128},{384,256},{1,385},{129,1},{257,129},{385... | collective-permute-start | bytes 688136 | tf_op jit(solution)/shard_map/ppermute | solution.py:35
  36.3 14.0 %collective-permute-start.6 = (bf16[448,256]{1,0:T(8,128)(2,1)S(1)}, bf16[448,256]{1,0:T(8,128)(2,1)S(1)}, u32[]{:S(2)}, u32[]{:S(2)}) collective-permute-start(bf16[448,256]{1,0:T(8,128)(2,1)S(1)} %copy-done.1), channel_id=1, source_target_pairs={{0,64},{32,96},{64,0},{96,32},{1,65},{33,97},{65,1},{97,33},{2,66}... | collective-permute-start | bytes 688136 | tf_op jit(solution)/shard_map/ppermute | solution.py:212
  45.9 4.4 %collective-permute-start.5 = (bf16[16,160,128]{2,1,0:T(8,128)(2,1)S(1)}, bf16[16,160,128]{2,1,0:T(8,128)(2,1)S(1)}, u32[]{:S(2)}, u32[]{:S(2)}) collective-permute-start(bf16[16,160,128]{2,1,0:T(8,128)(2,1)S(1)} %all-to-all-done.feats), channel_id=1, source_target_pairs={{0,1},{1,0},{2,3},{3,2},{4,5},{5,4},{6,7},{7,6},{8,9},{9,8},{10,11... | collective-permute-start | bytes 1966088 | tf_op jit(solution)/shard_map/ppermute | solution.py:20
  52.4 31.9 %all-to-all-start.1 = ((bf16[4,152,896]{2,1,0:T(8,128)(2,1)}), bf16[4,152,896]{2,1,0:T(8,128)(2,1)S(1)}, u32[]{:S(2)}, u32[]{:S(2)}) async-start(bf16[4,152,896]{2,1,0:T(8,128)(2,1)} %get-tuple-element.26), calls=%async_computation.1 | async-start | bytes 2179072 | tf_op jit(solution)/shard_map/all_to_all | solution.py:24
  59.7 12.2 %collective-permute-start.7 = (bf16[2,448,256]{2,1,0:T(8,128)(2,1)S(1)}, bf16[2,448,256]{2,1,0:T(8,128)(2,1)S(1)}, u32[]{:S(2)}, u32[]{:S(2)}) collective-permute-start(bf16[2,448,256]{2,1,0:T(8,128)(2,1)S(1)} %shard_map.74.own), channel_id=1, source_target_pairs={{0,384},{128,0},{256,128},{384,256},{1,385},{129,1},{257,129},{385... | collective-permute-start | bytes 1376264 | tf_op jit(solution)/shard_map/ppermute | solution.py:28
  62.5 13.9 %collective-permute-start.8 = (bf16[2,448,256]{2,1,0:T(8,128)(2,1)S(1)}, bf16[2,448,256]{2,1,0:T(8,128)(2,1)S(1)}, u32[]{:S(2)}, u32[]{:S(2)}) collective-permute-start(bf16[2,448,256]{2,1,0:T(8,128)(2,1)S(1)} %shard_map.74.own), channel_id=1, source_target_pairs={{0,128},{128,256},{256,384},{384,0},{1,129},{129,257},{257,385},{3... | collective-permute-start | bytes 1376264 | tf_op jit(solution)/shard_map/ppermute | solution.py:28
  77.2 11.7 %collective-permute-start.9 = (bf16[2,224,256]{2,1,0:T(8,128)(2,1)}, bf16[2,224,256]{2,1,0:T(8,128)(2,1)S(1)}, u32[]{:S(2)}, u32[]{:S(2)}) collective-permute-start(bf16[2,224,256]{2,1,0:T(8,128)(2,1)} %get-tuple-element.29), channel_id=1, source_target_pairs={{0,128},{128,256},{256,384},{384,0},{1,129},{129,257},{257,385},{3... | collective-permute-start | bytes 688136 | tf_op jit(solution)/shard_map/ppermute | solution.py:35
  79.1 9.8 %collective-permute-start.10 = (bf16[2,224,256]{2,1,0:T(8,128)(2,1)}, bf16[2,224,256]{2,1,0:T(8,128)(2,1)S(1)}, u32[]{:S(2)}, u32[]{:S(2)}) collective-permute-start(bf16[2,224,256]{2,1,0:T(8,128)(2,1)} %get-tuple-element.30), channel_id=1, source_target_pairs={{0,384},{128,0},{256,128},{384,256},{1,385},{129,1},{257,129},{385... | collective-permute-start | bytes 688136 | tf_op jit(solution)/shard_map/ppermute | solution.py:35
  84.6 9.0 %collective-permute-start.11 = (bf16[152,448]{1,0:T(8,128)(2,1)S(1)}, bf16[152,448]{1,0:T(8,128)(2,1)S(1)}, u32[]{:S(2)}, u32[]{:S(2)}) collective-permute-start(bf16[152,448]{1,0:T(8,128)(2,1)S(1)} %shard_map.73.hidden), channel_id=1, source_target_pairs={{0,32},{32,0},{64,96},{96,64},{1,33},{33,1},{65,97},{97,65},{2,34}... | collective-permute-start | bytes 408584 | tf_op jit(solution)/shard_map/ppermute | solution.py:230
  94.1 4.0 %collective-permute-start.12 = (bf16[8,2,80,256]{3,2,1,0:T(8,128)(2,1)S(1)}, bf16[8,2,80,256]{3,2,1,0:T(8,128)(2,1)S(1)}, u32[]{:S(2)}, u32[]{:S(2)}) collective-permute-start(bf16[8,2,80,256]{3,2,1,0:T(8,128)(2,1)S(1)} %get-tuple-element.37), channel_id=1, source_target_pairs={{0,1},{1,0},{2,3},{3,2},{4,5},{5,4},{6,7},{7,6},{8,9},{9,8},{10,11... | collective-permute-start | bytes 1966088 | tf_op jit(solution)/shard_map/ppermute | solution.py:20
  127.8 13.7 %collective-permute-start.14 = (bf16[16,256]{1,0:T(8,128)(2,1)S(1)}, bf16[16,256]{1,0:T(8,128)(2,1)S(1)}, u32[]{:S(2)}, u32[]{:S(2)}) collective-permute-start(bf16[16,256]{1,0:T(8,128)(2,1)S(1)} %slice.29), channel_id=1, source_target_pairs={{0,0},{2,2},{4,64},{6,66},{8,128},{10,130},{12,192},{14,194},{16,2... | collective-permute-start | bytes 24584 | tf_op jit(solution)/shard_map/ppermute | solution.py:254
  130.9 11.1 %collective-permute-start.13 = (bf16[4,2,4,256]{3,2,1,0:T(4,128)(2,1)S(1)}, bf16[4,2,4,256]{3,2,1,0:T(4,128)(2,1)S(1)}, u32[]{:S(2)}, u32[]{:S(2)}) collective-permute-start(bf16[4,2,4,256]{3,2,1,0:T(4,128)(2,1)S(1)} %get-tuple-element.38), channel_id=1, source_target_pairs={{0,32},{32,0},{64,96},{96,64},{1,33},{33,1},{65,97},{97,65},{2,34}... | collective-permute-start | bytes 49160 | tf_op jit(solution)/shard_map/ppermute | solution.py:272

commit v6 on v5

--- a/solution.py
+++ b/solution.py
@@ -13,7 +13,7 @@
 UP = [(i, (i + 1) % 4) for i in range(4)]
 DOWN = [(i, (i + 3) % 4) for i in range(4)]
 VMEM = 16 * 2**20
-HINTS = (5.5, 0.1, 1, 0.1, 5, 8, 5, 5)
+HINTS = (4.95, 0.1, 1, 0.1, 5, 8, 5, 5)
 
 
 def swap_cores(value):
@@ -66,8 +66,7 @@
     half = count // 2
     place = to % half // 4 * 8 + to // half * 4 + to % 4
     moved = dot((place == source).astype(BF16), tokens[...])
-    fill = jnp.zeros((out.shape[0] - count - decode.shape[0], tokens.shape[1]), F32)
-    out[...] = jnp.concatenate([moved, decode[...].astype(F32), fill], axis=0).astype(BF16)
+    out[...] = jnp.concatenate([moved, decode[...].astype(F32)], axis=0).astype(BF16)
 
 
 def halves_kernel(previous, following, up, down):
@@ -88,8 +87,12 @@
     part = pl.ds(pl.multiple_of(which * block, block), block)
     opposite = jnp.concatenate([first[:, part], second[:, part]], axis=0)
     rhs = jnp.concatenate([own[:, part], following[:, part], opposite, previous[:, part]], axis=1)
+    fill = jnp.zeros((-feats.shape[1] % 16, block), BF16)
     lhs = [
-        jnp.concatenate([feats[lax.rem(x + slot, 4) * 4 + b] for b in range(4)], axis=0) for slot in range(4)
+        jnp.concatenate(
+            [part for b in range(4) for part in (feats[lax.rem(x + slot, 4) * 4 + b], fill)], axis=0
+        )
+        for slot in range(4)
     ]
     return lax.dot_general(
         jnp.concatenate(lhs, axis=1), rhs, (((1,), (1,)), ((), ())), preferred_element_type=F32
@@ -103,9 +106,9 @@
 def gate_up_kernel(feats, started, own, following, first, second, previous, partial, residue):
     h = lax.axis_index("h")
     blocks, rows, _ = partial.shape
-    stride = feats.shape[1]
     weights = (own, following, first, second, previous)
     total = started[...] + half_product(feats, weights, 1 - lax.axis_index("c"))
+    stride = total.shape[0] // blocks
     for b in range(blocks):
         part = total[b * stride : b * stride + rows]
         rounded = part.astype(BF16)
@@ -170,7 +173,7 @@
     width = mine.shape[3]
     for q in range(mine.shape[0]):
         for k in range(mine.shape[1]):
-            column = lax.bitwise_xor(h, 2 * k)
+            column = lax.bitwise_xor(h, 3 * k)
             for ref, at in ((mine, column), (theirs, lax.bitwise_xor(column, 1))):
                 out[:, pl.ds(pl.multiple_of((q * 4 + at) * width, width), width)] = ref[q, k]
 
@@ -197,19 +200,19 @@
     used, total = n_rows + n_dec, 2 * each
 
     decode_part = lax.dynamic_slice_in_dim(decode_in, yz * block, block, 2)
-    feats = call(rows_kernel, jax.ShapeDtypeStruct((total, block), BF16), HINTS[7])(
+    feats = call(rows_kernel, jax.ShapeDtypeStruct((used, block), BF16), HINTS[7])(
         tokens, decode_part.transpose(1, 0, 2).reshape(n_dec, block)
     )
     feats = lax.ppermute(
         feats, ("h", "b"), [(h * 4 + b, b * 4 + h) for h in range(4) for b in range(4)]
     )
-    feats = exchange(jnp.broadcast_to(feats, (16, total, block)), LZ)
+    feats = exchange(jnp.broadcast_to(feats, (16, used, block)), LZ)
     own = call(weights_kernel, jax.ShapeDtypeStruct((2 * ff, depth), BF16), 1)(
         gate_weight.T, up_weight.T
     )
     own_near = near(own, "x")
     own_far = far(*own_near, "x", HINTS[0])
-    opposite = lax.ppermute(down_weight, "h", [(i, (i + 2) % 4) for i in range(4)])
+    opposite = lax.ppermute(down_weight, "h", [(i, 3 - i) for i in range(4)])
     feats, own_far = lax.optimization_barrier((feats, own_far))
     other = swap_cores(feats)
 
@@ -257,7 +260,7 @@
         [
             (
                 x * 64 + h * 16 + q * 4 + k * 2 + r,
-                q * 64 + (h ^ 2 * k) * 16 + x * 4 + (h ^ r),
+                q * 64 + (h ^ 3 * k) * 16 + x * 4 + (h ^ r),
             )
             for x in range(4)
             for h in range(4)

time: 143 us -> 142 us (level)
  the two profiles are of different devices: /device:TPU:56 before, /device:TPU:6 now
where the time goes in v6:
time: 142 us; the launch traced here: 140 us
  starting transfers between devices  76.9 us (54%)
  blocking collectives  27.4 us (19%)
  waiting for transfers between devices  24.1 us (17%)
  Pallas kernels  6.61 us (5%)
  local copies, waits for them, and re-layouts  3.63 us (3%)
    all_to_all x1, blocking collectives, exchange(): return lax.all_to_all(blocks, axes, split_axis=0, concat_axis=0, tiled=True)  27.4 us
    all_to_all x2, starting transfers between devices, exchange(): return lax.all_to_all(blocks, axes, split_axis=0, concat_axis=0, tiled=True)  19.5 us
    ppermute x4, starting transfers between devices, near(): return (lax.ppermute(value, axis, DOWN), lax.ppermute(value, axis, UP))  16.7 us
    ppermute x4, starting transfers between devices, far(): return (lax.ppermute(up, axis, UP), lax.ppermute(down, axis, DOWN))  13.4 us
    ppermute x4, waiting for transfers between devices, near(): return (lax.ppermute(value, axis, DOWN), lax.ppermute(value, axis, UP))  8.48 us
    ppermute x1, starting transfers between devices, local(): partner = lax.ppermute(hidden, 'h', beside)  7.48 us
    ppermute x1, waiting for transfers between devices, local(): partner = lax.ppermute(hidden, 'h', beside)  6 us
    ppermute x1, starting transfers between devices, local(): opposite = lax.ppermute(down_weight, 'h', [(i, 3 - i) for i in range(4)])  5.36 us
  transfers between devices with their start and end apart: 17, of which 9 were waited for; matrix products, arithmetic and copies ran while one was open for 1% of the time, Pallas kernels for 2%

profile of v6, /device:TPU:6, one launch (start us, length us, event | category | flops | bytes accessed | tf_op | source)
XLA Modules:
  0.0 140.0 jit_solution(4342531349124109354)
XLA Ops:
  3.4 7.8 %collective-permute-start.1 = (bf16[896,256]{1,0:T(8,128)(2,1)S(1)}, bf16[896,256]{1,0:T(8,128)(2,1)S(1)}, u32[]{:S(2)}, u32[]{:S(2)}) collective-permute-start(bf16[896,256]{1,0:T(8,128)(2,1)S(1)} %shard_map.69.own), channel_id=1, source_target_pairs={{0,128},{128,256},{256,384},{384,0},{1,129},{129,257},{257,385},{3... | collective-permute-start | bytes 1376264 | tf_op jit(solution)/shard_map/ppermute | solution.py:28
  11.2 1.9 %collective-permute-start.2 = (bf16[896,256]{1,0:T(8,128)(2,1)S(1)}, bf16[896,256]{1,0:T(8,128)(2,1)S(1)}, u32[]{:S(2)}, u32[]{:S(2)}) collective-permute-start(bf16[896,256]{1,0:T(8,128)(2,1)S(1)} %shard_map.69.own), channel_id=1, source_target_pairs={{0,384},{128,0},{256,128},{384,256},{1,385},{129,1},{257,129},{385... | collective-permute-start | bytes 1376264 | tf_op jit(solution)/shard_map/ppermute | solution.py:28
  14.0 13.7 %all-to-all-start = ((bf16[16,152,128]{2,1,0:T(8,128)(2,1)}), bf16[16,152,128]{2,1,0:T(8,128)(2,1)S(1)}, u32[]{:S(2)}, u32[]{:S(2)}) async-start(bf16[16,152,128]{2,1,0:T(8,128)(2,1)} %broadcast_in_dim.3), calls=%async_computation | async-start | bytes 1245184 | tf_op jit(solution)/shard_map/all_to_all | solution.py:24
  27.8 3.7 %collective-permute-start.3 = (bf16[448,256]{1,0:T(8,128)(2,1)S(1)}, bf16[448,256]{1,0:T(8,128)(2,1)S(1)}, u32[]{:S(2)}, u32[]{:S(2)}) collective-permute-start(bf16[448,256]{1,0:T(8,128)(2,1)S(1)} %get-tuple-element.20), channel_id=1, source_target_pairs={{0,128},{128,256},{256,384},{384,0},{1,129},{129,257},{257,385},{3... | collective-permute-start | bytes 688136 | tf_op jit(solution)/shard_map/ppermute | solution.py:35
  31.5 2.2 %collective-permute-start.4 = (bf16[448,256]{1,0:T(8,128)(2,1)S(1)}, bf16[448,256]{1,0:T(8,128)(2,1)S(1)}, u32[]{:S(2)}, u32[]{:S(2)}) collective-permute-start(bf16[448,256]{1,0:T(8,128)(2,1)S(1)} %get-tuple-element.21), channel_id=1, source_target_pairs={{0,384},{128,0},{256,128},{384,256},{1,385},{129,1},{257,129},{385... | collective-permute-start | bytes 688136 | tf_op jit(solution)/shard_map/ppermute | solution.py:35
  33.8 5.4 %collective-permute-start.6 = (bf16[448,256]{1,0:T(8,128)(2,1)S(1)}, bf16[448,256]{1,0:T(8,128)(2,1)S(1)}, u32[]{:S(2)}, u32[]{:S(2)}) collective-permute-start(bf16[448,256]{1,0:T(8,128)(2,1)S(1)} %copy-done.1), channel_id=1, source_target_pairs={{0,96},{32,64},{64,32},{96,0},{1,97},{33,65},{65,33},{97,1},{2,98}... | collective-permute-start | bytes 688136 | tf_op jit(solution)/shard_map/ppermute | solution.py:215
  39.2 1.5 %collective-permute-done.4.second = bf16[448,256]{1,0:T(8,128)(2,1)S(1)} collective-permute-done((bf16[448,256]{1,0:T(8,128)(2,1)S(1)}, bf16[448,256]{1,0:T(8,128)(2,1)S(1)}, u32[]{:S(2)}, u32[]{:S(2)}) %collective-permute-start.4) | collective-permute-done | bytes 229408 | tf_op jit(solution)/shard_map/ppermute | solution.py:35
  40.7 2.3 %all-to-all-done.feats = bf16[16,152,128]{2,1,0:T(8,128)(2,1)S(1)} async-done(((bf16[16,152,128]{2,1,0:T(8,128)(2,1)}), bf16[16,152,128]{2,1,0:T(8,128)(2,1)S(1)}, u32[]{:S(2)}, u32[]{:S(2)}) %all-to-all-start) | async-done | bytes 622624 | tf_op jit(solution)/shard_map/all_to_all | solution.py:24
  43.0 1.9 %collective-permute-start.5 = (bf16[16,152,128]{2,1,0:T(8,128)(2,1)S(1)}, bf16[16,152,128]{2,1,0:T(8,128)(2,1)S(1)}, u32[]{:S(2)}, u32[]{:S(2)}) collective-permute-start(bf16[16,152,128]{2,1,0:T(8,128)(2,1)S(1)} %all-to-all-done.feats), channel_id=1, source_target_pairs={{0,1},{1,0},{2,3},{3,2},{4,5},{5,4},{6,7},{7,6},{8,9},{9,8},{10,11... | collective-permute-start | bytes 1867784 | tf_op jit(solution)/shard_map/ppermute | solution.py:20
  46.9 2.1 %shard_map.72 = (bf16[4,152,896]{2,1,0:T(8,128)(2,1)}, bf16[152,896]{1,0:T(8,128)(2,1)S(1)}) custom-call(bf16[16,152,128]{2,1,0:T(8,128)(2,1)S(1)} %collective-permute-done.5.feats, f32[640,896]{1,0:T(8,128)S(1)} %shard_map.71.started, bf16[896,256]{1,0:T(8,128)(2,1)S(1)} %shard_map.69.own, bf16[896,256]{1,0:T(8,128)(2,1)S(1)} %collective-permute-done.2.following, ...), custom_call_target="tpu_custom_call" | custom-call | flops 110000000 | bytes 1048576 | tf_op jit(solution)/shard_map/pallas_call | solution.py:222
  49.0 5.8 %all-to-all-start.1 = ((bf16[4,152,896]{2,1,0:T(8,128)(2,1)}), bf16[4,152,896]{2,1,0:T(8,128)(2,1)S(1)}, u32[]{:S(2)}, u32[]{:S(2)}) async-start(bf16[4,152,896]{2,1,0:T(8,128)(2,1)} %get-tuple-element.26), calls=%async_computation.1 | async-start | bytes 2179072 | tf_op jit(solution)/shard_map/all_to_all | solution.py:24
  54.9 2.7 %collective-permute-start.7 = (bf16[2,448,256]{2,1,0:T(8,128)(2,1)S(1)}, bf16[2,448,256]{2,1,0:T(8,128)(2,1)S(1)}, u32[]{:S(2)}, u32[]{:S(2)}) collective-permute-start(bf16[2,448,256]{2,1,0:T(8,128)(2,1)S(1)} %shard_map.74.own), channel_id=1, source_target_pairs={{0,384},{128,0},{256,128},{384,256},{1,385},{129,1},{257,129},{385... | collective-permute-start | bytes 1376264 | tf_op jit(solution)/shard_map/ppermute | solution.py:28
  57.6 4.3 %collective-permute-start.8 = (bf16[2,448,256]{2,1,0:T(8,128)(2,1)S(1)}, bf16[2,448,256]{2,1,0:T(8,128)(2,1)S(1)}, u32[]{:S(2)}, u32[]{:S(2)}) collective-permute-start(bf16[2,448,256]{2,1,0:T(8,128)(2,1)S(1)} %shard_map.74.own), channel_id=1, source_target_pairs={{0,128},{128,256},{256,384},{384,0},{1,129},{129,257},{257,385},{3... | collective-permute-start | bytes 1376264 | tf_op jit(solution)/shard_map/ppermute | solution.py:28
  61.9 7.2 %collective-permute-done.7.following = bf16[2,448,256]{2,1,0:T(8,128)(2,1)S(1)} collective-permute-done((bf16[2,448,256]{2,1,0:T(8,128)(2,1)S(1)}, bf16[2,448,256]{2,1,0:T(8,128)(2,1)S(1)}, u32[]{:S(2)}, u32[]{:S(2)}) %collective-permute-start.7) | collective-permute-done | bytes 458784 | tf_op jit(solution)/shard_map/ppermute | solution.py:28
  71.2 5.5 %collective-permute-start.9 = (bf16[2,224,256]{2,1,0:T(8,128)(2,1)}, bf16[2,224,256]{2,1,0:T(8,128)(2,1)S(1)}, u32[]{:S(2)}, u32[]{:S(2)}) collective-permute-start(bf16[2,224,256]{2,1,0:T(8,128)(2,1)} %get-tuple-element.29), channel_id=1, source_target_pairs={{0,128},{128,256},{256,384},{384,0},{1,129},{129,257},{257,385},{3... | collective-permute-start | bytes 688136 | tf_op jit(solution)/shard_map/ppermute | solution.py:35
  76.8 1.9 %collective-permute-start.10 = (bf16[2,224,256]{2,1,0:T(8,128)(2,1)}, bf16[2,224,256]{2,1,0:T(8,128)(2,1)S(1)}, u32[]{:S(2)}, u32[]{:S(2)}) collective-permute-start(bf16[2,224,256]{2,1,0:T(8,128)(2,1)} %get-tuple-element.30), channel_id=1, source_target_pairs={{0,384},{128,0},{256,128},{384,256},{1,385},{129,1},{257,129},{385... | collective-permute-start | bytes 688136 | tf_op jit(solution)/shard_map/ppermute | solution.py:35
  79.0 7.5 %collective-permute-start.11 = (bf16[152,448]{1,0:T(8,128)(2,1)S(1)}, bf16[152,448]{1,0:T(8,128)(2,1)S(1)}, u32[]{:S(2)}, u32[]{:S(2)}) collective-permute-start(bf16[152,448]{1,0:T(8,128)(2,1)S(1)} %shard_map.73.hidden), channel_id=1, source_target_pairs={{0,32},{32,0},{64,96},{96,64},{1,33},{33,1},{65,97},{97,65},{2,34}... | collective-permute-start | bytes 408584 | tf_op jit(solution)/shard_map/ppermute | solution.py:233
  87.1 6.0 %collective-permute-done.11.hidden = bf16[152,448]{1,0:T(8,128)(2,1)S(1)} collective-permute-done((bf16[152,448]{1,0:T(8,128)(2,1)S(1)}, bf16[152,448]{1,0:T(8,128)(2,1)S(1)}, u32[]{:S(2)}, u32[]{:S(2)}) %collective-permute-start.11) | collective-permute-done | bytes 136224 | tf_op jit(solution)/shard_map/ppermute | solution.py:233
  93.6 1.9 %collective-permute-start.12 = (bf16[8,2,80,256]{3,2,1,0:T(8,128)(2,1)S(1)}, bf16[8,2,80,256]{3,2,1,0:T(8,128)(2,1)S(1)}, u32[]{:S(2)}, u32[]{:S(2)}) collective-permute-start(bf16[8,2,80,256]{3,2,1,0:T(8,128)(2,1)S(1)} %get-tuple-element.37), channel_id=1, source_target_pairs={{0,1},{1,0},{2,3},{3,2},{4,5},{5,4},{6,7},{7,6},{8,9},{9,8},{10,11... | collective-permute-start | bytes 1966088 | tf_op jit(solution)/shard_map/ppermute | solution.py:20
  95.5 2.1 %collective-permute-done.12 = bf16[8,2,80,256]{3,2,1,0:T(8,128)(2,1)S(1)} collective-permute-done((bf16[8,2,80,256]{3,2,1,0:T(8,128)(2,1)S(1)}, bf16[8,2,80,256]{3,2,1,0:T(8,128)(2,1)S(1)}, u32[]{:S(2)}, u32[]{:S(2)}) %collective-permute-start.12) | collective-permute-done | bytes 655392 | tf_op jit(solution)/shard_map/ppermute | solution.py:20
  98.8 27.4 %all_to_all.15 = bf16[16,80,256]{2,1,0:T(8,128)(2,1)S(1)} all-to-all(bf16[16,80,256]{2,1,0:T(8,128)(2,1)S(1)} %copy.20), channel_id=1, replica_groups=mesh['x'=4,'h'=4,'l'=2,'a'=2,'b'=4,'c'=2] {'l','a','b'}, dimensions={0} | all-to-all | bytes 1310720 | tf_op jit(solution)/shard_map/all_to_all | solution.py:24
  126.3 4.8 %collective-permute-start.14 = (bf16[16,256]{1,0:T(8,128)(2,1)S(1)}, bf16[16,256]{1,0:T(8,128)(2,1)S(1)}, u32[]{:S(2)}, u32[]{:S(2)}) collective-permute-start(bf16[16,256]{1,0:T(8,128)(2,1)S(1)} %slice.29), channel_id=1, source_target_pairs={{0,0},{2,2},{4,96},{6,98},{8,128},{10,130},{12,224},{14,226},{16,2... | collective-permute-start | bytes 24584 | tf_op jit(solution)/shard_map/ppermute | solution.py:257
  131.1 5.0 %collective-permute-start.13 = (bf16[4,2,4,256]{3,2,1,0:T(4,128)(2,1)S(1)}, bf16[4,2,4,256]{3,2,1,0:T(4,128)(2,1)S(1)}, u32[]{:S(2)}, u32[]{:S(2)}) collective-permute-start(bf16[4,2,4,256]{3,2,1,0:T(4,128)(2,1)S(1)} %get-tuple-element.38), channel_id=1, source_target_pairs={{0,32},{32,0},{64,96},{96,64},{1,33},{33,1},{65,97},{97,65},{2,34}... | collective-permute-start | bytes 49160 | tf_op jit(solution)/shard_map/ppermute | solution.py:275
  136.2 2.6 %collective-permute-done.14.rows = bf16[16,256]{1,0:T(8,128)(2,1)S(1)} collective-permute-done((bf16[16,256]{1,0:T(8,128)(2,1)S(1)}, bf16[16,256]{1,0:T(8,128)(2,1)S(1)}, u32[]{:S(2)}, u32[]{:S(2)}) %collective-permute-start.14) | collective-permute-done | bytes 8224 | tf_op jit(solution)/shard_map/ppermute | solution.py:257
  (48 shorter events, 11.7 us)
Async XLA Ops:
  0.6 0.9 copy-start
  1.6 0.8 copy-start.4
  2.3 1.0 copy-start.2
  2.3 1.0 copy-start.3
  2.5 10.6 %collective-permute-start = (bf16[152,128]{1,0:T(8,128)(2,1)S(1)}, bf16[152,128]{1,0:T(8,128)(2,1)S(1)}, u32[]{:S(2)}, u32[]{:S(2)}) collective-permute-start(bf16[152,128]{1,0:T(8,128)(2,1)S(1)} %shard_map.68), channel_id=1, source_target_pairs={{0,0},{2,32},{4,64},{6,96},{32,2},{34,34},{36,66},{38,98},{64,4},{... | collective-permute-start | bytes 116744 | tf_op jit(solution)/shard_map/ppermute | solution.py:206
  3.4 24.3 %collective-permute-start.1 = (bf16[896,256]{1,0:T(8,128)(2,1)S(1)}, bf16[896,256]{1,0:T(8,128)(2,1)S(1)}, u32[]{:S(2)}, u32[]{:S(2)}) collective-permute-start(bf16[896,256]{1,0:T(8,128)(2,1)S(1)} %shard_map.69.own), channel_id=1, source_target_pairs={{0,128},{128,256},{256,384},{384,0},{1,129},{129,257},{257,385},{3... | collective-permute-start | bytes 1376264 | tf_op jit(solution)/shard_map/ppermute | solution.py:28
  11.2 16.6 %collective-permute-start.2 = (bf16[896,256]{1,0:T(8,128)(2,1)S(1)}, bf16[896,256]{1,0:T(8,128)(2,1)S(1)}, u32[]{:S(2)}, u32[]{:S(2)}) collective-permute-start(bf16[896,256]{1,0:T(8,128)(2,1)S(1)} %shard_map.69.own), channel_id=1, source_target_pairs={{0,384},{128,0},{256,128},{384,256},{1,385},{129,1},{257,129},{385... | collective-permute-start | bytes 1376264 | tf_op jit(solution)/shard_map/ppermute | solution.py:28
  14.0 28.9 %all-to-all-start = ((bf16[16,152,128]{2,1,0:T(8,128)(2,1)}), bf16[16,152,128]{2,1,0:T(8,128)(2,1)S(1)}, u32[]{:S(2)}, u32[]{:S(2)}) async-start(bf16[16,152,128]{2,1,0:T(8,128)(2,1)} %broadcast_in_dim.3), calls=%async_computation | async-start | bytes 1245184 | tf_op jit(solution)/shard_map/all_to_all | solution.py:24
  27.7 6.1 %copy-start.1 = (bf16[448,256]{1,0:T(8,128)(2,1)S(1)}, bf16[448,256]{1,0:T(8,128)(2,1)}, u32[]{:S(2)}) copy-start(bf16[448,256]{1,0:T(8,128)(2,1)} %own.1) | copy-start | bytes 688132
  27.8 11.4 %collective-permute-start.3 = (bf16[448,256]{1,0:T(8,128)(2,1)S(1)}, bf16[448,256]{1,0:T(8,128)(2,1)S(1)}, u32[]{:S(2)}, u32[]{:S(2)}) collective-permute-start(bf16[448,256]{1,0:T(8,128)(2,1)S(1)} %get-tuple-element.20), channel_id=1, source_target_pairs={{0,128},{128,256},{256,384},{384,0},{1,129},{129,257},{257,385},{3... | collective-permute-start | bytes 688136 | tf_op jit(solution)/shard_map/ppermute | solution.py:35
  31.5 9.1 %collective-permute-start.4 = (bf16[448,256]{1,0:T(8,128)(2,1)S(1)}, bf16[448,256]{1,0:T(8,128)(2,1)S(1)}, u32[]{:S(2)}, u32[]{:S(2)}) collective-permute-start(bf16[448,256]{1,0:T(8,128)(2,1)S(1)} %get-tuple-element.21), channel_id=1, source_target_pairs={{0,384},{128,0},{256,128},{384,256},{1,385},{129,1},{257,129},{385... | collective-permute-start | bytes 688136 | tf_op jit(solution)/shard_map/ppermute | solution.py:35
  33.8 13.1 %collective-permute-start.6 = (bf16[448,256]{1,0:T(8,128)(2,1)S(1)}, bf16[448,256]{1,0:T(8,128)(2,1)S(1)}, u32[]{:S(2)}, u32[]{:S(2)}) collective-permute-start(bf16[448,256]{1,0:T(8,128)(2,1)S(1)} %copy-done.1), channel_id=1, source_target_pairs={{0,96},{32,64},{64,32},{96,0},{1,97},{33,65},{65,33},{97,1},{2,98}... | collective-permute-start | bytes 688136 | tf_op jit(solution)/shard_map/ppermute | solution.py:215
  43.0 3.9 %collective-permute-start.5 = (bf16[16,152,128]{2,1,0:T(8,128)(2,1)S(1)}, bf16[16,152,128]{2,1,0:T(8,128)(2,1)S(1)}, u32[]{:S(2)}, u32[]{:S(2)}) collective-permute-start(bf16[16,152,128]{2,1,0:T(8,128)(2,1)S(1)} %all-to-all-done.feats), channel_id=1, source_target_pairs={{0,1},{1,0},{2,3},{3,2},{4,5},{5,4},{6,7},{7,6},{8,9},{9,8},{10,11... | collective-permute-start | bytes 1867784 | tf_op jit(solution)/shard_map/ppermute | solution.py:20
  49.0 29.7 %all-to-all-start.1 = ((bf16[4,152,896]{2,1,0:T(8,128)(2,1)}), bf16[4,152,896]{2,1,0:T(8,128)(2,1)S(1)}, u32[]{:S(2)}, u32[]{:S(2)}) async-start(bf16[4,152,896]{2,1,0:T(8,128)(2,1)} %get-tuple-element.26), calls=%async_computation.1 | async-start | bytes 2179072 | tf_op jit(solution)/shard_map/all_to_all | solution.py:24
  54.9 14.3 %collective-permute-start.7 = (bf16[2,448,256]{2,1,0:T(8,128)(2,1)S(1)}, bf16[2,448,256]{2,1,0:T(8,128)(2,1)S(1)}, u32[]{:S(2)}, u32[]{:S(2)}) collective-permute-start(bf16[2,448,256]{2,1,0:T(8,128)(2,1)S(1)} %shard_map.74.own), channel_id=1, source_target_pairs={{0,384},{128,0},{256,128},{384,256},{1,385},{129,1},{257,129},{385... | collective-permute-start | bytes 1376264 | tf_op jit(solution)/shard_map/ppermute | solution.py:28
  57.6 12.8 %collective-permute-start.8 = (bf16[2,448,256]{2,1,0:T(8,128)(2,1)S(1)}, bf16[2,448,256]{2,1,0:T(8,128)(2,1)S(1)}, u32[]{:S(2)}, u32[]{:S(2)}) collective-permute-start(bf16[2,448,256]{2,1,0:T(8,128)(2,1)S(1)} %shard_map.74.own), channel_id=1, source_target_pairs={{0,128},{128,256},{256,384},{384,0},{1,129},{129,257},{257,385},{3... | collective-permute-start | bytes 1376264 | tf_op jit(solution)/shard_map/ppermute | solution.py:28
  71.2 15.3 %collective-permute-start.9 = (bf16[2,224,256]{2,1,0:T(8,128)(2,1)}, bf16[2,224,256]{2,1,0:T(8,128)(2,1)S(1)}, u32[]{:S(2)}, u32[]{:S(2)}) collective-permute-start(bf16[2,224,256]{2,1,0:T(8,128)(2,1)} %get-tuple-element.29), channel_id=1, source_target_pairs={{0,128},{128,256},{256,384},{384,0},{1,129},{129,257},{257,385},{3... | collective-permute-start | bytes 688136 | tf_op jit(solution)/shard_map/ppermute | solution.py:35
  76.8 9.8 %collective-permute-start.10 = (bf16[2,224,256]{2,1,0:T(8,128)(2,1)}, bf16[2,224,256]{2,1,0:T(8,128)(2,1)S(1)}, u32[]{:S(2)}, u32[]{:S(2)}) collective-permute-start(bf16[2,224,256]{2,1,0:T(8,128)(2,1)} %get-tuple-element.30), channel_id=1, source_target_pairs={{0,384},{128,0},{256,128},{384,256},{1,385},{129,1},{257,129},{385... | collective-permute-start | bytes 688136 | tf_op jit(solution)/shard_map/ppermute | solution.py:35
  79.0 14.0 %collective-permute-start.11 = (bf16[152,448]{1,0:T(8,128)(2,1)S(1)}, bf16[152,448]{1,0:T(8,128)(2,1)S(1)}, u32[]{:S(2)}, u32[]{:S(2)}) collective-permute-start(bf16[152,448]{1,0:T(8,128)(2,1)S(1)} %shard_map.73.hidden), channel_id=1, source_target_pairs={{0,32},{32,0},{64,96},{96,64},{1,33},{33,1},{65,97},{97,65},{2,34}... | collective-permute-start | bytes 408584 | tf_op jit(solution)/shard_map/ppermute | solution.py:233
  93.6 4.0 %collective-permute-start.12 = (bf16[8,2,80,256]{3,2,1,0:T(8,128)(2,1)S(1)}, bf16[8,2,80,256]{3,2,1,0:T(8,128)(2,1)S(1)}, u32[]{:S(2)}, u32[]{:S(2)}) collective-permute-start(bf16[8,2,80,256]{3,2,1,0:T(8,128)(2,1)S(1)} %get-tuple-element.37), channel_id=1, source_target_pairs={{0,1},{1,0},{2,3},{3,2},{4,5},{5,4},{6,7},{7,6},{8,9},{9,8},{10,11... | collective-permute-start | bytes 1966088 | tf_op jit(solution)/shard_map/ppermute | solution.py:20
  126.3 12.5 %collective-permute-start.14 = (bf16[16,256]{1,0:T(8,128)(2,1)S(1)}, bf16[16,256]{1,0:T(8,128)(2,1)S(1)}, u32[]{:S(2)}, u32[]{:S(2)}) collective-permute-start(bf16[16,256]{1,0:T(8,128)(2,1)S(1)} %slice.29), channel_id=1, source_target_pairs={{0,0},{2,2},{4,96},{6,98},{8,128},{10,130},{12,224},{14,226},{16,2... | collective-permute-start | bytes 24584 | tf_op jit(solution)/shard_map/ppermute | solution.py:257
  131.1 8.2 %collective-permute-start.13 = (bf16[4,2,4,256]{3,2,1,0:T(4,128)(2,1)S(1)}, bf16[4,2,4,256]{3,2,1,0:T(4,128)(2,1)S(1)}, u32[]{:S(2)}, u32[]{:S(2)}) collective-permute-start(bf16[4,2,4,256]{3,2,1,0:T(4,128)(2,1)S(1)} %get-tuple-element.38), channel_id=1, source_target_pairs={{0,32},{32,0},{64,96},{96,64},{1,33},{33,1},{65,97},{97,65},{2,34}... | collective-permute-start | bytes 49160 | tf_op jit(solution)/shard_map/ppermute | solution.py:275

commit v7 on v6

--- a/solution.py
+++ b/solution.py
@@ -12,7 +12,7 @@
 LZ = ("l", "a", "b")
 UP = [(i, (i + 1) % 4) for i in range(4)]
 DOWN = [(i, (i + 3) % 4) for i in range(4)]
-VMEM = 16 * 2**20
+VMEM = 10 * 2**20
 HINTS = (4.95, 0.1, 1, 0.1, 5, 8, 5, 5)
 
 

time: 142 us -> 142 us (level)
  no operation moved by 1% of the time
where the time goes in v7:
time: 142 us; the launch traced here: 140 us
  starting transfers between devices  76.9 us (54%)
  blocking collectives  27.4 us (19%)
  waiting for transfers between devices  24.1 us (17%)
  Pallas kernels  6.61 us (5%)
  local copies, waits for them, and re-layouts  3.63 us (3%)
    all_to_all x1, blocking collectives, exchange(): return lax.all_to_all(blocks, axes, split_axis=0, concat_axis=0, tiled=True)  27.4 us
    all_to_all x2, starting transfers between devices, exchange(): return lax.all_to_all(blocks, axes, split_axis=0, concat_axis=0, tiled=True)  19.5 us
    ppermute x4, starting transfers between devices, near(): return (lax.ppermute(value, axis, DOWN), lax.ppermute(value, axis, UP))  16.7 us
    ppermute x4, starting transfers between devices, far(): return (lax.ppermute(up, axis, UP), lax.ppermute(down, axis, DOWN))  13.4 us
    ppermute x4, waiting for transfers between devices, near(): return (lax.ppermute(value, axis, DOWN), lax.ppermute(value, axis, UP))  8.48 us
    ppermute x1, starting transfers between devices, local(): partner = lax.ppermute(hidden, 'h', beside)  7.48 us
    ppermute x1, waiting for transfers between devices, local(): partner = lax.ppermute(hidden, 'h', beside)  6 us
    ppermute x1, starting transfers between devices, local(): opposite = lax.ppermute(down_weight, 'h', [(i, 3 - i) for i in range(4)])  5.36 us
  transfers between devices with their start and end apart: 17, of which 9 were waited for; matrix products, arithmetic and copies ran while one was open for 1% of the time, Pallas kernels for 2%

profile of v7, /device:TPU:6, one launch (start us, length us, event | category | flops | bytes accessed | tf_op | source)
XLA Modules:
  0.0 139.9 jit_solution(7097560533802126768)
XLA Ops:
  3.4 7.8 %collective-permute-start.1 = (bf16[896,256]{1,0:T(8,128)(2,1)S(1)}, bf16[896,256]{1,0:T(8,128)(2,1)S(1)}, u32[]{:S(2)}, u32[]{:S(2)}) collective-permute-start(bf16[896,256]{1,0:T(8,128)(2,1)S(1)} %shard_map.69.own), channel_id=1, source_target_pairs={{0,128},{128,256},{256,384},{384,0},{1,129},{129,257},{257,385},{3... | collective-permute-start | bytes 1376264 | tf_op jit(solution)/shard_map/ppermute | solution.py:28
  11.2 1.9 %collective-permute-start.2 = (bf16[896,256]{1,0:T(8,128)(2,1)S(1)}, bf16[896,256]{1,0:T(8,128)(2,1)S(1)}, u32[]{:S(2)}, u32[]{:S(2)}) collective-permute-start(bf16[896,256]{1,0:T(8,128)(2,1)S(1)} %shard_map.69.own), channel_id=1, source_target_pairs={{0,384},{128,0},{256,128},{384,256},{1,385},{129,1},{257,129},{385... | collective-permute-start | bytes 1376264 | tf_op jit(solution)/shard_map/ppermute | solution.py:28
  14.0 13.7 %all-to-all-start = ((bf16[16,152,128]{2,1,0:T(8,128)(2,1)}), bf16[16,152,128]{2,1,0:T(8,128)(2,1)S(1)}, u32[]{:S(2)}, u32[]{:S(2)}) async-start(bf16[16,152,128]{2,1,0:T(8,128)(2,1)} %broadcast_in_dim.3), calls=%async_computation | async-start | bytes 1245184 | tf_op jit(solution)/shard_map/all_to_all | solution.py:24
  27.8 3.7 %collective-permute-start.3 = (bf16[448,256]{1,0:T(8,128)(2,1)S(1)}, bf16[448,256]{1,0:T(8,128)(2,1)S(1)}, u32[]{:S(2)}, u32[]{:S(2)}) collective-permute-start(bf16[448,256]{1,0:T(8,128)(2,1)S(1)} %get-tuple-element.20), channel_id=1, source_target_pairs={{0,128},{128,256},{256,384},{384,0},{1,129},{129,257},{257,385},{3... | collective-permute-start | bytes 688136 | tf_op jit(solution)/shard_map/ppermute | solution.py:35
  31.5 2.2 %collective-permute-start.4 = (bf16[448,256]{1,0:T(8,128)(2,1)S(1)}, bf16[448,256]{1,0:T(8,128)(2,1)S(1)}, u32[]{:S(2)}, u32[]{:S(2)}) collective-permute-start(bf16[448,256]{1,0:T(8,128)(2,1)S(1)} %get-tuple-element.21), channel_id=1, source_target_pairs={{0,384},{128,0},{256,128},{384,256},{1,385},{129,1},{257,129},{385... | collective-permute-start | bytes 688136 | tf_op jit(solution)/shard_map/ppermute | solution.py:35
  33.8 5.4 %collective-permute-start.6 = (bf16[448,256]{1,0:T(8,128)(2,1)S(1)}, bf16[448,256]{1,0:T(8,128)(2,1)S(1)}, u32[]{:S(2)}, u32[]{:S(2)}) collective-permute-start(bf16[448,256]{1,0:T(8,128)(2,1)S(1)} %copy-done.1), channel_id=1, source_target_pairs={{0,96},{32,64},{64,32},{96,0},{1,97},{33,65},{65,33},{97,1},{2,98}... | collective-permute-start | bytes 688136 | tf_op jit(solution)/shard_map/ppermute | solution.py:215
  39.2 1.5 %collective-permute-done.4.second = bf16[448,256]{1,0:T(8,128)(2,1)S(1)} collective-permute-done((bf16[448,256]{1,0:T(8,128)(2,1)S(1)}, bf16[448,256]{1,0:T(8,128)(2,1)S(1)}, u32[]{:S(2)}, u32[]{:S(2)}) %collective-permute-start.4) | collective-permute-done | bytes 229408 | tf_op jit(solution)/shard_map/ppermute | solution.py:35
  40.7 2.3 %all-to-all-done.feats = bf16[16,152,128]{2,1,0:T(8,128)(2,1)S(1)} async-done(((bf16[16,152,128]{2,1,0:T(8,128)(2,1)}), bf16[16,152,128]{2,1,0:T(8,128)(2,1)S(1)}, u32[]{:S(2)}, u32[]{:S(2)}) %all-to-all-start) | async-done | bytes 622624 | tf_op jit(solution)/shard_map/all_to_all | solution.py:24
  43.0 1.9 %collective-permute-start.5 = (bf16[16,152,128]{2,1,0:T(8,128)(2,1)S(1)}, bf16[16,152,128]{2,1,0:T(8,128)(2,1)S(1)}, u32[]{:S(2)}, u32[]{:S(2)}) collective-permute-start(bf16[16,152,128]{2,1,0:T(8,128)(2,1)S(1)} %all-to-all-done.feats), channel_id=1, source_target_pairs={{0,1},{1,0},{2,3},{3,2},{4,5},{5,4},{6,7},{7,6},{8,9},{9,8},{10,11... | collective-permute-start | bytes 1867784 | tf_op jit(solution)/shard_map/ppermute | solution.py:20
  46.9 2.1 %shard_map.72 = (bf16[4,152,896]{2,1,0:T(8,128)(2,1)}, bf16[152,896]{1,0:T(8,128)(2,1)S(1)}) custom-call(bf16[16,152,128]{2,1,0:T(8,128)(2,1)S(1)} %collective-permute-done.5.feats, f32[640,896]{1,0:T(8,128)S(1)} %shard_map.71.started, bf16[896,256]{1,0:T(8,128)(2,1)S(1)} %shard_map.69.own, bf16[896,256]{1,0:T(8,128)(2,1)S(1)} %collective-permute-done.2.following, ...), custom_call_target="tpu_custom_call" | custom-call | flops 110000000 | bytes 1048576 | tf_op jit(solution)/shard_map/pallas_call | solution.py:222
  49.0 5.8 %all-to-all-start.1 = ((bf16[4,152,896]{2,1,0:T(8,128)(2,1)}), bf16[4,152,896]{2,1,0:T(8,128)(2,1)S(1)}, u32[]{:S(2)}, u32[]{:S(2)}) async-start(bf16[4,152,896]{2,1,0:T(8,128)(2,1)} %get-tuple-element.26), calls=%async_computation.1 | async-start | bytes 2179072 | tf_op jit(solution)/shard_map/all_to_all | solution.py:24
  54.9 2.7 %collective-permute-start.7 = (bf16[2,448,256]{2,1,0:T(8,128)(2,1)S(1)}, bf16[2,448,256]{2,1,0:T(8,128)(2,1)S(1)}, u32[]{:S(2)}, u32[]{:S(2)}) collective-permute-start(bf16[2,448,256]{2,1,0:T(8,128)(2,1)S(1)} %shard_map.74.own), channel_id=1, source_target_pairs={{0,384},{128,0},{256,128},{384,256},{1,385},{129,1},{257,129},{385... | collective-permute-start | bytes 1376264 | tf_op jit(solution)/shard_map/ppermute | solution.py:28
  57.6 4.3 %collective-permute-start.8 = (bf16[2,448,256]{2,1,0:T(8,128)(2,1)S(1)}, bf16[2,448,256]{2,1,0:T(8,128)(2,1)S(1)}, u32[]{:S(2)}, u32[]{:S(2)}) collective-permute-start(bf16[2,448,256]{2,1,0:T(8,128)(2,1)S(1)} %shard_map.74.own), channel_id=1, source_target_pairs={{0,128},{128,256},{256,384},{384,0},{1,129},{129,257},{257,385},{3... | collective-permute-start | bytes 1376264 | tf_op jit(solution)/shard_map/ppermute | solution.py:28
  61.9 7.2 %collective-permute-done.7.following = bf16[2,448,256]{2,1,0:T(8,128)(2,1)S(1)} collective-permute-done((bf16[2,448,256]{2,1,0:T(8,128)(2,1)S(1)}, bf16[2,448,256]{2,1,0:T(8,128)(2,1)S(1)}, u32[]{:S(2)}, u32[]{:S(2)}) %collective-permute-start.7) | collective-permute-done | bytes 458784 | tf_op jit(solution)/shard_map/ppermute | solution.py:28
  71.2 5.5 %collective-permute-start.9 = (bf16[2,224,256]{2,1,0:T(8,128)(2,1)}, bf16[2,224,256]{2,1,0:T(8,128)(2,1)S(1)}, u32[]{:S(2)}, u32[]{:S(2)}) collective-permute-start(bf16[2,224,256]{2,1,0:T(8,128)(2,1)} %get-tuple-element.29), channel_id=1, source_target_pairs={{0,128},{128,256},{256,384},{384,0},{1,129},{129,257},{257,385},{3... | collective-permute-start | bytes 688136 | tf_op jit(solution)/shard_map/ppermute | solution.py:35
  76.8 1.9 %collective-permute-start.10 = (bf16[2,224,256]{2,1,0:T(8,128)(2,1)}, bf16[2,224,256]{2,1,0:T(8,128)(2,1)S(1)}, u32[]{:S(2)}, u32[]{:S(2)}) collective-permute-start(bf16[2,224,256]{2,1,0:T(8,128)(2,1)} %get-tuple-element.30), channel_id=1, source_target_pairs={{0,384},{128,0},{256,128},{384,256},{1,385},{129,1},{257,129},{385... | collective-permute-start | bytes 688136 | tf_op jit(solution)/shard_map/ppermute | solution.py:35
  79.0 7.5 %collective-permute-start.11 = (bf16[152,448]{1,0:T(8,128)(2,1)S(1)}, bf16[152,448]{1,0:T(8,128)(2,1)S(1)}, u32[]{:S(2)}, u32[]{:S(2)}) collective-permute-start(bf16[152,448]{1,0:T(8,128)(2,1)S(1)} %shard_map.73.hidden), channel_id=1, source_target_pairs={{0,32},{32,0},{64,96},{96,64},{1,33},{33,1},{65,97},{97,65},{2,34}... | collective-permute-start | bytes 408584 | tf_op jit(solution)/shard_map/ppermute | solution.py:233
  87.1 6.0 %collective-permute-done.11.hidden = bf16[152,448]{1,0:T(8,128)(2,1)S(1)} collective-permute-done((bf16[152,448]{1,0:T(8,128)(2,1)S(1)}, bf16[152,448]{1,0:T(8,128)(2,1)S(1)}, u32[]{:S(2)}, u32[]{:S(2)}) %collective-permute-start.11) | collective-permute-done | bytes 136224 | tf_op jit(solution)/shard_map/ppermute | solution.py:233
  93.6 1.9 %collective-permute-start.12 = (bf16[8,2,80,256]{3,2,1,0:T(8,128)(2,1)S(1)}, bf16[8,2,80,256]{3,2,1,0:T(8,128)(2,1)S(1)}, u32[]{:S(2)}, u32[]{:S(2)}) collective-permute-start(bf16[8,2,80,256]{3,2,1,0:T(8,128)(2,1)S(1)} %get-tuple-element.37), channel_id=1, source_target_pairs={{0,1},{1,0},{2,3},{3,2},{4,5},{5,4},{6,7},{7,6},{8,9},{9,8},{10,11... | collective-permute-start | bytes 1966088 | tf_op jit(solution)/shard_map/ppermute | solution.py:20
  95.5 2.1 %collective-permute-done.12 = bf16[8,2,80,256]{3,2,1,0:T(8,128)(2,1)S(1)} collective-permute-done((bf16[8,2,80,256]{3,2,1,0:T(8,128)(2,1)S(1)}, bf16[8,2,80,256]{3,2,1,0:T(8,128)(2,1)S(1)}, u32[]{:S(2)}, u32[]{:S(2)}) %collective-permute-start.12) | collective-permute-done | bytes 655392 | tf_op jit(solution)/shard_map/ppermute | solution.py:20
  98.8 27.4 %all_to_all.15 = bf16[16,80,256]{2,1,0:T(8,128)(2,1)S(1)} all-to-all(bf16[16,80,256]{2,1,0:T(8,128)(2,1)S(1)} %copy.20), channel_id=1, replica_groups=mesh['x'=4,'h'=4,'l'=2,'a'=2,'b'=4,'c'=2] {'l','a','b'}, dimensions={0} | all-to-all | bytes 1310720 | tf_op jit(solution)/shard_map/all_to_all | solution.py:24
  126.3 4.8 %collective-permute-start.14 = (bf16[16,256]{1,0:T(8,128)(2,1)S(1)}, bf16[16,256]{1,0:T(8,128)(2,1)S(1)}, u32[]{:S(2)}, u32[]{:S(2)}) collective-permute-start(bf16[16,256]{1,0:T(8,128)(2,1)S(1)} %slice.29), channel_id=1, source_target_pairs={{0,0},{2,2},{4,96},{6,98},{8,128},{10,130},{12,224},{14,226},{16,2... | collective-permute-start | bytes 24584 | tf_op jit(solution)/shard_map/ppermute | solution.py:257
  131.1 5.0 %collective-permute-start.13 = (bf16[4,2,4,256]{3,2,1,0:T(4,128)(2,1)S(1)}, bf16[4,2,4,256]{3,2,1,0:T(4,128)(2,1)S(1)}, u32[]{:S(2)}, u32[]{:S(2)}) collective-permute-start(bf16[4,2,4,256]{3,2,1,0:T(4,128)(2,1)S(1)} %get-tuple-element.38), channel_id=1, source_target_pairs={{0,32},{32,0},{64,96},{96,64},{1,33},{33,1},{65,97},{97,65},{2,34}... | collective-permute-start | bytes 49160 | tf_op jit(solution)/shard_map/ppermute | solution.py:275
  136.1 2.6 %collective-permute-done.14.rows = bf16[16,256]{1,0:T(8,128)(2,1)S(1)} collective-permute-done((bf16[16,256]{1,0:T(8,128)(2,1)S(1)}, bf16[16,256]{1,0:T(8,128)(2,1)S(1)}, u32[]{:S(2)}, u32[]{:S(2)}) %collective-permute-start.14) | collective-permute-done | bytes 8224 | tf_op jit(solution)/shard_map/ppermute | solution.py:257
  (48 shorter events, 11.7 us)
Async XLA Ops:
  0.6 0.9 copy-start
  1.6 0.8 copy-start.4
  2.3 1.0 copy-start.2
  2.3 1.0 copy-start.3
  2.5 10.6 %collective-permute-start = (bf16[152,128]{1,0:T(8,128)(2,1)S(1)}, bf16[152,128]{1,0:T(8,128)(2,1)S(1)}, u32[]{:S(2)}, u32[]{:S(2)}) collective-permute-start(bf16[152,128]{1,0:T(8,128)(2,1)S(1)} %shard_map.68), channel_id=1, source_target_pairs={{0,0},{2,32},{4,64},{6,96},{32,2},{34,34},{36,66},{38,98},{64,4},{... | collective-permute-start | bytes 116744 | tf_op jit(solution)/shard_map/ppermute | solution.py:206
  3.4 24.3 %collective-permute-start.1 = (bf16[896,256]{1,0:T(8,128)(2,1)S(1)}, bf16[896,256]{1,0:T(8,128)(2,1)S(1)}, u32[]{:S(2)}, u32[]{:S(2)}) collective-permute-start(bf16[896,256]{1,0:T(8,128)(2,1)S(1)} %shard_map.69.own), channel_id=1, source_target_pairs={{0,128},{128,256},{256,384},{384,0},{1,129},{129,257},{257,385},{3... | collective-permute-start | bytes 1376264 | tf_op jit(solution)/shard_map/ppermute | solution.py:28
  11.2 16.6 %collective-permute-start.2 = (bf16[896,256]{1,0:T(8,128)(2,1)S(1)}, bf16[896,256]{1,0:T(8,128)(2,1)S(1)}, u32[]{:S(2)}, u32[]{:S(2)}) collective-permute-start(bf16[896,256]{1,0:T(8,128)(2,1)S(1)} %shard_map.69.own), channel_id=1, source_target_pairs={{0,384},{128,0},{256,128},{384,256},{1,385},{129,1},{257,129},{385... | collective-permute-start | bytes 1376264 | tf_op jit(solution)/shard_map/ppermute | solution.py:28
  14.0 28.9 %all-to-all-start = ((bf16[16,152,128]{2,1,0:T(8,128)(2,1)}), bf16[16,152,128]{2,1,0:T(8,128)(2,1)S(1)}, u32[]{:S(2)}, u32[]{:S(2)}) async-start(bf16[16,152,128]{2,1,0:T(8,128)(2,1)} %broadcast_in_dim.3), calls=%async_computation | async-start | bytes 1245184 | tf_op jit(solution)/shard_map/all_to_all | solution.py:24
  27.7 6.1 %copy-start.1 = (bf16[448,256]{1,0:T(8,128)(2,1)S(1)}, bf16[448,256]{1,0:T(8,128)(2,1)}, u32[]{:S(2)}) copy-start(bf16[448,256]{1,0:T(8,128)(2,1)} %own.1) | copy-start | bytes 688132
  27.8 11.4 %collective-permute-start.3 = (bf16[448,256]{1,0:T(8,128)(2,1)S(1)}, bf16[448,256]{1,0:T(8,128)(2,1)S(1)}, u32[]{:S(2)}, u32[]{:S(2)}) collective-permute-start(bf16[448,256]{1,0:T(8,128)(2,1)S(1)} %get-tuple-element.20), channel_id=1, source_target_pairs={{0,128},{128,256},{256,384},{384,0},{1,129},{129,257},{257,385},{3... | collective-permute-start | bytes 688136 | tf_op jit(solution)/shard_map/ppermute | solution.py:35
  31.5 9.1 %collective-permute-start.4 = (bf16[448,256]{1,0:T(8,128)(2,1)S(1)}, bf16[448,256]{1,0:T(8,128)(2,1)S(1)}, u32[]{:S(2)}, u32[]{:S(2)}) collective-permute-start(bf16[448,256]{1,0:T(8,128)(2,1)S(1)} %get-tuple-element.21), channel_id=1, source_target_pairs={{0,384},{128,0},{256,128},{384,256},{1,385},{129,1},{257,129},{385... | collective-permute-start | bytes 688136 | tf_op jit(solution)/shard_map/ppermute | solution.py:35
  33.8 13.1 %collective-permute-start.6 = (bf16[448,256]{1,0:T(8,128)(2,1)S(1)}, bf16[448,256]{1,0:T(8,128)(2,1)S(1)}, u32[]{:S(2)}, u32[]{:S(2)}) collective-permute-start(bf16[448,256]{1,0:T(8,128)(2,1)S(1)} %copy-done.1), channel_id=1, source_target_pairs={{0,96},{32,64},{64,32},{96,0},{1,97},{33,65},{65,33},{97,1},{2,98}... | collective-permute-start | bytes 688136 | tf_op jit(solution)/shard_map/ppermute | solution.py:215
  43.0 3.9 %collective-permute-start.5 = (bf16[16,152,128]{2,1,0:T(8,128)(2,1)S(1)}, bf16[16,152,128]{2,1,0:T(8,128)(2,1)S(1)}, u32[]{:S(2)}, u32[]{:S(2)}) collective-permute-start(bf16[16,152,128]{2,1,0:T(8,128)(2,1)S(1)} %all-to-all-done.feats), channel_id=1, source_target_pairs={{0,1},{1,0},{2,3},{3,2},{4,5},{5,4},{6,7},{7,6},{8,9},{9,8},{10,11... | collective-permute-start | bytes 1867784 | tf_op jit(solution)/shard_map/ppermute | solution.py:20
  49.0 29.7 %all-to-all-start.1 = ((bf16[4,152,896]{2,1,0:T(8,128)(2,1)}), bf16[4,152,896]{2,1,0:T(8,128)(2,1)S(1)}, u32[]{:S(2)}, u32[]{:S(2)}) async-start(bf16[4,152,896]{2,1,0:T(8,128)(2,1)} %get-tuple-element.26), calls=%async_computation.1 | async-start | bytes 2179072 | tf_op jit(solution)/shard_map/all_to_all | solution.py:24
  54.9 14.3 %collective-permute-start.7 = (bf16[2,448,256]{2,1,0:T(8,128)(2,1)S(1)}, bf16[2,448,256]{2,1,0:T(8,128)(2,1)S(1)}, u32[]{:S(2)}, u32[]{:S(2)}) collective-permute-start(bf16[2,448,256]{2,1,0:T(8,128)(2,1)S(1)} %shard_map.74.own), channel_id=1, source_target_pairs={{0,384},{128,0},{256,128},{384,256},{1,385},{129,1},{257,129},{385... | collective-permute-start | bytes 1376264 | tf_op jit(solution)/shard_map/ppermute | solution.py:28
  57.6 12.8 %collective-permute-start.8 = (bf16[2,448,256]{2,1,0:T(8,128)(2,1)S(1)}, bf16[2,448,256]{2,1,0:T(8,128)(2,1)S(1)}, u32[]{:S(2)}, u32[]{:S(2)}) collective-permute-start(bf16[2,448,256]{2,1,0:T(8,128)(2,1)S(1)} %shard_map.74.own), channel_id=1, source_target_pairs={{0,128},{128,256},{256,384},{384,0},{1,129},{129,257},{257,385},{3... | collective-permute-start | bytes 1376264 | tf_op jit(solution)/shard_map/ppermute | solution.py:28
  71.2 15.3 %collective-permute-start.9 = (bf16[2,224,256]{2,1,0:T(8,128)(2,1)}, bf16[2,224,256]{2,1,0:T(8,128)(2,1)S(1)}, u32[]{:S(2)}, u32[]{:S(2)}) collective-permute-start(bf16[2,224,256]{2,1,0:T(8,128)(2,1)} %get-tuple-element.29), channel_id=1, source_target_pairs={{0,128},{128,256},{256,384},{384,0},{1,129},{129,257},{257,385},{3... | collective-permute-start | bytes 688136 | tf_op jit(solution)/shard_map/ppermute | solution.py:35
  76.8 9.8 %collective-permute-start.10 = (bf16[2,224,256]{2,1,0:T(8,128)(2,1)}, bf16[2,224,256]{2,1,0:T(8,128)(2,1)S(1)}, u32[]{:S(2)}, u32[]{:S(2)}) collective-permute-start(bf16[2,224,256]{2,1,0:T(8,128)(2,1)} %get-tuple-element.30), channel_id=1, source_target_pairs={{0,384},{128,0},{256,128},{384,256},{1,385},{129,1},{257,129},{385... | collective-permute-start | bytes 688136 | tf_op jit(solution)/shard_map/ppermute | solution.py:35
  79.0 14.0 %collective-permute-start.11 = (bf16[152,448]{1,0:T(8,128)(2,1)S(1)}, bf16[152,448]{1,0:T(8,128)(2,1)S(1)}, u32[]{:S(2)}, u32[]{:S(2)}) collective-permute-start(bf16[152,448]{1,0:T(8,128)(2,1)S(1)} %shard_map.73.hidden), channel_id=1, source_target_pairs={{0,32},{32,0},{64,96},{96,64},{1,33},{33,1},{65,97},{97,65},{2,34}... | collective-permute-start | bytes 408584 | tf_op jit(solution)/shard_map/ppermute | solution.py:233
  93.6 4.0 %collective-permute-start.12 = (bf16[8,2,80,256]{3,2,1,0:T(8,128)(2,1)S(1)}, bf16[8,2,80,256]{3,2,1,0:T(8,128)(2,1)S(1)}, u32[]{:S(2)}, u32[]{:S(2)}) collective-permute-start(bf16[8,2,80,256]{3,2,1,0:T(8,128)(2,1)S(1)} %get-tuple-element.37), channel_id=1, source_target_pairs={{0,1},{1,0},{2,3},{3,2},{4,5},{5,4},{6,7},{7,6},{8,9},{9,8},{10,11... | collective-permute-start | bytes 1966088 | tf_op jit(solution)/shard_map/ppermute | solution.py:20
  126.3 12.5 %collective-permute-start.14 = (bf16[16,256]{1,0:T(8,128)(2,1)S(1)}, bf16[16,256]{1,0:T(8,128)(2,1)S(1)}, u32[]{:S(2)}, u32[]{:S(2)}) collective-permute-start(bf16[16,256]{1,0:T(8,128)(2,1)S(1)} %slice.29), channel_id=1, source_target_pairs={{0,0},{2,2},{4,96},{6,98},{8,128},{10,130},{12,224},{14,226},{16,2... | collective-permute-start | bytes 24584 | tf_op jit(solution)/shard_map/ppermute | solution.py:257
  131.1 8.2 %collective-permute-start.13 = (bf16[4,2,4,256]{3,2,1,0:T(4,128)(2,1)S(1)}, bf16[4,2,4,256]{3,2,1,0:T(4,128)(2,1)S(1)}, u32[]{:S(2)}, u32[]{:S(2)}) collective-permute-start(bf16[4,2,4,256]{3,2,1,0:T(4,128)(2,1)S(1)} %get-tuple-element.38), channel_id=1, source_target_pairs={{0,32},{32,0},{64,96},{96,64},{1,33},{33,1},{65,97},{97,65},{2,34}... | collective-permute-start | bytes 49160 | tf_op jit(solution)/shard_map/ppermute | solution.py:275

commit v8 on v7

--- a/solution.py
+++ b/solution.py
@@ -13,7 +13,7 @@
 UP = [(i, (i + 1) % 4) for i in range(4)]
 DOWN = [(i, (i + 3) % 4) for i in range(4)]
 VMEM = 10 * 2**20
-HINTS = (4.95, 0.1, 1, 0.1, 5, 8, 5, 5)
+HINTS = (4.95, 0.1, 1, 10, 5, 8, 5, 5)
 
 
 def swap_cores(value):
@@ -218,7 +218,6 @@
 
     weights = (own, own_near[0], *own_far, own_near[1])
     started = call(gate_up_start_kernel, jax.ShapeDtypeStruct((4 * total, 2 * ff), F32), HINTS[5])(feats, *weights)
-    other, opposite = lax.optimization_barrier((other, opposite))
     partial, residue = call(
         gate_up_kernel,
         (

time: 142 us -> 139 us (0.979)
  blocking collectives: 27.4 us -> 24.5 us
  starting transfers between devices: 76.9 us -> 75 us
  waiting for transfers between devices: 24.1 us -> 26 us
    all_to_all x1, blocking collectives: 27.4 us -> 24.5 us  [exchange(): return lax.all_to_all(blocks, axes, split_axis=0, concat_axis=0, tiled=True)]
  transfers between devices with their start and end apart: 17 -> 17, of which waited for: 9 -> 8; matrix products, arithmetic and copies ran while one was open for 1% -> 1% of each run, Pallas kernels for 2% -> 4%
where the time goes in v8:
time: 139 us; the launch traced here: 137 us
  starting transfers between devices  75 us (54%)
  waiting for transfers between devices  26 us (19%)
  blocking collectives  24.5 us (18%)
  Pallas kernels  6.61 us (5%)
  local copies, waits for them, and re-layouts  3.63 us (3%)
    all_to_all x1, blocking collectives, exchange(): return lax.all_to_all(blocks, axes, split_axis=0, concat_axis=0, tiled=True)  24.5 us
    all_to_all x2, starting transfers between devices, exchange(): return lax.all_to_all(blocks, axes, split_axis=0, concat_axis=0, tiled=True)  18.4 us
    ppermute x4, starting transfers between devices, near(): return (lax.ppermute(value, axis, DOWN), lax.ppermute(value, axis, UP))  16.7 us
    ppermute x4, starting transfers between devices, far(): return (lax.ppermute(up, axis, UP), lax.ppermute(down, axis, DOWN))  13.4 us
    ppermute x4, waiting for transfers between devices, near(): return (lax.ppermute(value, axis, DOWN), lax.ppermute(value, axis, UP))  9.57 us
    ppermute x1, starting transfers between devices, local(): partner = lax.ppermute(hidden, 'h', beside)  7.48 us
    ppermute x1, waiting for transfers between devices, local(): partner = lax.ppermute(hidden, 'h', beside)  5.99 us
    ppermute x1, starting transfers between devices, local(): opposite = lax.ppermute(down_weight, 'h', [(i, 3 - i) for i in range(4)])  5.36 us
  transfers between devices with their start and end apart: 17, of which 8 were waited for; matrix products, arithmetic and copies ran while one was open for 1% of the time, Pallas kernels for 4%

profile of v8, /device:TPU:6, one launch (start us, length us, event | category | flops | bytes accessed | tf_op | source)
XLA Modules:
  0.0 137.1 jit_solution(4247920226502730945)
XLA Ops:
  3.4 7.8 %collective-permute-start.1 = (bf16[896,256]{1,0:T(8,128)(2,1)S(1)}, bf16[896,256]{1,0:T(8,128)(2,1)S(1)}, u32[]{:S(2)}, u32[]{:S(2)}) collective-permute-start(bf16[896,256]{1,0:T(8,128)(2,1)S(1)} %shard_map.69.own), channel_id=1, source_target_pairs={{0,128},{128,256},{256,384},{384,0},{1,129},{129,257},{257,385},{3... | collective-permute-start | bytes 1376264 | tf_op jit(solution)/shard_map/ppermute | solution.py:28
  11.2 1.9 %collective-permute-start.2 = (bf16[896,256]{1,0:T(8,128)(2,1)S(1)}, bf16[896,256]{1,0:T(8,128)(2,1)S(1)}, u32[]{:S(2)}, u32[]{:S(2)}) collective-permute-start(bf16[896,256]{1,0:T(8,128)(2,1)S(1)} %shard_map.69.own), channel_id=1, source_target_pairs={{0,384},{128,0},{256,128},{384,256},{1,385},{129,1},{257,129},{385... | collective-permute-start | bytes 1376264 | tf_op jit(solution)/shard_map/ppermute | solution.py:28
  14.0 13.7 %all-to-all-start = ((bf16[16,152,128]{2,1,0:T(8,128)(2,1)}), bf16[16,152,128]{2,1,0:T(8,128)(2,1)S(1)}, u32[]{:S(2)}, u32[]{:S(2)}) async-start(bf16[16,152,128]{2,1,0:T(8,128)(2,1)} %broadcast_in_dim.3), calls=%async_computation | async-start | bytes 1245184 | tf_op jit(solution)/shard_map/all_to_all | solution.py:24
  27.8 3.7 %collective-permute-start.3 = (bf16[448,256]{1,0:T(8,128)(2,1)S(1)}, bf16[448,256]{1,0:T(8,128)(2,1)S(1)}, u32[]{:S(2)}, u32[]{:S(2)}) collective-permute-start(bf16[448,256]{1,0:T(8,128)(2,1)S(1)} %get-tuple-element.18), channel_id=1, source_target_pairs={{0,128},{128,256},{256,384},{384,0},{1,129},{129,257},{257,385},{3... | collective-permute-start | bytes 688136 | tf_op jit(solution)/shard_map/ppermute | solution.py:35
  31.5 2.2 %collective-permute-start.4 = (bf16[448,256]{1,0:T(8,128)(2,1)S(1)}, bf16[448,256]{1,0:T(8,128)(2,1)S(1)}, u32[]{:S(2)}, u32[]{:S(2)}) collective-permute-start(bf16[448,256]{1,0:T(8,128)(2,1)S(1)} %get-tuple-element.19), channel_id=1, source_target_pairs={{0,384},{128,0},{256,128},{384,256},{1,385},{129,1},{257,129},{385... | collective-permute-start | bytes 688136 | tf_op jit(solution)/shard_map/ppermute | solution.py:35
  33.8 5.4 %collective-permute-start.6 = (bf16[448,256]{1,0:T(8,128)(2,1)S(1)}, bf16[448,256]{1,0:T(8,128)(2,1)S(1)}, u32[]{:S(2)}, u32[]{:S(2)}) collective-permute-start(bf16[448,256]{1,0:T(8,128)(2,1)S(1)} %copy-done.3), channel_id=1, source_target_pairs={{0,96},{32,64},{64,32},{96,0},{1,97},{33,65},{65,33},{97,1},{2,98}... | collective-permute-start | bytes 688136 | tf_op jit(solution)/shard_map/ppermute | solution.py:215
  39.2 1.5 %collective-permute-done.4.second = bf16[448,256]{1,0:T(8,128)(2,1)S(1)} collective-permute-done((bf16[448,256]{1,0:T(8,128)(2,1)S(1)}, bf16[448,256]{1,0:T(8,128)(2,1)S(1)}, u32[]{:S(2)}, u32[]{:S(2)}) %collective-permute-start.4) | collective-permute-done | bytes 229408 | tf_op jit(solution)/shard_map/ppermute | solution.py:35
  40.7 2.3 %all-to-all-done.feats = bf16[16,152,128]{2,1,0:T(8,128)(2,1)S(1)} async-done(((bf16[16,152,128]{2,1,0:T(8,128)(2,1)}), bf16[16,152,128]{2,1,0:T(8,128)(2,1)S(1)}, u32[]{:S(2)}, u32[]{:S(2)}) %all-to-all-start) | async-done | bytes 622624 | tf_op jit(solution)/shard_map/all_to_all | solution.py:24
  43.0 1.9 %collective-permute-start.5 = (bf16[16,152,128]{2,1,0:T(8,128)(2,1)S(1)}, bf16[16,152,128]{2,1,0:T(8,128)(2,1)S(1)}, u32[]{:S(2)}, u32[]{:S(2)}) collective-permute-start(bf16[16,152,128]{2,1,0:T(8,128)(2,1)S(1)} %all-to-all-done.feats), channel_id=1, source_target_pairs={{0,1},{1,0},{2,3},{3,2},{4,5},{5,4},{6,7},{7,6},{8,9},{9,8},{10,11... | collective-permute-start | bytes 1867784 | tf_op jit(solution)/shard_map/ppermute | solution.py:20
  46.9 2.1 %shard_map.72 = (bf16[4,152,896]{2,1,0:T(8,128)(2,1)}, bf16[152,896]{1,0:T(8,128)(2,1)S(1)}) custom-call(bf16[16,152,128]{2,1,0:T(8,128)(2,1)S(1)} %collective-permute-done.5.feats, f32[640,896]{1,0:T(8,128)S(1)} %shard_map.71.started, bf16[896,256]{1,0:T(8,128)(2,1)S(1)} %shard_map.69.own, bf16[896,256]{1,0:T(8,128)(2,1)S(1)} %collective-permute-done.2.following, ...), custom_call_target="tpu_custom_call" | custom-call | flops 110000000 | bytes 1048576 | tf_op jit(solution)/shard_map/pallas_call | solution.py:221
  49.0 4.7 %all-to-all-start.1 = ((bf16[4,152,896]{2,1,0:T(8,128)(2,1)}), bf16[4,152,896]{2,1,0:T(8,128)(2,1)S(1)}, u32[]{:S(2)}, u32[]{:S(2)}) async-start(bf16[4,152,896]{2,1,0:T(8,128)(2,1)} %get-tuple-element.23), calls=%async_computation.1 | async-start | bytes 2179072 | tf_op jit(solution)/shard_map/all_to_all | solution.py:24
  53.8 2.7 %collective-permute-start.7 = (bf16[2,448,256]{2,1,0:T(8,128)(2,1)S(1)}, bf16[2,448,256]{2,1,0:T(8,128)(2,1)S(1)}, u32[]{:S(2)}, u32[]{:S(2)}) collective-permute-start(bf16[2,448,256]{2,1,0:T(8,128)(2,1)S(1)} %shard_map.74.own), channel_id=1, source_target_pairs={{0,384},{128,0},{256,128},{384,256},{1,385},{129,1},{257,129},{385... | collective-permute-start | bytes 1376264 | tf_op jit(solution)/shard_map/ppermute | solution.py:28
  56.5 4.3 %collective-permute-start.8 = (bf16[2,448,256]{2,1,0:T(8,128)(2,1)S(1)}, bf16[2,448,256]{2,1,0:T(8,128)(2,1)S(1)}, u32[]{:S(2)}, u32[]{:S(2)}) collective-permute-start(bf16[2,448,256]{2,1,0:T(8,128)(2,1)S(1)} %shard_map.74.own), channel_id=1, source_target_pairs={{0,128},{128,256},{256,384},{384,0},{1,129},{129,257},{257,385},{3... | collective-permute-start | bytes 1376264 | tf_op jit(solution)/shard_map/ppermute | solution.py:28
  60.9 8.3 %collective-permute-done.7.following = bf16[2,448,256]{2,1,0:T(8,128)(2,1)S(1)} collective-permute-done((bf16[2,448,256]{2,1,0:T(8,128)(2,1)S(1)}, bf16[2,448,256]{2,1,0:T(8,128)(2,1)S(1)}, u32[]{:S(2)}, u32[]{:S(2)}) %collective-permute-start.7) | collective-permute-done | bytes 458784 | tf_op jit(solution)/shard_map/ppermute | solution.py:28
  71.2 2.4 %collective-permute-start.10 = (bf16[2,224,256]{2,1,0:T(8,128)(2,1)}, bf16[2,224,256]{2,1,0:T(8,128)(2,1)S(1)}, u32[]{:S(2)}, u32[]{:S(2)}) collective-permute-start(bf16[2,224,256]{2,1,0:T(8,128)(2,1)} %get-tuple-element.26), channel_id=1, source_target_pairs={{0,384},{128,0},{256,128},{384,256},{1,385},{129,1},{257,129},{385... | collective-permute-start | bytes 688136 | tf_op jit(solution)/shard_map/ppermute | solution.py:35
  73.7 5.0 %collective-permute-start.9 = (bf16[2,224,256]{2,1,0:T(8,128)(2,1)}, bf16[2,224,256]{2,1,0:T(8,128)(2,1)S(1)}, u32[]{:S(2)}, u32[]{:S(2)}) collective-permute-start(bf16[2,224,256]{2,1,0:T(8,128)(2,1)} %get-tuple-element.25), channel_id=1, source_target_pairs={{0,128},{128,256},{256,384},{384,0},{1,129},{129,257},{257,385},{3... | collective-permute-start | bytes 688136 | tf_op jit(solution)/shard_map/ppermute | solution.py:35
  79.0 7.5 %collective-permute-start.11 = (bf16[152,448]{1,0:T(8,128)(2,1)S(1)}, bf16[152,448]{1,0:T(8,128)(2,1)S(1)}, u32[]{:S(2)}, u32[]{:S(2)}) collective-permute-start(bf16[152,448]{1,0:T(8,128)(2,1)S(1)} %shard_map.73.hidden), channel_id=1, source_target_pairs={{0,32},{32,0},{64,96},{96,64},{1,33},{33,1},{65,97},{97,65},{2,34}... | collective-permute-start | bytes 408584 | tf_op jit(solution)/shard_map/ppermute | solution.py:232
  87.1 6.0 %collective-permute-done.11.hidden = bf16[152,448]{1,0:T(8,128)(2,1)S(1)} collective-permute-done((bf16[152,448]{1,0:T(8,128)(2,1)S(1)}, bf16[152,448]{1,0:T(8,128)(2,1)S(1)}, u32[]{:S(2)}, u32[]{:S(2)}) %collective-permute-start.11) | collective-permute-done | bytes 136224 | tf_op jit(solution)/shard_map/ppermute | solution.py:232
  93.6 1.9 %collective-permute-start.12 = (bf16[8,2,80,256]{3,2,1,0:T(8,128)(2,1)S(1)}, bf16[8,2,80,256]{3,2,1,0:T(8,128)(2,1)S(1)}, u32[]{:S(2)}, u32[]{:S(2)}) collective-permute-start(bf16[8,2,80,256]{3,2,1,0:T(8,128)(2,1)S(1)} %get-tuple-element.33), channel_id=1, source_target_pairs={{0,1},{1,0},{2,3},{3,2},{4,5},{5,4},{6,7},{7,6},{8,9},{9,8},{10,11... | collective-permute-start | bytes 1966088 | tf_op jit(solution)/shard_map/ppermute | solution.py:20
  95.5 2.1 %collective-permute-done.12 = bf16[8,2,80,256]{3,2,1,0:T(8,128)(2,1)S(1)} collective-permute-done((bf16[8,2,80,256]{3,2,1,0:T(8,128)(2,1)S(1)}, bf16[8,2,80,256]{3,2,1,0:T(8,128)(2,1)S(1)}, u32[]{:S(2)}, u32[]{:S(2)}) %collective-permute-start.12) | collective-permute-done | bytes 655392 | tf_op jit(solution)/shard_map/ppermute | solution.py:20
  98.8 24.5 %all_to_all.15 = bf16[16,80,256]{2,1,0:T(8,128)(2,1)S(1)} all-to-all(bf16[16,80,256]{2,1,0:T(8,128)(2,1)S(1)} %copy.20), channel_id=1, replica_groups=mesh['x'=4,'h'=4,'l'=2,'a'=2,'b'=4,'c'=2] {'l','a','b'}, dimensions={0} | all-to-all | bytes 1310720 | tf_op jit(solution)/shard_map/all_to_all | solution.py:24
  123.4 4.6 %collective-permute-start.14 = (bf16[16,256]{1,0:T(8,128)(2,1)S(1)}, bf16[16,256]{1,0:T(8,128)(2,1)S(1)}, u32[]{:S(2)}, u32[]{:S(2)}) collective-permute-start(bf16[16,256]{1,0:T(8,128)(2,1)S(1)} %slice.29), channel_id=1, source_target_pairs={{0,0},{2,2},{4,96},{6,98},{8,128},{10,130},{12,224},{14,226},{16,2... | collective-permute-start | bytes 24584 | tf_op jit(solution)/shard_map/ppermute | solution.py:256
  128.1 4.4 %collective-permute-start.13 = (bf16[4,2,4,256]{3,2,1,0:T(4,128)(2,1)S(1)}, bf16[4,2,4,256]{3,2,1,0:T(4,128)(2,1)S(1)}, u32[]{:S(2)}, u32[]{:S(2)}) collective-permute-start(bf16[4,2,4,256]{3,2,1,0:T(4,128)(2,1)S(1)} %get-tuple-element.34), channel_id=1, source_target_pairs={{0,32},{32,0},{64,96},{96,64},{1,33},{33,1},{65,97},{97,65},{2,34}... | collective-permute-start | bytes 49160 | tf_op jit(solution)/shard_map/ppermute | solution.py:274
  132.5 3.4 %collective-permute-done.14.rows = bf16[16,256]{1,0:T(8,128)(2,1)S(1)} collective-permute-done((bf16[16,256]{1,0:T(8,128)(2,1)S(1)}, bf16[16,256]{1,0:T(8,128)(2,1)S(1)}, u32[]{:S(2)}, u32[]{:S(2)}) %collective-permute-start.14) | collective-permute-done | bytes 8224 | tf_op jit(solution)/shard_map/ppermute | solution.py:256
  (48 shorter events, 11.7 us)
Async XLA Ops:
  0.6 0.9 copy-start
  1.6 0.8 copy-start.4
  2.3 1.0 copy-start.1
  2.3 1.0 copy-start.2
  2.5 10.6 %collective-permute-start = (bf16[152,128]{1,0:T(8,128)(2,1)S(1)}, bf16[152,128]{1,0:T(8,128)(2,1)S(1)}, u32[]{:S(2)}, u32[]{:S(2)}) collective-permute-start(bf16[152,128]{1,0:T(8,128)(2,1)S(1)} %shard_map.68), channel_id=1, source_target_pairs={{0,0},{2,32},{4,64},{6,96},{32,2},{34,34},{36,66},{38,98},{64,4},{... | collective-permute-start | bytes 116744 | tf_op jit(solution)/shard_map/ppermute | solution.py:206
  3.4 24.3 %collective-permute-start.1 = (bf16[896,256]{1,0:T(8,128)(2,1)S(1)}, bf16[896,256]{1,0:T(8,128)(2,1)S(1)}, u32[]{:S(2)}, u32[]{:S(2)}) collective-permute-start(bf16[896,256]{1,0:T(8,128)(2,1)S(1)} %shard_map.69.own), channel_id=1, source_target_pairs={{0,128},{128,256},{256,384},{384,0},{1,129},{129,257},{257,385},{3... | collective-permute-start | bytes 1376264 | tf_op jit(solution)/shard_map/ppermute | solution.py:28
  11.2 16.6 %collective-permute-start.2 = (bf16[896,256]{1,0:T(8,128)(2,1)S(1)}, bf16[896,256]{1,0:T(8,128)(2,1)S(1)}, u32[]{:S(2)}, u32[]{:S(2)}) collective-permute-start(bf16[896,256]{1,0:T(8,128)(2,1)S(1)} %shard_map.69.own), channel_id=1, source_target_pairs={{0,384},{128,0},{256,128},{384,256},{1,385},{129,1},{257,129},{385... | collective-permute-start | bytes 1376264 | tf_op jit(solution)/shard_map/ppermute | solution.py:28
  14.0 28.9 %all-to-all-start = ((bf16[16,152,128]{2,1,0:T(8,128)(2,1)}), bf16[16,152,128]{2,1,0:T(8,128)(2,1)S(1)}, u32[]{:S(2)}, u32[]{:S(2)}) async-start(bf16[16,152,128]{2,1,0:T(8,128)(2,1)} %broadcast_in_dim.3), calls=%async_computation | async-start | bytes 1245184 | tf_op jit(solution)/shard_map/all_to_all | solution.py:24
  27.7 6.1 %copy-start.3 = (bf16[448,256]{1,0:T(8,128)(2,1)S(1)}, bf16[448,256]{1,0:T(8,128)(2,1)}, u32[]{:S(2)}) copy-start(bf16[448,256]{1,0:T(8,128)(2,1)} %own.1) | copy-start | bytes 688132
  27.8 11.4 %collective-permute-start.3 = (bf16[448,256]{1,0:T(8,128)(2,1)S(1)}, bf16[448,256]{1,0:T(8,128)(2,1)S(1)}, u32[]{:S(2)}, u32[]{:S(2)}) collective-permute-start(bf16[448,256]{1,0:T(8,128)(2,1)S(1)} %get-tuple-element.18), channel_id=1, source_target_pairs={{0,128},{128,256},{256,384},{384,0},{1,129},{129,257},{257,385},{3... | collective-permute-start | bytes 688136 | tf_op jit(solution)/shard_map/ppermute | solution.py:35
  31.5 9.1 %collective-permute-start.4 = (bf16[448,256]{1,0:T(8,128)(2,1)S(1)}, bf16[448,256]{1,0:T(8,128)(2,1)S(1)}, u32[]{:S(2)}, u32[]{:S(2)}) collective-permute-start(bf16[448,256]{1,0:T(8,128)(2,1)S(1)} %get-tuple-element.19), channel_id=1, source_target_pairs={{0,384},{128,0},{256,128},{384,256},{1,385},{129,1},{257,129},{385... | collective-permute-start | bytes 688136 | tf_op jit(solution)/shard_map/ppermute | solution.py:35
  33.8 20.0 %collective-permute-start.6 = (bf16[448,256]{1,0:T(8,128)(2,1)S(1)}, bf16[448,256]{1,0:T(8,128)(2,1)S(1)}, u32[]{:S(2)}, u32[]{:S(2)}) collective-permute-start(bf16[448,256]{1,0:T(8,128)(2,1)S(1)} %copy-done.3), channel_id=1, source_target_pairs={{0,96},{32,64},{64,32},{96,0},{1,97},{33,65},{65,33},{97,1},{2,98}... | collective-permute-start | bytes 688136 | tf_op jit(solution)/shard_map/ppermute | solution.py:215
  43.0 3.9 %collective-permute-start.5 = (bf16[16,152,128]{2,1,0:T(8,128)(2,1)S(1)}, bf16[16,152,128]{2,1,0:T(8,128)(2,1)S(1)}, u32[]{:S(2)}, u32[]{:S(2)}) collective-permute-start(bf16[16,152,128]{2,1,0:T(8,128)(2,1)S(1)} %all-to-all-done.feats), channel_id=1, source_target_pairs={{0,1},{1,0},{2,3},{3,2},{4,5},{5,4},{6,7},{7,6},{8,9},{9,8},{10,11... | collective-permute-start | bytes 1867784 | tf_op jit(solution)/shard_map/ppermute | solution.py:20
  49.0 29.7 %all-to-all-start.1 = ((bf16[4,152,896]{2,1,0:T(8,128)(2,1)}), bf16[4,152,896]{2,1,0:T(8,128)(2,1)S(1)}, u32[]{:S(2)}, u32[]{:S(2)}) async-start(bf16[4,152,896]{2,1,0:T(8,128)(2,1)} %get-tuple-element.23), calls=%async_computation.1 | async-start | bytes 2179072 | tf_op jit(solution)/shard_map/all_to_all | solution.py:24
  53.8 15.4 %collective-permute-start.7 = (bf16[2,448,256]{2,1,0:T(8,128)(2,1)S(1)}, bf16[2,448,256]{2,1,0:T(8,128)(2,1)S(1)}, u32[]{:S(2)}, u32[]{:S(2)}) collective-permute-start(bf16[2,448,256]{2,1,0:T(8,128)(2,1)S(1)} %shard_map.74.own), channel_id=1, source_target_pairs={{0,384},{128,0},{256,128},{384,256},{1,385},{129,1},{257,129},{385... | collective-permute-start | bytes 1376264 | tf_op jit(solution)/shard_map/ppermute | solution.py:28
  56.5 13.9 %collective-permute-start.8 = (bf16[2,448,256]{2,1,0:T(8,128)(2,1)S(1)}, bf16[2,448,256]{2,1,0:T(8,128)(2,1)S(1)}, u32[]{:S(2)}, u32[]{:S(2)}) collective-permute-start(bf16[2,448,256]{2,1,0:T(8,128)(2,1)S(1)} %shard_map.74.own), channel_id=1, source_target_pairs={{0,128},{128,256},{256,384},{384,0},{1,129},{129,257},{257,385},{3... | collective-permute-start | bytes 1376264 | tf_op jit(solution)/shard_map/ppermute | solution.py:28
  71.2 15.3 %collective-permute-start.10 = (bf16[2,224,256]{2,1,0:T(8,128)(2,1)}, bf16[2,224,256]{2,1,0:T(8,128)(2,1)S(1)}, u32[]{:S(2)}, u32[]{:S(2)}) collective-permute-start(bf16[2,224,256]{2,1,0:T(8,128)(2,1)} %get-tuple-element.26), channel_id=1, source_target_pairs={{0,384},{128,0},{256,128},{384,256},{1,385},{129,1},{257,129},{385... | collective-permute-start | bytes 688136 | tf_op jit(solution)/shard_map/ppermute | solution.py:35
  73.7 12.8 %collective-permute-start.9 = (bf16[2,224,256]{2,1,0:T(8,128)(2,1)}, bf16[2,224,256]{2,1,0:T(8,128)(2,1)S(1)}, u32[]{:S(2)}, u32[]{:S(2)}) collective-permute-start(bf16[2,224,256]{2,1,0:T(8,128)(2,1)} %get-tuple-element.25), channel_id=1, source_target_pairs={{0,128},{128,256},{256,384},{384,0},{1,129},{129,257},{257,385},{3... | collective-permute-start | bytes 688136 | tf_op jit(solution)/shard_map/ppermute | solution.py:35
  79.0 14.0 %collective-permute-start.11 = (bf16[152,448]{1,0:T(8,128)(2,1)S(1)}, bf16[152,448]{1,0:T(8,128)(2,1)S(1)}, u32[]{:S(2)}, u32[]{:S(2)}) collective-permute-start(bf16[152,448]{1,0:T(8,128)(2,1)S(1)} %shard_map.73.hidden), channel_id=1, source_target_pairs={{0,32},{32,0},{64,96},{96,64},{1,33},{33,1},{65,97},{97,65},{2,34}... | collective-permute-start | bytes 408584 | tf_op jit(solution)/shard_map/ppermute | solution.py:232
  93.6 4.0 %collective-permute-start.12 = (bf16[8,2,80,256]{3,2,1,0:T(8,128)(2,1)S(1)}, bf16[8,2,80,256]{3,2,1,0:T(8,128)(2,1)S(1)}, u32[]{:S(2)}, u32[]{:S(2)}) collective-permute-start(bf16[8,2,80,256]{3,2,1,0:T(8,128)(2,1)S(1)} %get-tuple-element.33), channel_id=1, source_target_pairs={{0,1},{1,0},{2,3},{3,2},{4,5},{5,4},{6,7},{7,6},{8,9},{9,8},{10,11... | collective-permute-start | bytes 1966088 | tf_op jit(solution)/shard_map/ppermute | solution.py:20
  123.4 12.5 %collective-permute-start.14 = (bf16[16,256]{1,0:T(8,128)(2,1)S(1)}, bf16[16,256]{1,0:T(8,128)(2,1)S(1)}, u32[]{:S(2)}, u32[]{:S(2)}) collective-permute-start(bf16[16,256]{1,0:T(8,128)(2,1)S(1)} %slice.29), channel_id=1, source_target_pairs={{0,0},{2,2},{4,96},{6,98},{8,128},{10,130},{12,224},{14,226},{16,2... | collective-permute-start | bytes 24584 | tf_op jit(solution)/shard_map/ppermute | solution.py:256
  128.1 8.4 %collective-permute-start.13 = (bf16[4,2,4,256]{3,2,1,0:T(4,128)(2,1)S(1)}, bf16[4,2,4,256]{3,2,1,0:T(4,128)(2,1)S(1)}, u32[]{:S(2)}, u32[]{:S(2)}) collective-permute-start(bf16[4,2,4,256]{3,2,1,0:T(4,128)(2,1)S(1)} %get-tuple-element.34), channel_id=1, source_target_pairs={{0,32},{32,0},{64,96},{96,64},{1,33},{33,1},{65,97},{97,65},{2,34}... | collective-permute-start | bytes 49160 | tf_op jit(solution)/shard_map/ppermute | solution.py:274

commit v9 on v8

--- a/solution.py
+++ b/solution.py
@@ -213,7 +213,6 @@
     own_near = near(own, "x")
     own_far = far(*own_near, "x", HINTS[0])
     opposite = lax.ppermute(down_weight, "h", [(i, 3 - i) for i in range(4)])
-    feats, own_far = lax.optimization_barrier((feats, own_far))
     other = swap_cores(feats)
 
     weights = (own, own_near[0], *own_far, own_near[1])

time: 139 us -> 141 us (1.014)
  waiting for transfers between devices: 26 us -> 20.9 us
  blocking collectives: 24.5 us -> 28.7 us
    all_to_all x1, blocking collectives: 24.5 us -> 28.7 us  [exchange(): return lax.all_to_all(blocks, axes, split_axis=0, concat_axis=0, tiled=True)]
    ppermute x1, waiting for transfers between devices: 5.99 us -> 2.66 us  [local(): partner = lax.ppermute(hidden, 'h', beside)]
    ppermute x1, waiting for transfers between devices: 3.39 us -> 1.91 us  [local(): lax.ppermute(sums[half:], ('x', 'h', 'l', 'a', 'b'), [(x * 64 + h * 16 +...]
    ppermute x4, waiting for transfers between devices: 1.49 us -> 0.01 us  [far(): return (lax.ppermute(up, axis, UP), lax.ppermute(down, axis, DOWN))]
  transfers between devices with their start and end apart: 17 -> 17, of which waited for: 8 -> 7; matrix products, arithmetic and copies ran while one was open for 1% -> 1% of each run, Pallas kernels for 4% -> 4%
where the time goes in v9:
time: 141 us; the launch traced here: 138 us
  starting transfers between devices  76.2 us (54%)
  blocking collectives  28.7 us (20%)
  waiting for transfers between devices  20.9 us (15%)
  Pallas kernels  7.31 us (5%)
  local copies, waits for them, and re-layouts  3.63 us (3%)
    all_to_all x1, blocking collectives, exchange(): return lax.all_to_all(blocks, axes, split_axis=0, concat_axis=0, tiled=True)  28.7 us
    all_to_all x2, starting transfers between devices, exchange(): return lax.all_to_all(blocks, axes, split_axis=0, concat_axis=0, tiled=True)  19.2 us
    ppermute x4, starting transfers between devices, near(): return (lax.ppermute(value, axis, DOWN), lax.ppermute(value, axis, UP))  16.7 us
    ppermute x4, starting transfers between devices, far(): return (lax.ppermute(up, axis, UP), lax.ppermute(down, axis, DOWN))  13.3 us
    ppermute x4, waiting for transfers between devices, near(): return (lax.ppermute(value, axis, DOWN), lax.ppermute(value, axis, UP))  9.5 us
    ppermute x1, starting transfers between devices, local(): partner = lax.ppermute(hidden, 'h', beside)  6.73 us
    ppermute x1, starting transfers between devices, local(): lax.ppermute(sums[half:], ('x', 'h', 'l', 'a', 'b'), [(x * 64 + h * 16 +...  5.58 us
    ppermute x1, starting transfers between devices, local(): opposite = lax.ppermute(down_weight, 'h', [(i, 3 - i) for i in range(4)])  5.03 us
  transfers between devices with their start and end apart: 17, of which 7 were waited for; matrix products, arithmetic and copies ran while one was open for 1% of the time, Pallas kernels for 4%

profile of v9, /device:TPU:6, one launch (start us, length us, event | category | flops | bytes accessed | tf_op | source)
XLA Modules:
  0.0 138.0 jit_solution(15728960000793847589)
XLA Ops:
  3.4 2.7 %collective-permute-start.2 = (bf16[896,256]{1,0:T(8,128)(2,1)S(1)}, bf16[896,256]{1,0:T(8,128)(2,1)S(1)}, u32[]{:S(2)}, u32[]{:S(2)}) collective-permute-start(bf16[896,256]{1,0:T(8,128)(2,1)S(1)} %shard_map.69.own), channel_id=1, source_target_pairs={{0,384},{128,0},{256,128},{384,256},{1,385},{129,1},{257,129},{385... | collective-permute-start | bytes 1376264 | tf_op jit(solution)/shard_map/ppermute | solution.py:28
  6.2 6.9 %collective-permute-start.3 = (bf16[896,256]{1,0:T(8,128)(2,1)S(1)}, bf16[896,256]{1,0:T(8,128)(2,1)S(1)}, u32[]{:S(2)}, u32[]{:S(2)}) collective-permute-start(bf16[896,256]{1,0:T(8,128)(2,1)S(1)} %shard_map.69.own), channel_id=1, source_target_pairs={{0,128},{128,256},{256,384},{384,0},{1,129},{129,257},{257,385},{3... | collective-permute-start | bytes 1376264 | tf_op jit(solution)/shard_map/ppermute | solution.py:28
  14.0 14.9 %all-to-all-start = ((bf16[16,152,128]{2,1,0:T(8,128)(2,1)}), bf16[16,152,128]{2,1,0:T(8,128)(2,1)S(1)}, u32[]{:S(2)}, u32[]{:S(2)}) async-start(bf16[16,152,128]{2,1,0:T(8,128)(2,1)} %broadcast_in_dim.3), calls=%async_computation | async-start | bytes 1245184 | tf_op jit(solution)/shard_map/all_to_all | solution.py:24
  29.7 1.9 %collective-permute-start.4 = (bf16[448,256]{1,0:T(8,128)(2,1)}, bf16[448,256]{1,0:T(8,128)(2,1)S(1)}, u32[]{:S(2)}, u32[]{:S(2)}) collective-permute-start(bf16[448,256]{1,0:T(8,128)(2,1)} %get-tuple-element.15), channel_id=1, source_target_pairs={{0,128},{128,256},{256,384},{384,0},{1,129},{129,257},{257,385},{3... | collective-permute-start | bytes 688136 | tf_op jit(solution)/shard_map/ppermute | solution.py:35
  31.6 3.9 %collective-permute-start.5 = (bf16[448,256]{1,0:T(8,128)(2,1)S(1)}, bf16[448,256]{1,0:T(8,128)(2,1)S(1)}, u32[]{:S(2)}, u32[]{:S(2)}) collective-permute-start(bf16[448,256]{1,0:T(8,128)(2,1)S(1)} %get-tuple-element.16), channel_id=1, source_target_pairs={{0,384},{128,0},{256,128},{384,256},{1,385},{129,1},{257,129},{385... | collective-permute-start | bytes 688136 | tf_op jit(solution)/shard_map/ppermute | solution.py:35
  35.6 5.0 %collective-permute-start.6 = (bf16[448,256]{1,0:T(8,128)(2,1)S(1)}, bf16[448,256]{1,0:T(8,128)(2,1)S(1)}, u32[]{:S(2)}, u32[]{:S(2)}) collective-permute-start(bf16[448,256]{1,0:T(8,128)(2,1)S(1)} %copy-done.3), channel_id=1, source_target_pairs={{0,96},{32,64},{64,32},{96,0},{1,97},{33,65},{65,33},{97,1},{2,98}... | collective-permute-start | bytes 688136 | tf_op jit(solution)/shard_map/ppermute | solution.py:215
  40.6 3.6 %all-to-all-done.feats = bf16[16,152,128]{2,1,0:T(8,128)(2,1)S(1)} async-done(((bf16[16,152,128]{2,1,0:T(8,128)(2,1)}), bf16[16,152,128]{2,1,0:T(8,128)(2,1)S(1)}, u32[]{:S(2)}, u32[]{:S(2)}) %all-to-all-start) | async-done | bytes 622624 | tf_op jit(solution)/shard_map/all_to_all | solution.py:24
  44.2 1.9 %collective-permute-start.1 = (bf16[16,152,128]{2,1,0:T(8,128)(2,1)S(1)}, bf16[16,152,128]{2,1,0:T(8,128)(2,1)S(1)}, u32[]{:S(2)}, u32[]{:S(2)}) collective-permute-start(bf16[16,152,128]{2,1,0:T(8,128)(2,1)S(1)} %all-to-all-done.feats), channel_id=1, source_target_pairs={{0,1},{1,0},{2,3},{3,2},{4,5},{5,4},{6,7},{7,6},{8,9},{9,8},{10,11... | collective-permute-start | bytes 1867784 | tf_op jit(solution)/shard_map/ppermute | solution.py:20
  48.1 2.1 %shard_map.72 = (bf16[4,152,896]{2,1,0:T(8,128)(2,1)}, bf16[152,896]{1,0:T(8,128)(2,1)S(1)}) custom-call(bf16[16,152,128]{2,1,0:T(8,128)(2,1)S(1)} %collective-permute-done.1.feats, f32[640,896]{1,0:T(8,128)S(1)} %shard_map.71.started, bf16[896,256]{1,0:T(8,128)(2,1)S(1)} %shard_map.69.own, bf16[896,256]{1,0:T(8,128)(2,1)S(1)} %collective-permute-done.2.following, ...), custom_call_target="tpu_custom_call" | custom-call | flops 110000000 | bytes 1048576 | tf_op jit(solution)/shard_map/pallas_call | solution.py:220
  50.2 4.3 %all-to-all-start.1 = ((bf16[4,152,896]{2,1,0:T(8,128)(2,1)}), bf16[4,152,896]{2,1,0:T(8,128)(2,1)S(1)}, u32[]{:S(2)}, u32[]{:S(2)}) async-start(bf16[4,152,896]{2,1,0:T(8,128)(2,1)} %get-tuple-element.17), calls=%async_computation.1 | async-start | bytes 2179072 | tf_op jit(solution)/shard_map/all_to_all | solution.py:24
  54.6 1.9 %collective-permute-start.7 = (bf16[2,448,256]{2,1,0:T(8,128)(2,1)S(1)}, bf16[2,448,256]{2,1,0:T(8,128)(2,1)S(1)}, u32[]{:S(2)}, u32[]{:S(2)}) collective-permute-start(bf16[2,448,256]{2,1,0:T(8,128)(2,1)S(1)} %shard_map.74.own), channel_id=1, source_target_pairs={{0,384},{128,0},{256,128},{384,256},{1,385},{129,1},{257,129},{385... | collective-permute-start | bytes 1376264 | tf_op jit(solution)/shard_map/ppermute | solution.py:28
  56.5 5.1 %collective-permute-start.8 = (bf16[2,448,256]{2,1,0:T(8,128)(2,1)S(1)}, bf16[2,448,256]{2,1,0:T(8,128)(2,1)S(1)}, u32[]{:S(2)}, u32[]{:S(2)}) collective-permute-start(bf16[2,448,256]{2,1,0:T(8,128)(2,1)S(1)} %shard_map.74.own), channel_id=1, source_target_pairs={{0,128},{128,256},{256,384},{384,0},{1,129},{129,257},{257,385},{3... | collective-permute-start | bytes 1376264 | tf_op jit(solution)/shard_map/ppermute | solution.py:28
  61.7 8.3 %collective-permute-done.7.following = bf16[2,448,256]{2,1,0:T(8,128)(2,1)S(1)} collective-permute-done((bf16[2,448,256]{2,1,0:T(8,128)(2,1)S(1)}, bf16[2,448,256]{2,1,0:T(8,128)(2,1)S(1)}, u32[]{:S(2)}, u32[]{:S(2)}) %collective-permute-start.7) | collective-permute-done | bytes 458784 | tf_op jit(solution)/shard_map/ppermute | solution.py:28
  70.0 1.2 collective-permute-done.8.previous
  72.0 1.9 %collective-permute-start.10 = (bf16[2,224,256]{2,1,0:T(8,128)(2,1)}, bf16[2,224,256]{2,1,0:T(8,128)(2,1)S(1)}, u32[]{:S(2)}, u32[]{:S(2)}) collective-permute-start(bf16[2,224,256]{2,1,0:T(8,128)(2,1)} %get-tuple-element.20), channel_id=1, source_target_pairs={{0,384},{128,0},{256,128},{384,256},{1,385},{129,1},{257,129},{385... | collective-permute-start | bytes 688136 | tf_op jit(solution)/shard_map/ppermute | solution.py:35
  73.9 5.6 %collective-permute-start.9 = (bf16[2,224,256]{2,1,0:T(8,128)(2,1)}, bf16[2,224,256]{2,1,0:T(8,128)(2,1)S(1)}, u32[]{:S(2)}, u32[]{:S(2)}) collective-permute-start(bf16[2,224,256]{2,1,0:T(8,128)(2,1)} %get-tuple-element.19), channel_id=1, source_target_pairs={{0,128},{128,256},{256,384},{384,0},{1,129},{129,257},{257,385},{3... | collective-permute-start | bytes 688136 | tf_op jit(solution)/shard_map/ppermute | solution.py:35
  79.9 6.7 %collective-permute-start.11 = (bf16[152,448]{1,0:T(8,128)(2,1)S(1)}, bf16[152,448]{1,0:T(8,128)(2,1)S(1)}, u32[]{:S(2)}, u32[]{:S(2)}) collective-permute-start(bf16[152,448]{1,0:T(8,128)(2,1)S(1)} %shard_map.73.hidden), channel_id=1, source_target_pairs={{0,32},{32,0},{64,96},{96,64},{1,33},{33,1},{65,97},{97,65},{2,34}... | collective-permute-start | bytes 408584 | tf_op jit(solution)/shard_map/ppermute | solution.py:231
  87.1 2.7 %collective-permute-done.11.hidden = bf16[152,448]{1,0:T(8,128)(2,1)S(1)} collective-permute-done((bf16[152,448]{1,0:T(8,128)(2,1)S(1)}, bf16[152,448]{1,0:T(8,128)(2,1)S(1)}, u32[]{:S(2)}, u32[]{:S(2)}) %collective-permute-start.11) | collective-permute-done | bytes 136224 | tf_op jit(solution)/shard_map/ppermute | solution.py:231
  90.3 1.9 %collective-permute-start.12 = (bf16[8,2,80,256]{3,2,1,0:T(8,128)(2,1)S(1)}, bf16[8,2,80,256]{3,2,1,0:T(8,128)(2,1)S(1)}, u32[]{:S(2)}, u32[]{:S(2)}) collective-permute-start(bf16[8,2,80,256]{3,2,1,0:T(8,128)(2,1)S(1)} %get-tuple-element.27), channel_id=1, source_target_pairs={{0,1},{1,0},{2,3},{3,2},{4,5},{5,4},{6,7},{7,6},{8,9},{9,8},{10,11... | collective-permute-start | bytes 1966088 | tf_op jit(solution)/shard_map/ppermute | solution.py:20
  92.2 2.1 %collective-permute-done.12 = bf16[8,2,80,256]{3,2,1,0:T(8,128)(2,1)S(1)} collective-permute-done((bf16[8,2,80,256]{3,2,1,0:T(8,128)(2,1)S(1)}, bf16[8,2,80,256]{3,2,1,0:T(8,128)(2,1)S(1)}, u32[]{:S(2)}, u32[]{:S(2)}) %collective-permute-start.12) | collective-permute-done | bytes 655392 | tf_op jit(solution)/shard_map/ppermute | solution.py:20
  95.5 28.7 %all_to_all.15 = bf16[16,80,256]{2,1,0:T(8,128)(2,1)S(1)} all-to-all(bf16[16,80,256]{2,1,0:T(8,128)(2,1)S(1)} %copy.20), channel_id=1, replica_groups=mesh['x'=4,'h'=4,'l'=2,'a'=2,'b'=4,'c'=2] {'l','a','b'}, dimensions={0} | all-to-all | bytes 1310720 | tf_op jit(solution)/shard_map/all_to_all | solution.py:24
  124.3 5.6 %collective-permute-start.14 = (bf16[16,256]{1,0:T(8,128)(2,1)S(1)}, bf16[16,256]{1,0:T(8,128)(2,1)S(1)}, u32[]{:S(2)}, u32[]{:S(2)}) collective-permute-start(bf16[16,256]{1,0:T(8,128)(2,1)S(1)} %slice.29), channel_id=1, source_target_pairs={{0,0},{2,2},{4,96},{6,98},{8,128},{10,130},{12,224},{14,226},{16,2... | collective-permute-start | bytes 24584 | tf_op jit(solution)/shard_map/ppermute | solution.py:255
  129.9 4.9 %collective-permute-start.13 = (bf16[4,2,4,256]{3,2,1,0:T(4,128)(2,1)S(1)}, bf16[4,2,4,256]{3,2,1,0:T(4,128)(2,1)S(1)}, u32[]{:S(2)}, u32[]{:S(2)}) collective-permute-start(bf16[4,2,4,256]{3,2,1,0:T(4,128)(2,1)S(1)} %get-tuple-element.28), channel_id=1, source_target_pairs={{0,32},{32,0},{64,96},{96,64},{1,33},{33,1},{65,97},{97,65},{2,34}... | collective-permute-start | bytes 49160 | tf_op jit(solution)/shard_map/ppermute | solution.py:273
  134.9 1.9 %collective-permute-done.14.rows = bf16[16,256]{1,0:T(8,128)(2,1)S(1)} collective-permute-done((bf16[16,256]{1,0:T(8,128)(2,1)S(1)}, bf16[16,256]{1,0:T(8,128)(2,1)S(1)}, u32[]{:S(2)}, u32[]{:S(2)}) %collective-permute-start.14) | collective-permute-done | bytes 8224 | tf_op jit(solution)/shard_map/ppermute | solution.py:255
  (48 shorter events, 11.1 us)
Async XLA Ops:
  0.6 0.9 copy-start
  1.6 0.8 copy-start.4
  2.3 1.0 copy-start.1
  2.3 1.0 copy-start.2
  2.5 10.6 %collective-permute-start = (bf16[152,128]{1,0:T(8,128)(2,1)S(1)}, bf16[152,128]{1,0:T(8,128)(2,1)S(1)}, u32[]{:S(2)}, u32[]{:S(2)}) collective-permute-start(bf16[152,128]{1,0:T(8,128)(2,1)S(1)} %shard_map.68), channel_id=1, source_target_pairs={{0,0},{2,32},{4,64},{6,96},{32,2},{34,34},{36,66},{38,98},{64,4},{... | collective-permute-start | bytes 116744 | tf_op jit(solution)/shard_map/ppermute | solution.py:206
  3.4 25.5 %collective-permute-start.2 = (bf16[896,256]{1,0:T(8,128)(2,1)S(1)}, bf16[896,256]{1,0:T(8,128)(2,1)S(1)}, u32[]{:S(2)}, u32[]{:S(2)}) collective-permute-start(bf16[896,256]{1,0:T(8,128)(2,1)S(1)} %shard_map.69.own), channel_id=1, source_target_pairs={{0,384},{128,0},{256,128},{384,256},{1,385},{129,1},{257,129},{385... | collective-permute-start | bytes 1376264 | tf_op jit(solution)/shard_map/ppermute | solution.py:28
  6.2 22.8 %collective-permute-start.3 = (bf16[896,256]{1,0:T(8,128)(2,1)S(1)}, bf16[896,256]{1,0:T(8,128)(2,1)S(1)}, u32[]{:S(2)}, u32[]{:S(2)}) collective-permute-start(bf16[896,256]{1,0:T(8,128)(2,1)S(1)} %shard_map.69.own), channel_id=1, source_target_pairs={{0,128},{128,256},{256,384},{384,0},{1,129},{129,257},{257,385},{3... | collective-permute-start | bytes 1376264 | tf_op jit(solution)/shard_map/ppermute | solution.py:28
  14.0 30.2 %all-to-all-start = ((bf16[16,152,128]{2,1,0:T(8,128)(2,1)}), bf16[16,152,128]{2,1,0:T(8,128)(2,1)S(1)}, u32[]{:S(2)}, u32[]{:S(2)}) async-start(bf16[16,152,128]{2,1,0:T(8,128)(2,1)} %broadcast_in_dim.3), calls=%async_computation | async-start | bytes 1245184 | tf_op jit(solution)/shard_map/all_to_all | solution.py:24
  28.9 6.6 %copy-start.3 = (bf16[448,256]{1,0:T(8,128)(2,1)S(1)}, bf16[448,256]{1,0:T(8,128)(2,1)}, u32[]{:S(2)}) copy-start(bf16[448,256]{1,0:T(8,128)(2,1)} %own.1) | copy-start | bytes 688132
  29.7 16.4 %collective-permute-start.4 = (bf16[448,256]{1,0:T(8,128)(2,1)}, bf16[448,256]{1,0:T(8,128)(2,1)S(1)}, u32[]{:S(2)}, u32[]{:S(2)}) collective-permute-start(bf16[448,256]{1,0:T(8,128)(2,1)} %get-tuple-element.15), channel_id=1, source_target_pairs={{0,128},{128,256},{256,384},{384,0},{1,129},{129,257},{257,385},{3... | collective-permute-start | bytes 688136 | tf_op jit(solution)/shard_map/ppermute | solution.py:35
  31.6 14.5 %collective-permute-start.5 = (bf16[448,256]{1,0:T(8,128)(2,1)S(1)}, bf16[448,256]{1,0:T(8,128)(2,1)S(1)}, u32[]{:S(2)}, u32[]{:S(2)}) collective-permute-start(bf16[448,256]{1,0:T(8,128)(2,1)S(1)} %get-tuple-element.16), channel_id=1, source_target_pairs={{0,384},{128,0},{256,128},{384,256},{1,385},{129,1},{257,129},{385... | collective-permute-start | bytes 688136 | tf_op jit(solution)/shard_map/ppermute | solution.py:35
  35.6 19.0 %collective-permute-start.6 = (bf16[448,256]{1,0:T(8,128)(2,1)S(1)}, bf16[448,256]{1,0:T(8,128)(2,1)S(1)}, u32[]{:S(2)}, u32[]{:S(2)}) collective-permute-start(bf16[448,256]{1,0:T(8,128)(2,1)S(1)} %copy-done.3), channel_id=1, source_target_pairs={{0,96},{32,64},{64,32},{96,0},{1,97},{33,65},{65,33},{97,1},{2,98}... | collective-permute-start | bytes 688136 | tf_op jit(solution)/shard_map/ppermute | solution.py:215
  44.2 3.9 %collective-permute-start.1 = (bf16[16,152,128]{2,1,0:T(8,128)(2,1)S(1)}, bf16[16,152,128]{2,1,0:T(8,128)(2,1)S(1)}, u32[]{:S(2)}, u32[]{:S(2)}) collective-permute-start(bf16[16,152,128]{2,1,0:T(8,128)(2,1)S(1)} %all-to-all-done.feats), channel_id=1, source_target_pairs={{0,1},{1,0},{2,3},{3,2},{4,5},{5,4},{6,7},{7,6},{8,9},{9,8},{10,11... | collective-permute-start | bytes 1867784 | tf_op jit(solution)/shard_map/ppermute | solution.py:20
  50.2 29.3 %all-to-all-start.1 = ((bf16[4,152,896]{2,1,0:T(8,128)(2,1)}), bf16[4,152,896]{2,1,0:T(8,128)(2,1)S(1)}, u32[]{:S(2)}, u32[]{:S(2)}) async-start(bf16[4,152,896]{2,1,0:T(8,128)(2,1)} %get-tuple-element.17), calls=%async_computation.1 | async-start | bytes 2179072 | tf_op jit(solution)/shard_map/all_to_all | solution.py:24
  54.6 15.4 %collective-permute-start.7 = (bf16[2,448,256]{2,1,0:T(8,128)(2,1)S(1)}, bf16[2,448,256]{2,1,0:T(8,128)(2,1)S(1)}, u32[]{:S(2)}, u32[]{:S(2)}) collective-permute-start(bf16[2,448,256]{2,1,0:T(8,128)(2,1)S(1)} %shard_map.74.own), channel_id=1, source_target_pairs={{0,384},{128,0},{256,128},{384,256},{1,385},{129,1},{257,129},{385... | collective-permute-start | bytes 1376264 | tf_op jit(solution)/shard_map/ppermute | solution.py:28
  56.5 14.6 %collective-permute-start.8 = (bf16[2,448,256]{2,1,0:T(8,128)(2,1)S(1)}, bf16[2,448,256]{2,1,0:T(8,128)(2,1)S(1)}, u32[]{:S(2)}, u32[]{:S(2)}) collective-permute-start(bf16[2,448,256]{2,1,0:T(8,128)(2,1)S(1)} %shard_map.74.own), channel_id=1, source_target_pairs={{0,128},{128,256},{256,384},{384,0},{1,129},{129,257},{257,385},{3... | collective-permute-start | bytes 1376264 | tf_op jit(solution)/shard_map/ppermute | solution.py:28
  72.0 14.6 %collective-permute-start.10 = (bf16[2,224,256]{2,1,0:T(8,128)(2,1)}, bf16[2,224,256]{2,1,0:T(8,128)(2,1)S(1)}, u32[]{:S(2)}, u32[]{:S(2)}) collective-permute-start(bf16[2,224,256]{2,1,0:T(8,128)(2,1)} %get-tuple-element.20), channel_id=1, source_target_pairs={{0,384},{128,0},{256,128},{384,256},{1,385},{129,1},{257,129},{385... | collective-permute-start | bytes 688136 | tf_op jit(solution)/shard_map/ppermute | solution.py:35
  73.9 12.7 %collective-permute-start.9 = (bf16[2,224,256]{2,1,0:T(8,128)(2,1)}, bf16[2,224,256]{2,1,0:T(8,128)(2,1)S(1)}, u32[]{:S(2)}, u32[]{:S(2)}) collective-permute-start(bf16[2,224,256]{2,1,0:T(8,128)(2,1)} %get-tuple-element.19), channel_id=1, source_target_pairs={{0,128},{128,256},{256,384},{384,0},{1,129},{129,257},{257,385},{3... | collective-permute-start | bytes 688136 | tf_op jit(solution)/shard_map/ppermute | solution.py:35
  79.9 9.9 %collective-permute-start.11 = (bf16[152,448]{1,0:T(8,128)(2,1)S(1)}, bf16[152,448]{1,0:T(8,128)(2,1)S(1)}, u32[]{:S(2)}, u32[]{:S(2)}) collective-permute-start(bf16[152,448]{1,0:T(8,128)(2,1)S(1)} %shard_map.73.hidden), channel_id=1, source_target_pairs={{0,32},{32,0},{64,96},{96,64},{1,33},{33,1},{65,97},{97,65},{2,34}... | collective-permute-start | bytes 408584 | tf_op jit(solution)/shard_map/ppermute | solution.py:231
  90.3 4.0 %collective-permute-start.12 = (bf16[8,2,80,256]{3,2,1,0:T(8,128)(2,1)S(1)}, bf16[8,2,80,256]{3,2,1,0:T(8,128)(2,1)S(1)}, u32[]{:S(2)}, u32[]{:S(2)}) collective-permute-start(bf16[8,2,80,256]{3,2,1,0:T(8,128)(2,1)S(1)} %get-tuple-element.27), channel_id=1, source_target_pairs={{0,1},{1,0},{2,3},{3,2},{4,5},{5,4},{6,7},{7,6},{8,9},{9,8},{10,11... | collective-permute-start | bytes 1966088 | tf_op jit(solution)/shard_map/ppermute | solution.py:20
  124.3 12.5 %collective-permute-start.14 = (bf16[16,256]{1,0:T(8,128)(2,1)S(1)}, bf16[16,256]{1,0:T(8,128)(2,1)S(1)}, u32[]{:S(2)}, u32[]{:S(2)}) collective-permute-start(bf16[16,256]{1,0:T(8,128)(2,1)S(1)} %slice.29), channel_id=1, source_target_pairs={{0,0},{2,2},{4,96},{6,98},{8,128},{10,130},{12,224},{14,226},{16,2... | collective-permute-start | bytes 24584 | tf_op jit(solution)/shard_map/ppermute | solution.py:255
  129.9 7.5 %collective-permute-start.13 = (bf16[4,2,4,256]{3,2,1,0:T(4,128)(2,1)S(1)}, bf16[4,2,4,256]{3,2,1,0:T(4,128)(2,1)S(1)}, u32[]{:S(2)}, u32[]{:S(2)}) collective-permute-start(bf16[4,2,4,256]{3,2,1,0:T(4,128)(2,1)S(1)} %get-tuple-element.28), channel_id=1, source_target_pairs={{0,32},{32,0},{64,96},{96,64},{1,33},{33,1},{65,97},{97,65},{2,34}... | collective-permute-start | bytes 49160 | tf_op jit(solution)/shard_map/ppermute | solution.py:273
